TPU v7x, 256 devices: a whole 4x4x8 slice. The times are simulated.
256 devices in a mesh: az: 64 (over y, x_lo, z), ht: 4 (over x_hi, core).
Axes of the slice: x: 4 (x_hi: 2, x_lo: 2; x = x_hi * 2 + x_lo), y: 4, z: 8, core: 2. Of those that a mesh axis runs over, the one named last changes fastest.
Arguments:
- state: float32 [4, 2048, 64, 256], P(None, 'az', 'ht'), may hold values from -6 to 6
- zone_id: int32 [2048, 256], P('az'), may hold values from 0 to 7
- ground_aux: float32 [2048, 256], P('az'), may hold values from -6 to 6
- resistance: float32 [8], replicated, may hold values from 0.3 to 3
- relax_rate: float32 [8], replicated, may hold values from 0.1 to 2.5
- cutoff: int32 [64], replicated, may hold values from 1 to 128, as said below
Outputs:
- filtered_state: float32 [4, 2048, 64, 256], P(None, 'az', 'ht')
Inputs may be any that keep to these rules, and one draw needn't show every extreme that they name: `cutoff`: some cycle keeps exactly 128 modes.
All inputs are finite; a program needn't handle non-finite values.
Results may differ from a plain program's by a relative error of at most 0.000064.
Values sent between devices are 32-bit elements; how exact they have to be, the bound alone decides.
No kernel may reach another device: no remote copies, remote signals or barrier semaphores. Data moves between devices by JAX's collectives and lax.ppermute only.
A program may use at most 64 MiB of HBM per device.

v0:
```python
import math

import jax
import jax.numpy as jnp
from jax import lax
from jax.sharding import PartitionSpec as P

NA = 2048
NI = 64
MODES = 128


time_step = 0.4


def padded_2(cells, sides, width, closed):
    for axis, dim in sides:
        count = lax.axis_size(axis)
        ends = count if closed else count - 1
        head = lax.slice_in_dim(cells, 0, width, axis=dim)
        tail = lax.slice_in_dim(cells, cells.shape[dim] - width, cells.shape[dim], axis=dim)
        cells = jnp.concatenate(
            [
                lax.ppermute(tail, axis, [(i, (i + 1) % count) for i in range(ends)]),
                cells,
                lax.ppermute(head, axis, [((i + 1) % count, i) for i in range(ends)]),
            ],
            axis=dim,
        )
    return cells


def radial_terms(total_az, count):
    radius = total_az / (2.0 * math.pi) + jnp.arange(count, dtype=jnp.float32)
    inv_radius = 1.0 / radius
    inv_arc = total_az / (2.0 * math.pi) * inv_radius
    return (inv_radius, inv_arc)


def zone_lookup(zone_id, table):
    match = zone_id[..., None] == jnp.arange(table.shape[0], dtype=jnp.int32)
    return jnp.sum(jnp.where(match, table, jnp.zeros_like(table)), axis=-1)


def radial_diff(field):
    zero = jnp.zeros_like(field[..., :1])
    return 0.5 * (
        jnp.concatenate([field[..., 1:], zero], -1) - jnp.concatenate([zero, field[..., :-1]], -1)
    )


def tendency(state, az_pad, ht_pad, inv_radius, inv_arc):
    pres, vel_r = (state[0], state[1])
    theta_p = 0.5 * (az_pad[0, 2:] - az_pad[0, :-2]) * inv_arc
    theta_t = 0.5 * (az_pad[1, 2:] - az_pad[1, :-2]) * inv_arc
    height_p = 0.5 * (ht_pad[0, :, 2:] - ht_pad[0, :, :-2])
    height_z = 0.5 * (ht_pad[1, :, 2:] - ht_pad[1, :, :-2])
    rate_p = -(radial_diff(vel_r) + vel_r * inv_radius + theta_t + height_z)
    return jnp.stack([rate_p, -radial_diff(pres), -theta_p, -height_p])


def ground_ghost(state, aux, inv_resist):
    wall = (state[0, :, 0, :] - aux) * inv_resist
    return jnp.stack([state[0, :, 0, :], 2.0 * wall - state[3, :, 0, :]])[:, :, None, :]


def mode_tables(first_cell, count):
    modes = jnp.arange(MODES, dtype=jnp.int32)
    cells = first_cell + jnp.arange(count, dtype=jnp.int32)
    phase = (modes[:, None] * cells[None, :] % NA).astype(jnp.float32) * (2.0 * math.pi / NA)
    analysis = jnp.concatenate([jnp.cos(phase), jnp.sin(phase)], 0)
    weight = jnp.where(modes == 0, 1.0, 2.0).astype(jnp.float32) / NA
    weight = jnp.concatenate([weight, weight])
    return (analysis, analysis * weight[:, None])


def per_device(state, zone_id, ground_aux, resistance, relax_rate, cutoff):
    sectors = state.shape[1]
    radii = state.shape[3]
    inv_radius, inv_arc = radial_terms(NA, radii)
    inv_resist = zone_lookup(zone_id, 1.0 / resistance)
    relax = zone_lookup(zone_id, relax_rate)
    on_ground = lax.axis_index("ht") == 0
    highest = lax.Precision.HIGHEST
    modes = jnp.arange(MODES, dtype=jnp.int32)
    row_modes = jnp.concatenate([modes, modes])

    def rates(current, aux):
        pair_t = jnp.stack([current[0], current[2]])
        az_pad = padded_2(pair_t, (("az", 1),), 1, True)
        pair_z = jnp.stack([current[0], current[3]])
        padded = padded_2(pair_z, (("ht", 2),), 1, False)
        bottom = jnp.where(on_ground, ground_ghost(current, aux, inv_resist), padded[:, :, :1])
        ht_pad = jnp.concatenate([bottom, padded[:, :, 1:]], 2)
        return tendency(current, az_pad, ht_pad, inv_radius, inv_arc)

    first = rates(state, ground_aux)
    middle = state + time_step * first
    mid_aux = ground_aux + time_step * relax * (state[0, :, 0, :] - ground_aux)
    second = rates(middle, mid_aux)
    stepped = 0.5 * (state + middle + time_step * second)
    inner = stepped[..., :NI]
    analysis, synthesis = mode_tables(lax.axis_index("az") * sectors, sectors)
    partial_coef = jnp.einsum("ma,cahr->cmhr", analysis, inner, precision=highest)
    coef = lax.psum(partial_coef, "az")
    keep = (row_modes[:, None] < cutoff[None, :]).astype(jnp.float32)
    filtered = jnp.einsum(
        "ma,cmhr->cahr", synthesis, coef * keep[None, :, None, :], precision=highest
    )
    return jnp.concatenate([filtered, stepped[..., NI:]], 3)


def solution(mesh):
    return jax.shard_map(
        per_device,
        mesh=mesh,
        in_specs=(P(None, "az", "ht", None), P("az", None), P("az", None), P(), P(), P()),
        out_specs=P(None, "az", "ht", None),
        check_vma=False,
    )
```

profile of v0, /device:TPU:32, one launch (start us, length us, event | category | flops | bytes accessed | tf_op | source)
XLA Modules:
  0.0 692.0 jit_solution(14066822311380308475)
XLA Ops:
  6.5 2.8 copy.78
  9.3 1.3 slice_bitcast_fusion.2
  10.7 0.8 copy-done.1
  11.4 0.7 fusion.44
  12.1 1.9 collective-permute-start.1
  14.1 0.6 fusion.41
  14.8 2.0 collective-permute-start.3
  16.7 1.3 collective-permute-start.2
  18.5 1.9 fusion.68
  20.8 1.7 collective-permute-done.2
  23.0 1.2 copy-done
  24.2 1.4 fusion.4
  26.0 6.3 collective-permute-start.7
  32.4 1.3 collective-permute-start.6
  33.8 2.0 collective-permute-start.5
  35.7 5.4 collective-permute-start.4
  41.8 1.0 collective-permute-done.5
  43.4 2.6 fusion.3
  46.0 5.1 convolution_bitcast_fusion
  51.9 1.9 slice.228
  53.8 620.6 %all-reduce.10.cloned.1.call-done = f32[4,256,16,64]{1,3,2,0:T(8,128)} async-done(((f32[4,256,16,64]{1,3,2,0:T(8,128)}), f32[4,256,16,64]{1,3,2,0:T(8,128)}) %all-reduce.10.cloned.1.call-update) | async-done | bytes 4194320 | tf_op jit(solution)/shard_map/psum | solution.py:105
  674.4 7.5 %fusion.6 = f32[4,32,16,64]{3,1,2,0:T(8,128)S(1)} fusion(f32[4,256,16,64]{1,3,2,0:T(8,128)} %all-reduce.10.cloned.1.call-done, f32[256,64]{0,1:T(8,128)S(1)} %compare_convert_fusion, f32[128,32]{0,1:T(8,128)S(1)} %get-tuple-element.37, f32[128,32]{0,1:T(8,128)S(1)} %get-tuple-element.36, f32[256]{0:T(256)S(1)} %pad_maximum_fusion.28), kind=kOutput, calls=%fused_computation.12 | convolution fusion | flops 403718144 | bytes 4817920 | tf_op jit(solution)/shard_map/ma,cmhr->cahr/dot_general | solution.py:107
  681.9 0.6 pad_maximum_fusion.2
  682.6 2.5 copy.86
  (53 shorter events, 3.7 us)
Async XLA Ops:
  6.5 667.8 %all-reduce.10.cloned.1.call-start = ((), (), s32[]{:S(2)}) async-start(), calls=%async_computation | async-start | bytes 8388608 | tf_op jit(solution)/shard_map/psum | solution.py:105
  10.6 0.8 copy-start.1
  10.6 7.4 %copy-start.8 = (f32[8]{0:T(128)S(1)}, f32[8]{0:T(128)}, u32[]{:S(2)}) copy-start(f32[8]{0:T(128)} %param.9) | copy-start | bytes 100
  10.6 7.6 %copy-start.5 = (s32[32,256]{1,0:T(8,128)S(1)}, s32[32,256]{1,0:T(8,128)}, u32[]{:S(2)}) copy-start(s32[32,256]{1,0:T(8,128)} %param.7) | copy-start | bytes 98308
  10.6 7.6 %copy-start.6 = (f32[8]{0:T(128)S(1)}, f32[8]{0:T(128)}, u32[]{:S(2)}) copy-start(f32[8]{0:T(128)} %param.10) | copy-start | bytes 100
  10.6 7.8 %copy-start.4 = (f32[32,256]{1,0:T(8,128)S(1)}, f32[32,256]{1,0:T(8,128)}, u32[]{:S(2)}) copy-start(f32[32,256]{1,0:T(8,128)} %param.8) | copy-start | bytes 98308
  12.1 8.6 %collective-permute-start.1 = (f32[2,1,16,256]{3,1,2,0:T(1,128)}, f32[2,1,16,256]{3,1,2,0:T(1,128)S(1)}, u32[]{:S(2)}, u32[]{:S(2)}) collective-permute-start(f32[2,1,16,256]{3,1,2,0:T(1,128)} %get-tuple-element.23), channel_id=1, source_target_pairs={{0,4},{4,8},{8,12},{12,16},{16,20},{20,24},{24,28},{28,32},{32,36}... | collective-permute-start | bytes 98312 | tf_op jit(solution)/shard_map/ppermute | solution.py:24
  14.0 6.7 collective-permute-start
  14.8 5.9 collective-permute-start.3
  16.7 5.7 collective-permute-start.2
  18.5 4.0 copy-start.2
  22.7 1.6 copy-start
  26.0 16.9 %collective-permute-start.7 = (f32[2,32,1,256]{3,1,0,2:T(8,128)S(1)}, f32[2,32,1,256]{3,1,0,2:T(8,128)S(1)}, u32[]{:S(2)}, u32[]{:S(2)}) collective-permute-start(f32[2,32,1,256]{3,1,0,2:T(8,128)S(1)} %get-tuple-element.21), channel_id=1, source_target_pairs={{0,1},{1,2},{2,3},{4,5},{5,6},{6,7},{8,9},{9,10},{10,11},{12,13},{... | collective-permute-start | bytes 196616 | tf_op jit(solution)/shard_map/ppermute | solution.py:24
  32.4 10.5 %collective-permute-start.6 = (f32[2,32,1,256]{3,1,0,2:T(8,128)S(1)}, f32[2,32,1,256]{3,1,0,2:T(8,128)S(1)}, u32[]{:S(2)}, u32[]{:S(2)}) collective-permute-start(f32[2,32,1,256]{3,1,0,2:T(8,128)S(1)} %get-tuple-element.20), channel_id=1, source_target_pairs={{1,0},{2,1},{3,2},{5,4},{6,5},{7,6},{9,8},{10,9},{11,10},{13,12},{... | collective-permute-start | bytes 196616 | tf_op jit(solution)/shard_map/ppermute | solution.py:26
  33.8 9.0 %collective-permute-start.5 = (f32[2,1,16,256]{3,1,2,0:T(1,128)S(1)}, f32[2,1,16,256]{3,1,2,0:T(1,128)S(1)}, u32[]{:S(2)}, u32[]{:S(2)}) collective-permute-start(f32[2,1,16,256]{3,1,2,0:T(1,128)S(1)} %get-tuple-element.19), channel_id=1, source_target_pairs={{0,4},{4,8},{8,12},{12,16},{16,20},{20,24},{24,28},{28,32},{32,36}... | collective-permute-start | bytes 98312 | tf_op jit(solution)/shard_map/ppermute | solution.py:24
  35.7 7.0 %collective-permute-start.4 = (f32[2,1,16,256]{3,1,2,0:T(1,128)S(1)}, f32[2,1,16,256]{3,1,2,0:T(1,128)S(1)}, u32[]{:S(2)}, u32[]{:S(2)}) collective-permute-start(f32[2,1,16,256]{3,1,2,0:T(1,128)S(1)} %get-tuple-element.18), channel_id=1, source_target_pairs={{4,0},{8,4},{12,8},{16,12},{20,16},{24,20},{28,24},{32,28},{36,32}... | collective-permute-start | bytes 98312 | tf_op jit(solution)/shard_map/ppermute | solution.py:26
  51.1 0.7 copy-start.7
  53.8 628.1 %copy-start.3 = (f32[4,32,16,192]{3,1,2,0:T(8,128)S(1)}, f32[4,32,16,192]{3,1,2,0:T(8,128)}, u32[]{:S(2)}) copy-start(f32[4,32,16,192]{3,1,2,0:T(8,128)} %slice.228) | copy-start | bytes 4718596
Sparse Core Ops, SparseCore 0:
  51.3 623.0 all-reduce.9
where the time goes:
time: 693 us; the launch traced here: 692 us
  waiting for transfers between devices  623 us (90%)
  starting transfers between devices  20.3 us (3%)
  local copies, waits for them, and re-layouts  13.9 us (2%)
  between operations  13.7 us (2%)
  matrix products  12.6 us (2%)
  other arithmetic  8.13 us (1%)
    psum x1, waiting for transfers between devices, per_device(): coef = lax.psum(partial_coef, 'az')  621 us
  transfers between devices with their start and end apart: 9, of which 3 were waited for; matrix products, arithmetic and copies ran while one was open for 1% of the time, Pallas kernels for 0%

commit v1 on v0

v1 whole, which is shorter than its diff:
```python
import functools
import math

import jax
import jax.numpy as jnp
import numpy as np
from jax import lax
from jax.experimental import pallas as pl
from jax.experimental.pallas import tpu as pltpu
from jax.sharding import Mesh, PartitionSpec as P

NA = 2048
NI = 64
MODES = 128
ZONES = 8
SECTORS = 64
ROWS = NA // SECTORS
HALF = ROWS // 2
HTS = 16
NR = 256
COMPS = 4
DT = 0.4

AZ = ("y", "x", "z")
SPREAD = ("y", "z", "x")
HT = ("hx", "core")


def sector_of_chunk():
    y, z, x = np.meshgrid(np.arange(4), np.arange(8), np.arange(2), indexing="ij")
    return ((y * 2 + x) * 8 + z).reshape(-1)


def mode_tables():
    azimuth = (sector_of_chunk()[: SECTORS // 2, None] * ROWS + np.arange(HALF)[None, :]).reshape(-1)
    tables = []
    for parity in range(2):
        modes = np.arange(parity, MODES, 2)
        phase = (modes[:, None] * azimuth[None, :] % NA) * (2.0 * math.pi / NA)
        turn = (modes * HALF % NA) * (2.0 * math.pi / NA)
        more = np.zeros((MODES // 2, 128))
        more[:, 0] = np.cos(turn)
        more[:, 1] = np.sin(turn)
        more[:, 2] = np.where(modes == 0, 1.0, 2.0) / NA
        tables.append((np.concatenate([np.cos(phase), np.sin(phase)], 0), more))
    waves, turns = [np.stack(t).astype(np.float32) for t in zip(*tables)]
    return (*split(waves), turns)


def split(x):
    x = x.astype(np.float32) if isinstance(x, np.ndarray) else x
    large = x.astype(jnp.bfloat16)
    return large, (x - large.astype(jnp.float32)).astype(jnp.bfloat16)


def product(a, b, dims):
    dot = functools.partial(lax.dot_general, dimension_numbers=(dims, ((), ())), preferred_element_type=jnp.float32)
    return dot(a[0], b[0]) + (dot(a[0], b[1]) + dot(a[1], b[0]))


def radial_diff(x):
    n = x.shape[-1]
    lane = lax.broadcasted_iota(jnp.int32, (1, n), 1)
    after = jnp.where(lane == NR - 1, 0.0, 0.5)
    before = jnp.where(lane == 0, 0.0, 0.5)
    return after * pltpu.roll(x, n - 1, x.ndim - 1) - before * pltpu.roll(x, 1, x.ndim - 1)


def row_diff(x, low, high):
    up = jnp.concatenate([x[1:], high], 0)
    down = jnp.concatenate([low, x[:-1]], 0)
    return 0.5 * (up - down)


def radial_rates(n):
    lane = lax.broadcasted_iota(jnp.int32, (1, n), 1).astype(jnp.float32)
    inv_r = 1.0 / (NA / (2.0 * math.pi) + lane)
    return inv_r, 0.5 * (NA / (2.0 * math.pi)) * inv_r


def plane(state, comp, height, width=NR):
    return state[comp, :, height, 0:width]


def lookup(ids, table):
    out = jnp.zeros(ids.shape, jnp.float32)
    for k in range(ZONES):
        out = jnp.where(ids == k, table[k], out)
    return out


HT_ROWS = 136
AZ_ROWS = 72


def pack_kernel(state, up, down):
    inv_r, half_arc = radial_rates(NR)
    zero = jnp.zeros((1, NR), jnp.float32)
    for out, edge, inside, sign in ((up, HTS - 1, HTS - 2, 1.0), (down, 0, 1, -1.0)):
        p, w, u, v = [plane(state, i, edge) for i in (0, 3, 1, 2)]
        p_in, w_in = plane(state, 0, inside), plane(state, 3, inside)
        out[0:32] = p
        out[32:64] = w
        turn = 2.0 * row_diff(v, zero, zero) * half_arc
        out[64:96] = p - DT * (radial_diff(u) + u * inv_r + turn - (0.5 * sign) * w_in)
        out[96:128] = w + (0.5 * DT * sign) * p_in
        out[128:129] = v[0:1]
        out[129:130] = v[ROWS - 1 : ROWS]
        out[130:HT_ROWS] = jnp.zeros((HT_ROWS - 130, NR), jnp.float32)


def ground_kernel(resistance, relax, state, zone, aux, ground):
    ids, q = zone[...], aux[...]
    p0, w0 = plane(state, 0, 0), plane(state, 3, 0)
    twice = 2.0 * (1.0 / lookup(ids, resistance))
    ground[0] = twice * (p0 - q) - w0
    ground[1] = twice
    ground[2] = q + DT * lookup(ids, relax) * (p0 - q)


def edge_kernel(flag, state, low, high, ground, to_left, to_right):
    inv_r, half_arc = radial_rates(NR)
    on_ground = flag[0] == 1
    for out, j, inside, sign, corner in ((to_right, ROWS - 1, ROWS - 2, 1.0, 129), (to_left, 0, 1, -1.0, 128)):
        p, u, v, w = [state[i, j] for i in range(4)]
        w_low = jnp.where(on_ground, ground[0, j : j + 1], low[32 + j : 33 + j])
        out[0:16] = p
        out[16:32] = v
        rate = radial_diff(u) + u * inv_r + row_diff(w, w_low, high[32 + j : 33 + j]) - sign * half_arc * state[2, inside]
        out[32:48] = p - DT * rate
        out[48:64] = v + (DT * sign) * half_arc * state[0, inside]
        out[64:65] = low[corner : corner + 1]
        out[65:66] = high[corner : corner + 1]
        out[66:AZ_ROWS] = jnp.zeros((AZ_ROWS - 66, NR), jnp.float32)


def two_stages(width, flag, state, low, high, left, right, ground, mid, ghost, emit):
    on_ground, on_top = flag[0] == 1, flag[1] == 1
    inv_r, half_arc = radial_rates(width)
    cols = slice(0, width)
    turn = DT * half_arc

    p0, p1, u0, v0, w0, w1 = [plane(state, i, k, width) for i, k in ((0, 0), (0, 1), (1, 0), (2, 0), (3, 0), (3, 1))]
    p15, w15 = plane(state, 0, HTS - 1, width), plane(state, 3, HTS - 1, width)
    bp = jnp.where(on_ground, p0, low[0:32, cols])
    bw = jnp.where(on_ground, ground[0, :, cols], low[32:64, cols])
    ghost[0], ghost[1], ghost[2], ghost[3] = bp, bw, high[0:32, cols], high[32:64, cols]

    sub = lax.broadcasted_iota(jnp.int32, (ROWS, width), 0)

    def corners(k):
        return turn * jnp.where(
            sub == 0, left[k : k + 1, cols], jnp.where(sub == ROWS - 1, -right[k : k + 1, cols], 0.0)
        )

    top_p = high[64:96, cols] + (0.5 * DT) * w15 + corners(65)
    top_w = high[96:128, cols] + (0.5 * DT) * p15
    low_p = low[64:96, cols] - (0.5 * DT) * w0 + corners(64)
    low_w = low[96:128, cols] - (0.5 * DT) * p0
    v_diff = 2.0 * row_diff(v0, left[16:17, cols], right[16:17, cols]) * half_arc
    mid_p0 = p0 - DT * (radial_diff(u0) + u0 * inv_r + v_diff + 0.5 * (w1 - bw))
    mid_w0 = w0 - (0.5 * DT) * (p1 - bp)
    ghost[4] = jnp.where(on_ground, mid_p0, low_p)
    ghost[5] = jnp.where(on_ground, ground[1, :, cols] * (mid_p0 - ground[2, :, cols]) - mid_w0, low_w)
    ghost[6] = jnp.where(on_top, 0.0, top_p)
    ghost[7] = jnp.where(on_top, 0.0, top_w)

    mid[0, 0] = left[32:48, cols] - turn * state[2, 0, :, cols]
    mid[2, 0] = left[48:64, cols] - turn * state[0, 0, :, cols]
    mid[0, ROWS + 1] = right[32:48, cols] + turn * state[2, ROWS - 1, :, cols]
    mid[2, ROWS + 1] = right[48:64, cols] + turn * state[0, ROWS - 1, :, cols]

    def rates(p, u, v_diff, p_diff, w, j, first):
        p_low, w_low, p_high, w_high = [ghost[first + i, pl.ds(j, 1)] for i in range(4)]
        return (
            radial_diff(u) + u * inv_r + v_diff * half_arc + row_diff(w, w_low, w_high),
            radial_diff(p),
            half_arc * p_diff,
            row_diff(p, p_low, p_high),
        )

    def first(j, p_diff, v_diff):
        p, u, v, w = [state[i, j, :, cols] for i in range(4)]
        for i, (s, rate) in enumerate(zip((p, u, v, w), rates(p, u, v_diff, p_diff, w, j, 0))):
            mid[i, j + 1] = s - DT * rate

    first(0, state[0, 1, :, cols] - left[0:16, cols], state[2, 1, :, cols] - left[16:32, cols])
    end = ROWS - 2
    first(ROWS - 1, right[0:16, cols] - state[0, end, :, cols], right[16:32, cols] - state[2, end, :, cols])

    @pl.loop(1, ROWS - 1, unroll=5)
    def _(j):
        first(
            j,
            state[0, j + 1, :, cols] - state[0, j - 1, :, cols],
            state[2, j + 1, :, cols] - state[2, j - 1, :, cols],
        )

    def second(j):
        p, u, v, w = [mid[i, j + 1] for i in range(4)]
        found = rates(p, u, mid[2, j + 2] - mid[2, j], mid[0, j + 2] - mid[0, j], w, j, 4)
        return [0.5 * (state[i, j, :, cols] + m - DT * r) for i, (m, r) in enumerate(zip((p, u, v, w), found))]

    @pl.loop(0, HALF, unroll=2)
    def _(l):
        emit(l, second(l), second(l + HALF))


def inner_kernel(flag, state, low, high, left, right, ground, packed, mid, ghost):
    near = lax.broadcasted_iota(jnp.int32, (HTS, 128), 1) < NI

    def emit(l, one, two):
        for i in range(COMPS):
            both = jnp.where(near, one[i], pltpu.roll(two[i], NI, 1))
            packed[pl.ds(i * HTS * HALF + l, HTS, stride=HALF), :] = both

    two_stages(128, flag, state, low, high, left, right, ground, mid, ghost, emit)


def outer_kernel(flag, state, low, high, left, right, ground, stepped, mid, ghost):
    def emit(l, one, two):
        for i in range(COMPS):
            stepped[i, l] = one[i]
            stepped[i, l + HALF] = two[i]

    two_stages(NR, flag, state, low, high, left, right, ground, mid, ghost, emit)


def filter_kernel(large, small, turn, cutoff, x_ref, o_ref):
    n = NA // 4
    first, second = x_ref[:n], x_ref[n:]
    h = MODES // 2
    mode = lax.broadcasted_iota(jnp.int32, (h, 128), 0) * 2
    near = lax.broadcasted_iota(jnp.int32, (h, 128), 1) < NI
    limit = jnp.concatenate([cutoff[...], cutoff[...]], 1)
    outs = []
    for parity in range(2):
        folded = first + second if parity == 0 else first - second
        waves = large[parity], small[parity]
        cs, sn, weight = [turn[parity, :, k : k + 1] for k in range(3)]
        coef = product(waves, split(folded), ((1,), (0,)))
        a, b = coef[:h], coef[h:]
        a_all = jnp.where(near, a, a * cs - b * sn)
        b_all = jnp.where(near, b, a * sn + b * cs)
        keep = jnp.where(mode + parity < limit, weight, 0.0)
        a_all = (a_all + pltpu.roll(a_all, NI, 1)) * keep
        b_all = (b_all + pltpu.roll(b_all, NI, 1)) * keep
        a_back = jnp.where(near, a_all, a_all * cs + b_all * sn)
        b_back = jnp.where(near, b_all, b_all * cs - a_all * sn)
        back = jnp.concatenate([a_back, b_back], 0)
        outs.append(product(waves, split(back), ((0,), (0,))))
    o_ref[:n] = outs[0] + outs[1]
    o_ref[n:] = outs[0] - outs[1]


def merge_kernel(stepped, back, out, rows, tile, beside, sems):
    near = lax.broadcasted_iota(jnp.int32, (HTS, 128), 1) < NI
    loads = [
        pltpu.make_async_copy(stepped.at[i, :, :, pl.ds(0, 128)], beside.at[i], sems.at[0, i]) for i in range(COMPS)
    ]
    for copy in loads:
        copy.start()
    for i in range(COMPS * HTS):
        rows[pl.ds(i // HTS * HTS * HALF + i % HTS, HALF, stride=HTS), :] = back[i * HALF : (i + 1) * HALF]
    stores = []
    for i in range(COMPS):
        loads[i].wait()
        for l in range(HALF):
            at = (i * HALF + l) * HTS
            both = rows[at : at + HTS]
            tile[i, l] = jnp.where(near, both, beside[i, l])
            tile[i, l + HALF] = jnp.where(near, pltpu.roll(both, NI, 1), beside[i, l + HALF])
        stores.append(pltpu.make_async_copy(tile.at[i], out.at[i, :, :, pl.ds(0, 128)], sems.at[1, i]))
        stores[i].start()
    for copy in stores:
        copy.wait()


def per_device(state, zone_id, ground_aux, resistance, relax_rate, cutoff):
    f32 = jnp.float32
    ht = lax.axis_index(HT)
    flags = jnp.stack([ht == 0, ht == 3]).astype(jnp.int32)

    vmem = pl.BlockSpec(memory_space=pltpu.VMEM)
    smem = pl.BlockSpec(memory_space=pltpu.SMEM)
    anywhere = pl.BlockSpec(memory_space=pl.ANY)

    def call(kernel, mib=8, **more):
        return pl.pallas_call(kernel, compiler_params=pltpu.CompilerParams(vmem_limit_bytes=mib * 2**20), **more)

    def shapes(*dims):
        return tuple(jax.ShapeDtypeStruct(d, f32) for d in dims)

    up, down = call(
        pack_kernel, out_shape=shapes((HT_ROWS, NR), (HT_ROWS, NR)), in_specs=[vmem], out_specs=(vmem, vmem), name="pack"
    )(state)
    low = lax.ppermute(up, HT, [(i, i + 1) for i in range(3)])
    high = lax.ppermute(down, HT, [(i + 1, i) for i in range(3)])
    ground = call(
        ground_kernel,
        out_shape=shapes((3, ROWS, NR))[0],
        in_specs=[smem] * 2 + [vmem] * 3,
        out_specs=vmem,
        name="ground",
    )(resistance, relax_rate, state, zone_id, ground_aux)
    to_left, to_right = call(
        edge_kernel,
        out_shape=shapes((AZ_ROWS, NR), (AZ_ROWS, NR)),
        in_specs=[smem] + [vmem] * 4,
        out_specs=(vmem, vmem),
        name="edge",
    )(flags, state, low, high, ground)
    left = lax.ppermute(to_right, AZ, [(i, (i + 1) % SECTORS) for i in range(SECTORS)])
    right = lax.ppermute(to_left, AZ, [((i + 1) % SECTORS, i) for i in range(SECTORS)])

    operands = (flags, state, low, high, left, right, ground)

    def scratch(width):
        return [pltpu.VMEM((COMPS, ROWS + 2, HTS, width), f32), pltpu.VMEM((8, ROWS, width), f32)]

    packed = call(
        inner_kernel,
        mib=12,
        out_shape=shapes((COMPS * HTS * HALF, 128))[0],
        in_specs=[smem] + [vmem] * 6,
        out_specs=vmem,
        scratch_shapes=scratch(128),
        cost_estimate=pl.CostEstimate(flops=10**7, bytes_accessed=6 * 10**6, transcendentals=0),
        name="inner",
    )(*operands)
    circle = lax.all_to_all(packed.reshape(SECTORS, HALF, 128), SPREAD, 0, 0, tiled=True)
    stepped = call(
        outer_kernel,
        mib=16,
        out_shape=shapes((COMPS, ROWS, HTS, NR))[0],
        in_specs=[smem] + [vmem] * 6,
        out_specs=vmem,
        scratch_shapes=scratch(NR),
        cost_estimate=pl.CostEstimate(flops=2 * 10**7, bytes_accessed=2 * 10**7, transcendentals=0),
        name="outer",
    )(*operands)
    kept = call(
        filter_kernel, out_shape=shapes((NA // 2, 128))[0], in_specs=[vmem] * 5, out_specs=vmem, name="filter"
    )(*map(jnp.asarray, mode_tables()), cutoff.reshape(1, NI), circle.reshape(NA // 2, 128))
    back = lax.all_to_all(kept.reshape(SECTORS, HALF, 128), SPREAD, 0, 0, tiled=True)
    return call(
        merge_kernel,
        out_shape=jax.ShapeDtypeStruct(stepped.shape, f32),
        in_specs=[anywhere, vmem],
        out_specs=anywhere,
        scratch_shapes=[
            pltpu.VMEM((COMPS * HTS * HALF, 128), f32),
            pltpu.VMEM((COMPS, ROWS, HTS, 128), f32),
            pltpu.VMEM((COMPS, ROWS, HTS, 128), f32),
            pltpu.SemaphoreType.DMA((2, COMPS)),
        ],
        input_output_aliases={0: 0},
        name="merge",
    )(stepped, back.reshape(COMPS * HTS * HALF, 128))


def solution(mesh):
    fine = Mesh(mesh.devices.reshape(4, 2, 8, 2, 2), AZ + HT)
    return jax.shard_map(
        per_device,
        mesh=fine,
        in_specs=(P(None, AZ, HT, None), P(AZ, None), P(AZ, None), P(), P(), P()),
        out_specs=P(None, AZ, HT, None),
        check_vma=False,
    )
```

time: 693 us -> 80.3 us (0.12)
  the two profiles are of different devices: /device:TPU:32 before, /device:TPU:1 now
where the time goes in v1:
time: 80.3 us; the launch traced here: 79.9 us
  blocking collectives  23.2 us (29%)
  starting transfers between devices  22 us (27%)
  waiting for transfers between devices  18.8 us (23%)
  Pallas kernels  12.6 us (16%)
  local copies, waits for them, and re-layouts  3.13 us (4%)
    all_to_all x1, blocking collectives, per_device(): lax.all_to_all(packed.reshape(SECTORS, HALF, 128), SPREAD, 0, 0, tiled=True)  23.2 us
    all_to_all x1, waiting for transfers between devices, per_device(): lax.all_to_all(kept.reshape(SECTORS, HALF, 128), SPREAD, 0, 0, tiled=True)  13.5 us
    ppermute x1, starting transfers between devices, per_device(): lax.ppermute(to_left, AZ, [((i + 1) % SECTORS, i) for i in range(SECTORS)])  6.55 us
    ppermute x1, starting transfers between devices, per_device(): low = lax.ppermute(up, HT, [(i, i + 1) for i in range(3)])  6.17 us
    all_to_all x1, starting transfers between devices, per_device(): lax.all_to_all(kept.reshape(SECTORS, HALF, 128), SPREAD, 0, 0, tiled=True)  5.6 us
    pallas_call x1, Pallas kernels, per_device(): call(outer_kernel, mib=16, out_shape=shapes((COMPS, ROWS, HTS, NR))[0], i...  4.25 us
    ppermute x1, waiting for transfers between devices, per_device(): high = lax.ppermute(down, HT, [(i + 1, i) for i in range(3)])  3.69 us
    unnamed x20, local copies, waits for them, and re-layouts  3.13 us
  transfers between devices with their start and end apart: 5, of which 3 were waited for; matrix products, arithmetic and copies ran while one was open for 0% of the time, Pallas kernels for 6%

profile of v1, /device:TPU:1, one launch (start us, length us, event | category | flops | bytes accessed | tf_op | source)
XLA Modules:
  0.0 79.9 jit_solution(13445055128931023793)
XLA Ops:
  0.0 1.6 %copy-done = f32[4,32,16,256]{3,2,1,0:T(8,128)S(1)} copy-done((f32[4,32,16,256]{3,2,1,0:T(8,128)S(1)}, f32[4,32,16,256]{3,2,1,0:T(8,128)}, u32[]{:S(2)}) %copy-start) | copy-done | bytes 2097176
  1.6 0.2 pack.1
  1.8 6.2 %collective-permute-start = (f32[136,256]{1,0:T(8,128)S(1)}, f32[136,256]{1,0:T(8,128)S(1)}, u32[]{:S(2)}, u32[]{:S(2)}) collective-permute-start(f32[136,256]{1,0:T(8,128)S(1)} %get-tuple-element.9), channel_id=1, source_target_pairs={{0,1},{1,2},{2,3},{4,5},{5,6},{6,7},{8,9},{9,10},{10,11},{12,13},{... | collective-permute-start | bytes 417800 | tf_op jit(solution)/shard_map/ppermute | solution.py:297
  8.0 1.9 %collective-permute-start.1 = (f32[136,256]{1,0:T(8,128)S(1)}, f32[136,256]{1,0:T(8,128)S(1)}, u32[]{:S(2)}, u32[]{:S(2)}) collective-permute-start(f32[136,256]{1,0:T(8,128)S(1)} %get-tuple-element.10), channel_id=1, source_target_pairs={{1,0},{2,1},{3,2},{5,4},{6,5},{7,6},{9,8},{10,9},{11,10},{13,12},{... | collective-permute-start | bytes 417800 | tf_op jit(solution)/shard_map/ppermute | solution.py:298
  10.0 0.0 copy-start.5
  10.0 0.7 copy-done.5
  10.7 0.8 copy-done.6
  11.5 0.6 ground.1
  12.1 0.1 add_convert_fusion.flag
  12.2 0.0 collective-permute-done.low
  12.2 3.7 %collective-permute-done.1.high = f32[136,256]{1,0:T(8,128)S(1)} collective-permute-done((f32[136,256]{1,0:T(8,128)S(1)}, f32[136,256]{1,0:T(8,128)S(1)}, u32[]{:S(2)}, u32[]{:S(2)}) %collective-permute-start.1) | collective-permute-done | bytes 139296 | tf_op jit(solution)/shard_map/ppermute | solution.py:298
  15.9 0.6 edge.1
  16.5 1.7 %collective-permute-start.2 = (f32[72,256]{1,0:T(8,128)S(1)}, f32[72,256]{1,0:T(8,128)S(1)}, u32[]{:S(2)}, u32[]{:S(2)}) collective-permute-start(f32[72,256]{1,0:T(8,128)S(1)} %get-tuple-element.11), channel_id=1, source_target_pairs={{0,4},{4,8},{8,12},{12,16},{16,20},{20,24},{24,28},{28,32},{32,36}... | collective-permute-start | bytes 221192 | tf_op jit(solution)/shard_map/ppermute | solution.py:313
  18.3 6.5 %collective-permute-start.3 = (f32[72,256]{1,0:T(8,128)S(1)}, f32[72,256]{1,0:T(8,128)S(1)}, u32[]{:S(2)}, u32[]{:S(2)}) collective-permute-start(f32[72,256]{1,0:T(8,128)S(1)} %get-tuple-element.12), channel_id=1, source_target_pairs={{4,0},{8,4},{12,8},{16,12},{20,16},{24,20},{28,24},{32,28},{36,32}... | collective-permute-start | bytes 221192 | tf_op jit(solution)/shard_map/ppermute | solution.py:314
  24.8 1.6 %collective-permute-done.2.left = f32[72,256]{1,0:T(8,128)S(1)} collective-permute-done((f32[72,256]{1,0:T(8,128)S(1)}, f32[72,256]{1,0:T(8,128)S(1)}, u32[]{:S(2)}, u32[]{:S(2)}) %collective-permute-start.2) | collective-permute-done | bytes 73760 | tf_op jit(solution)/shard_map/ppermute | solution.py:313
  26.4 0.0 collective-permute-done.3.right
  26.4 2.7 %inner.1 = f32[1024,128]{1,0:T(8,128)S(1)} custom-call(s32[2]{0:T(128)S(1)} %add_convert_fusion.flag, f32[4,32,16,256]{3,2,1,0:T(8,128)S(1)} %copy-done.1, f32[136,256]{1,0:T(8,128)S(1)} %collective-permute-done.low, f32[136,256]{1,0:T(8,128)S(1)} %collective-permute-done.1.high, f32[72,256]{1,0:T(8,128)S(1)} %collective-permute-done.2.left, ...), custom_call_target="tpu_custom_call" | custom-call | flops 10000000 | bytes 6000000 | tf_op jit(solution)/shard_map/inner/pallas_call | solution.py:321
  29.2 23.2 %all_to_all.10 = f32[64,16,128]{2,1,0:T(8,128)S(1)} all-to-all(f32[64,16,128]{2,1,0:T(8,128)S(1)} %bitcast.9), channel_id=1, replica_groups=mesh['y'=4,'x'=2,'z'=8,'hx'=2,'core'=2] {'y','z','x'}, dimensions={0} | all-to-all | bytes 1048576 | tf_op jit(solution)/shard_map/all_to_all | solution.py:331
  52.4 0.0 copy-done.4
  52.4 2.0 %filter.1 = f32[1024,128]{1,0:T(8,128)} custom-call(bf16[2,128,512]{2,1,0:T(8,128)(2,1)S(1)} %copy-done.3, bf16[2,128,512]{2,1,0:T(8,128)(2,1)S(1)} %copy-done.2, f32[2,64,128]{2,1,0:T(8,128)S(1)} %copy-done.4, s32[1,64]{1,0:T(1,128)S(1)} %bitcast.10, f32[1024,128]{1,0:T(8,128)S(1)} %bitcast.8), custom_call_target="tpu_custom_call" | custom-call | tf_op jit(solution)/shard_map/filter/pallas_call | solution.py:342
  54.4 5.6 %all-to-all-start.1 = ((f32[64,16,128]{2,1,0:T(8,128)}), f32[64,16,128]{2,1,0:T(8,128)S(1)}, u32[]{:S(2)}, u32[]{:S(2)}) async-start(f32[64,16,128]{2,1,0:T(8,128)} %bitcast.5), calls=%async_computation.1 | async-start | bytes 1048576 | tf_op jit(solution)/shard_map/all_to_all | solution.py:345
  60.0 4.2 %outer.1.stepped = f32[4,32,16,256]{3,2,1,0:T(8,128)} custom-call(s32[2]{0:T(128)S(1)} %add_convert_fusion.flag, f32[4,32,16,256]{3,2,1,0:T(8,128)S(1)} %copy-done.1, f32[136,256]{1,0:T(8,128)S(1)} %collective-permute-done.low, f32[136,256]{1,0:T(8,128)S(1)} %collective-permute-done.1.high, f32[72,256]{1,0:T(8,128)S(1)} %collective-permute-done.2.left, ...), custom_call_target="tpu_custom_call" | custom-call | flops 20000000 | bytes 20000000 | tf_op jit(solution)/shard_map/outer/pallas_call | solution.py:332
  64.2 13.5 %all-to-all-done.1 = f32[64,16,128]{2,1,0:T(8,128)S(1)} async-done(((f32[64,16,128]{2,1,0:T(8,128)}), f32[64,16,128]{2,1,0:T(8,128)S(1)}, u32[]{:S(2)}, u32[]{:S(2)}) %all-to-all-start.1) | async-done | bytes 524320 | tf_op jit(solution)/shard_map/all_to_all | solution.py:345
  77.7 2.1 %merge.1 = f32[4,32,16,256]{3,2,1,0:T(8,128)} custom-call(f32[4,32,16,256]{3,2,1,0:T(8,128)} %outer.1.stepped, f32[1024,128]{1,0:T(8,128)S(1)} %bitcast.7), custom_call_target="tpu_custom_call", output_to_operand_aliasing={{}: (0, {})} | custom-call | tf_op jit(solution)/shard_map/merge/pallas_call | solution.py:346
  (15 shorter events, 0.0 us)
Async XLA Ops:
  0.0 1.6 %copy-start = (f32[4,32,16,256]{3,2,1,0:T(8,128)S(1)}, f32[4,32,16,256]{3,2,1,0:T(8,128)}, u32[]{:S(2)}) copy-start(f32[4,32,16,256]{3,2,1,0:T(8,128)} %state.9) | copy-start | bytes 6291460
  1.6 8.4 %copy-start.1 = (f32[4,32,16,256]{3,2,1,0:T(8,128)S(1)}, f32[4,32,16,256]{3,2,1,0:T(8,128)}, u32[]{:S(2)}) copy-start(f32[4,32,16,256]{3,2,1,0:T(8,128)} %state.9) | copy-start | bytes 6291460
  1.6 8.4 %copy-start.8 = (f32[8]{0:T(128)S(1)}, f32[8]{0:T(128)}, u32[]{:S(2)}) copy-start(f32[8]{0:T(128)} %resistance.1) | copy-start | bytes 100
  1.6 8.4 %copy-start.9 = (f32[8]{0:T(128)S(1)}, f32[8]{0:T(128)}, u32[]{:S(2)}) copy-start(f32[8]{0:T(128)} %relax.1) | copy-start | bytes 100
  1.8 10.4 %collective-permute-start = (f32[136,256]{1,0:T(8,128)S(1)}, f32[136,256]{1,0:T(8,128)S(1)}, u32[]{:S(2)}, u32[]{:S(2)}) collective-permute-start(f32[136,256]{1,0:T(8,128)S(1)} %get-tuple-element.9), channel_id=1, source_target_pairs={{0,1},{1,2},{2,3},{4,5},{5,6},{6,7},{8,9},{9,10},{10,11},{12,13},{... | collective-permute-start | bytes 417800 | tf_op jit(solution)/shard_map/ppermute | solution.py:297
  8.0 7.9 %collective-permute-start.1 = (f32[136,256]{1,0:T(8,128)S(1)}, f32[136,256]{1,0:T(8,128)S(1)}, u32[]{:S(2)}, u32[]{:S(2)}) collective-permute-start(f32[136,256]{1,0:T(8,128)S(1)} %get-tuple-element.10), channel_id=1, source_target_pairs={{1,0},{2,1},{3,2},{5,4},{6,5},{7,6},{9,8},{10,9},{11,10},{13,12},{... | collective-permute-start | bytes 417800 | tf_op jit(solution)/shard_map/ppermute | solution.py:298
  10.0 0.8 copy-start.5
  10.7 0.8 copy-start.6
  16.5 9.9 %collective-permute-start.2 = (f32[72,256]{1,0:T(8,128)S(1)}, f32[72,256]{1,0:T(8,128)S(1)}, u32[]{:S(2)}, u32[]{:S(2)}) collective-permute-start(f32[72,256]{1,0:T(8,128)S(1)} %get-tuple-element.11), channel_id=1, source_target_pairs={{0,4},{4,8},{8,12},{12,16},{16,20},{20,24},{24,28},{28,32},{32,36}... | collective-permute-start | bytes 221192 | tf_op jit(solution)/shard_map/ppermute | solution.py:313
  18.2 34.1 %copy-start.2 = (bf16[2,128,512]{2,1,0:T(8,128)(2,1)S(1)}, bf16[2,128,512]{2,1,0:T(8,128)(2,1)}, u32[]{:S(2)}) copy-start(bf16[2,128,512]{2,1,0:T(8,128)(2,1)} %constant.19.clone.small) | copy-start | bytes 786436
  18.2 34.1 %copy-start.3 = (bf16[2,128,512]{2,1,0:T(8,128)(2,1)S(1)}, bf16[2,128,512]{2,1,0:T(8,128)(2,1)}, u32[]{:S(2)}) copy-start(bf16[2,128,512]{2,1,0:T(8,128)(2,1)} %constant.18.clone.large) | copy-start | bytes 786436
  18.2 34.1 %copy-start.4 = (f32[2,64,128]{2,1,0:T(8,128)S(1)}, f32[2,64,128]{2,1,0:T(8,128)}, u32[]{:S(2)}) copy-start(f32[2,64,128]{2,1,0:T(8,128)} %constant.20.clone.turn) | copy-start | bytes 196612
  18.2 34.1 %copy-start.7 = (s32[64]{0:T(128)S(1)}, s32[64]{0:T(128)}, u32[]{:S(2)}) copy-start(s32[64]{0:T(128)} %param.14) | copy-start | bytes 772
  18.3 8.2 %collective-permute-start.3 = (f32[72,256]{1,0:T(8,128)S(1)}, f32[72,256]{1,0:T(8,128)S(1)}, u32[]{:S(2)}, u32[]{:S(2)}) collective-permute-start(f32[72,256]{1,0:T(8,128)S(1)} %get-tuple-element.12), channel_id=1, source_target_pairs={{4,0},{8,4},{12,8},{16,12},{20,16},{24,20},{28,24},{32,28},{36,32}... | collective-permute-start | bytes 221192 | tf_op jit(solution)/shard_map/ppermute | solution.py:314
  54.4 23.4 %all-to-all-start.1 = ((f32[64,16,128]{2,1,0:T(8,128)}), f32[64,16,128]{2,1,0:T(8,128)S(1)}, u32[]{:S(2)}, u32[]{:S(2)}) async-start(f32[64,16,128]{2,1,0:T(8,128)} %bitcast.5), calls=%async_computation.1 | async-start | bytes 1048576 | tf_op jit(solution)/shard_map/all_to_all | solution.py:345

commit v2 on v1

--- a/solution.py
+++ b/solution.py
@@ -16,6 +16,7 @@
 SECTORS = 64
 ROWS = NA // SECTORS
 HALF = ROWS // 2
+LONG = HALF + 1
 HTS = 16
 NR = 256
 COMPS = 4
@@ -32,19 +33,25 @@
 
 
 def mode_tables():
-    azimuth = (sector_of_chunk()[: SECTORS // 2, None] * ROWS + np.arange(HALF)[None, :]).reshape(-1)
+    first = sector_of_chunk()[: SECTORS // 2, None] * ROWS
+    there = (first - 1 + np.arange(LONG)[None, :]).reshape(-1)
+    back = (first + np.arange(HALF)[None, :]).reshape(-1)
     tables = []
     for parity in range(2):
         modes = np.arange(parity, MODES, 2)
-        phase = (modes[:, None] * azimuth[None, :] % NA) * (2.0 * math.pi / NA)
-        turn = (modes * HALF % NA) * (2.0 * math.pi / NA)
+        waves = []
+        for azimuth in (there, back):
+            phase = (modes[:, None] * azimuth[None, :] % NA) * (2.0 * math.pi / NA)
+            waves.append(np.concatenate([np.cos(phase), np.sin(phase)], 0))
         more = np.zeros((MODES // 2, 128))
-        more[:, 0] = np.cos(turn)
-        more[:, 1] = np.sin(turn)
-        more[:, 2] = np.where(modes == 0, 1.0, 2.0) / NA
-        tables.append((np.concatenate([np.cos(phase), np.sin(phase)], 0), more))
-    waves, turns = [np.stack(t).astype(np.float32) for t in zip(*tables)]
-    return (*split(waves), turns)
+        for k, by in enumerate((LONG, HALF)):
+            turn = (modes * by % NA) * (2.0 * math.pi / NA)
+            more[:, 2 * k] = np.cos(turn)
+            more[:, 2 * k + 1] = np.sin(turn)
+        more[:, 4] = np.where(modes == 0, 1.0, 2.0) / NA
+        tables.append((*waves, more))
+    there, back, turns = [np.stack(t).astype(np.float32) for t in zip(*tables)]
+    return (*split(there), *split(back), turns)
 
 
 def split(x):
@@ -90,10 +97,10 @@
 
 
 HT_ROWS = 136
-AZ_ROWS = 72
-
-
-def pack_kernel(state, up, down):
+AZ_ROWS = 64
+
+
+def pack_kernel(state, up, down, to_left, to_right):
     inv_r, half_arc = radial_rates(NR)
     zero = jnp.zeros((1, NR), jnp.float32)
     for out, edge, inside, sign in ((up, HTS - 1, HTS - 2, 1.0), (down, 0, 1, -1.0)):
@@ -108,6 +115,14 @@
         out[129:130] = v[ROWS - 1 : ROWS]
         out[130:HT_ROWS] = jnp.zeros((HT_ROWS - 130, NR), jnp.float32)
 
+    for out, j, inside, sign in ((to_right, ROWS - 1, ROWS - 2, 1.0), (to_left, 0, 1, -1.0)):
+        p, u, v, w = [state[i, j] for i in range(4)]
+        out[0:16] = p
+        out[16:32] = v
+        rate = radial_diff(u) + u * inv_r + row_diff(w, zero, zero) - sign * half_arc * state[2, inside]
+        out[32:48] = p - DT * rate
+        out[48:64] = v + (DT * sign) * half_arc * state[0, inside]
+
 
 def ground_kernel(resistance, relax, state, zone, aux, ground):
     ids, q = zone[...], aux[...]
@@ -118,23 +133,7 @@
     ground[2] = q + DT * lookup(ids, relax) * (p0 - q)
 
 
-def edge_kernel(flag, state, low, high, ground, to_left, to_right):
-    inv_r, half_arc = radial_rates(NR)
-    on_ground = flag[0] == 1
-    for out, j, inside, sign, corner in ((to_right, ROWS - 1, ROWS - 2, 1.0, 129), (to_left, 0, 1, -1.0, 128)):
-        p, u, v, w = [state[i, j] for i in range(4)]
-        w_low = jnp.where(on_ground, ground[0, j : j + 1], low[32 + j : 33 + j])
-        out[0:16] = p
-        out[16:32] = v
-        rate = radial_diff(u) + u * inv_r + row_diff(w, w_low, high[32 + j : 33 + j]) - sign * half_arc * state[2, inside]
-        out[32:48] = p - DT * rate
-        out[48:64] = v + (DT * sign) * half_arc * state[0, inside]
-        out[64:65] = low[corner : corner + 1]
-        out[65:66] = high[corner : corner + 1]
-        out[66:AZ_ROWS] = jnp.zeros((AZ_ROWS - 66, NR), jnp.float32)
-
-
-def two_stages(width, flag, state, low, high, left, right, ground, mid, ghost, emit):
+def two_stages(width, flag, state, low, high, left, right, ground, mid, ghost):
     on_ground, on_top = flag[0] == 1, flag[1] == 1
     inv_r, half_arc = radial_rates(width)
     cols = slice(0, width)
@@ -146,16 +145,9 @@
     bw = jnp.where(on_ground, ground[0, :, cols], low[32:64, cols])
     ghost[0], ghost[1], ghost[2], ghost[3] = bp, bw, high[0:32, cols], high[32:64, cols]
 
-    sub = lax.broadcasted_iota(jnp.int32, (ROWS, width), 0)
-
-    def corners(k):
-        return turn * jnp.where(
-            sub == 0, left[k : k + 1, cols], jnp.where(sub == ROWS - 1, -right[k : k + 1, cols], 0.0)
-        )
-
-    top_p = high[64:96, cols] + (0.5 * DT) * w15 + corners(65)
+    top_p = high[64:96, cols] + (0.5 * DT) * w15
     top_w = high[96:128, cols] + (0.5 * DT) * p15
-    low_p = low[64:96, cols] - (0.5 * DT) * w0 + corners(64)
+    low_p = low[64:96, cols] - (0.5 * DT) * w0
     low_w = low[96:128, cols] - (0.5 * DT) * p0
     v_diff = 2.0 * row_diff(v0, left[16:17, cols], right[16:17, cols]) * half_arc
     mid_p0 = p0 - DT * (radial_diff(u0) + u0 * inv_r + v_diff + 0.5 * (w1 - bw))
@@ -201,34 +193,68 @@
         found = rates(p, u, mid[2, j + 2] - mid[2, j], mid[0, j + 2] - mid[0, j], w, j, 4)
         return [0.5 * (state[i, j, :, cols] + m - DT * r) for i, (m, r) in enumerate(zip((p, u, v, w), found))]
 
-    @pl.loop(0, HALF, unroll=2)
-    def _(l):
-        emit(l, second(l), second(l + HALF))
-
-
-def inner_kernel(flag, state, low, high, left, right, ground, packed, mid, ghost):
+    return second
+
+
+def corner_weight(width):
+    return (0.5 * DT) * (0.5 * DT) * radial_rates(width)[1]
+
+
+def inner_kernel(flag, state, low, high, left, right, ground, packed, to_left, to_right, mid, ghost):
     near = lax.broadcasted_iota(jnp.int32, (HTS, 128), 1) < NI
-
-    def emit(l, one, two):
+    height = lax.broadcasted_iota(jnp.int32, (HTS, 128), 0)
+    second = two_stages(128, flag, state, low, high, left, right, ground, mid, ghost)
+
+    def emit(r, one, two):
         for i in range(COMPS):
             both = jnp.where(near, one[i], pltpu.roll(two[i], NI, 1))
-            packed[pl.ds(i * HTS * HALF + l, HTS, stride=HALF), :] = both
-
-    two_stages(128, flag, state, low, high, left, right, ground, mid, ghost, emit)
-
-
-def outer_kernel(flag, state, low, high, left, right, ground, stepped, mid, ghost):
-    def emit(l, one, two):
-        for i in range(COMPS):
-            stepped[i, l] = one[i]
-            stepped[i, l + HALF] = two[i]
-
-    two_stages(NR, flag, state, low, high, left, right, ground, mid, ghost, emit)
-
-
-def filter_kernel(large, small, turn, cutoff, x_ref, o_ref):
-    n = NA // 4
-    first, second = x_ref[:n], x_ref[n:]
+            packed[pl.ds(i * HTS * LONG + r, HTS, stride=LONG), :] = both
+
+    @pl.loop(0, HALF - 1, unroll=3)
+    def _(l):
+        emit(l + 1, second(l), second(l + LONG))
+
+    weight = corner_weight(128)
+
+    def beyond(row):
+        at, end = 32 + row * (ROWS - 1), row * (ROWS - 1)
+        w_low = jnp.where(flag[0] == 1, ground[0, end : end + 1], low[at : at + 1])
+        return (w_low, high[at : at + 1]), (low[128 + row : 129 + row], high[128 + row : 129 + row])
+
+    def owed(row, sign):
+        out = [jnp.zeros((HTS, 128), jnp.float32)] * 2
+        for below, above in beyond(row):
+            below, above = [(by * weight) * x[:, 0:128] for by, x in ((-sign, below), (sign, above))]
+            out.append(jnp.where(height == HTS - 1, above, jnp.where(height == 0, below, 0.0)))
+        return out
+
+    emit(0, owed(0, 1.0), second(HALF))
+    emit(HALF, second(HALF - 1), owed(1, -1.0))
+
+    for out, row in ((to_left, 0), (to_right, 1)):
+        (w_low, w_high), (v_low, v_high) = beyond(row)
+        out[...] = jnp.concatenate([w_low, w_high, v_low, v_high, jnp.zeros((4, NR), jnp.float32)], 0)
+
+
+def outer_kernel(flag, state, low, high, left, right, ground, left_corner, right_corner, stepped, mid, ghost):
+    second = two_stages(NR, flag, state, low, high, left, right, ground, mid, ghost)
+
+    @pl.loop(0, ROWS, unroll=2)
+    def _(j):
+        for i, value in enumerate(second(j)):
+            stepped[i, j] = value
+
+    weight = corner_weight(NR)
+    for j, corner, sign in ((0, left_corner, -1.0), (ROWS - 1, right_corner, 1.0)):
+        for i, k in ((2, 0), (3, 2)):
+            stepped[i, j, 0:1] = stepped[i, j, 0:1] - (sign * weight) * corner[k : k + 1]
+            end = slice(HTS - 1, HTS)
+            stepped[i, j, end] = stepped[i, j, end] + (sign * weight) * corner[k + 1 : k + 2]
+
+
+def filter_kernel(there, there_small, back, back_small, turn, cutoff, x_ref, o_ref):
+    n, m = NA // 4, SECTORS // 2 * LONG
+    first, second = x_ref[:m], x_ref[m:]
     h = MODES // 2
     mode = lax.broadcasted_iota(jnp.int32, (h, 128), 0) * 2
     near = lax.broadcasted_iota(jnp.int32, (h, 128), 1) < NI
@@ -236,19 +262,18 @@
     outs = []
     for parity in range(2):
         folded = first + second if parity == 0 else first - second
-        waves = large[parity], small[parity]
-        cs, sn, weight = [turn[parity, :, k : k + 1] for k in range(3)]
-        coef = product(waves, split(folded), ((1,), (0,)))
+        cs, sn, cs_back, sn_back, weight = [turn[parity, :, k : k + 1] for k in range(5)]
+        coef = product((there[parity], there_small[parity]), split(folded), ((1,), (0,)))
         a, b = coef[:h], coef[h:]
         a_all = jnp.where(near, a, a * cs - b * sn)
         b_all = jnp.where(near, b, a * sn + b * cs)
         keep = jnp.where(mode + parity < limit, weight, 0.0)
         a_all = (a_all + pltpu.roll(a_all, NI, 1)) * keep
         b_all = (b_all + pltpu.roll(b_all, NI, 1)) * keep
-        a_back = jnp.where(near, a_all, a_all * cs + b_all * sn)
-        b_back = jnp.where(near, b_all, b_all * cs - a_all * sn)
-        back = jnp.concatenate([a_back, b_back], 0)
-        outs.append(product(waves, split(back), ((0,), (0,))))
+        a_back = jnp.where(near, a_all, a_all * cs_back + b_all * sn_back)
+        b_back = jnp.where(near, b_all, b_all * cs_back - a_all * sn_back)
+        both = jnp.concatenate([a_back, b_back], 0)
+        outs.append(product((back[parity], back_small[parity]), split(both), ((0,), (0,))))
     o_ref[:n] = outs[0] + outs[1]
     o_ref[n:] = outs[0] - outs[1]
 
@@ -291,11 +316,13 @@
     def shapes(*dims):
         return tuple(jax.ShapeDtypeStruct(d, f32) for d in dims)
 
-    up, down = call(
-        pack_kernel, out_shape=shapes((HT_ROWS, NR), (HT_ROWS, NR)), in_specs=[vmem], out_specs=(vmem, vmem), name="pack"
+    up, down, to_left, to_right = call(
+        pack_kernel,
+        out_shape=shapes((HT_ROWS, NR), (HT_ROWS, NR), (AZ_ROWS, NR), (AZ_ROWS, NR)),
+        in_specs=[vmem],
+        out_specs=(vmem,) * 4,
+        name="pack",
     )(state)
-    low = lax.ppermute(up, HT, [(i, i + 1) for i in range(3)])
-    high = lax.ppermute(down, HT, [(i + 1, i) for i in range(3)])
     ground = call(
         ground_kernel,
         out_shape=shapes((3, ROWS, NR))[0],
@@ -303,45 +330,43 @@
         out_specs=vmem,
         name="ground",
     )(resistance, relax_rate, state, zone_id, ground_aux)
-    to_left, to_right = call(
-        edge_kernel,
-        out_shape=shapes((AZ_ROWS, NR), (AZ_ROWS, NR)),
-        in_specs=[smem] + [vmem] * 4,
-        out_specs=(vmem, vmem),
-        name="edge",
-    )(flags, state, low, high, ground)
-    left = lax.ppermute(to_right, AZ, [(i, (i + 1) % SECTORS) for i in range(SECTORS)])
-    right = lax.ppermute(to_left, AZ, [((i + 1) % SECTORS, i) for i in range(SECTORS)])
+    to_next, to_last = [(i, (i + 1) % SECTORS) for i in range(SECTORS)], [((i + 1) % SECTORS, i) for i in range(SECTORS)]
+    low = lax.ppermute(up, HT, [(i, i + 1) for i in range(3)])
+    high = lax.ppermute(down, HT, [(i + 1, i) for i in range(3)])
+    left = lax.ppermute(to_right, AZ, to_next)
+    right = lax.ppermute(to_left, AZ, to_last)
 
     operands = (flags, state, low, high, left, right, ground)
 
     def scratch(width):
         return [pltpu.VMEM((COMPS, ROWS + 2, HTS, width), f32), pltpu.VMEM((8, ROWS, width), f32)]
 
-    packed = call(
+    packed, to_left, to_right = call(
         inner_kernel,
         mib=12,
-        out_shape=shapes((COMPS * HTS * HALF, 128))[0],
+        out_shape=shapes((COMPS * HTS * LONG, 128), (8, NR), (8, NR)),
         in_specs=[smem] + [vmem] * 6,
-        out_specs=vmem,
+        out_specs=(vmem,) * 3,
         scratch_shapes=scratch(128),
         cost_estimate=pl.CostEstimate(flops=10**7, bytes_accessed=6 * 10**6, transcendentals=0),
         name="inner",
     )(*operands)
-    circle = lax.all_to_all(packed.reshape(SECTORS, HALF, 128), SPREAD, 0, 0, tiled=True)
+    circle = lax.all_to_all(packed.reshape(SECTORS, LONG, 1, 128), SPREAD, 0, 0, tiled=True)
+    left_corner = lax.ppermute(to_right, AZ, to_next)
+    right_corner = lax.ppermute(to_left, AZ, to_last)
     stepped = call(
         outer_kernel,
         mib=16,
         out_shape=shapes((COMPS, ROWS, HTS, NR))[0],
-        in_specs=[smem] + [vmem] * 6,
+        in_specs=[smem] + [vmem] * 8,
         out_specs=vmem,
         scratch_shapes=scratch(NR),
         cost_estimate=pl.CostEstimate(flops=2 * 10**7, bytes_accessed=2 * 10**7, transcendentals=0),
         name="outer",
-    )(*operands)
+    )(*operands, left_corner, right_corner)
     kept = call(
-        filter_kernel, out_shape=shapes((NA // 2, 128))[0], in_specs=[vmem] * 5, out_specs=vmem, name="filter"
-    )(*map(jnp.asarray, mode_tables()), cutoff.reshape(1, NI), circle.reshape(NA // 2, 128))
+        filter_kernel, out_shape=shapes((NA // 2, 128))[0], in_specs=[vmem] * 7, out_specs=vmem, name="filter"
+    )(*map(jnp.asarray, mode_tables()), cutoff.reshape(1, NI), circle.reshape(SECTORS * LONG, 128))
     back = lax.all_to_all(kept.reshape(SECTORS, HALF, 128), SPREAD, 0, 0, tiled=True)
     return call(
         merge_kernel,

time: 80.3 us -> 78 us (0.971)
  waiting for transfers between devices: 18.8 us -> 8.96 us
  starting transfers between devices: 22 us -> 27.8 us
  blocking collectives: 23.2 us -> 25.2 us
    all_to_all x1, waiting for transfers between devices: 13.5 us -> 0.01 us  [per_device(): lax.all_to_all(kept.reshape(SECTORS, HALF, 128), SPREAD, 0, 0, tiled=True)]
    ppermute x2 -> x4, waiting for transfers between devices: 1.61 us -> 8.96 us  [the longest x1 8.95 us: per_device(): left_corner = lax.ppermute(to_right, AZ, to_next)]
    ppermute x2 -> x4, starting transfers between devices: 8.26 us -> 14 us  [the longest x1 6.51 us: per_device(): right = lax.ppermute(to_left, AZ, to_last)]
    ppermute x1, waiting for transfers between devices: 3.69 us -> 0.01 us  [per_device(): high = lax.ppermute(down, HT, [(i + 1, i) for i in range(3)])]
    all_to_all x1, blocking collectives: 23.2 us -> 25.2 us  [per_device(): lax.all_to_all(packed.reshape(SECTORS, LONG, 1, 128), SPREAD, 0, 0, tiled...]
    pallas_call x3 -> x2, Pallas kernels: 3.6 us -> 2.63 us  [the longest x1 2.38 us: per_device(): call(inner_kernel, mib=12, out_shape=shapes((COMPS * HTS * LONG, 128), (8...]
    unnamed x20 -> x24, local copies, waits for them, and re-layouts: 3.13 us -> 3.15 us
  transfers between devices with their start and end apart: 5 -> 7, of which waited for: 3 -> 1; matrix products, arithmetic and copies ran while one was open for 0% -> 0% of each run, Pallas kernels for 6% -> 7%
where the time goes in v2:
time: 78 us; the launch traced here: 77.6 us
  starting transfers between devices  27.8 us (36%)
  blocking collectives  25.2 us (32%)
  Pallas kernels  12.3 us (16%)
  waiting for transfers between devices  8.96 us (11%)
  local copies, waits for them, and re-layouts  3.15 us (4%)
    all_to_all x1, blocking collectives, per_device(): lax.all_to_all(packed.reshape(SECTORS, LONG, 1, 128), SPREAD, 0, 0, tiled...  25.2 us
    ppermute x1, waiting for transfers between devices, per_device(): left_corner = lax.ppermute(to_right, AZ, to_next)  8.95 us
    ppermute x1, starting transfers between devices, per_device(): right = lax.ppermute(to_left, AZ, to_last)  6.51 us
    ppermute x1, starting transfers between devices, per_device(): low = lax.ppermute(up, HT, [(i, i + 1) for i in range(3)])  6.17 us
    all_to_all x1, starting transfers between devices, per_device(): lax.all_to_all(kept.reshape(SECTORS, HALF, 128), SPREAD, 0, 0, tiled=True)  5.75 us
    pallas_call x1, Pallas kernels, per_device(): call(outer_kernel, mib=16, out_shape=shapes((COMPS, ROWS, HTS, NR))[0], i...  4.81 us
    ppermute x1, starting transfers between devices, per_device(): right_corner = lax.ppermute(to_left, AZ, to_last)  4.69 us
    unnamed x24, local copies, waits for them, and re-layouts  3.15 us
  transfers between devices with their start and end apart: 7, of which 1 were waited for; matrix products, arithmetic and copies ran while one was open for 0% of the time, Pallas kernels for 7%

profile of v2, /device:TPU:1, one launch (start us, length us, event | category | flops | bytes accessed | tf_op | source)
XLA Modules:
  0.0 77.6 jit_solution(15057083604945041636)
XLA Ops:
  0.0 1.6 %copy-done = f32[4,32,16,256]{3,2,1,0:T(8,128)S(1)} copy-done((f32[4,32,16,256]{3,2,1,0:T(8,128)S(1)}, f32[4,32,16,256]{3,2,1,0:T(8,128)}, u32[]{:S(2)}) %copy-start) | copy-done | bytes 2097176
  1.6 0.3 pack.1
  1.9 6.2 %collective-permute-start = (f32[136,256]{1,0:T(8,128)S(1)}, f32[136,256]{1,0:T(8,128)S(1)}, u32[]{:S(2)}, u32[]{:S(2)}) collective-permute-start(f32[136,256]{1,0:T(8,128)S(1)} %get-tuple-element.12), channel_id=1, source_target_pairs={{0,1},{1,2},{2,3},{4,5},{5,6},{6,7},{8,9},{9,10},{10,11},{12,13},{... | collective-permute-start | bytes 417800 | tf_op jit(solution)/shard_map/ppermute | solution.py:334
  8.0 1.9 %collective-permute-start.1 = (f32[136,256]{1,0:T(8,128)S(1)}, f32[136,256]{1,0:T(8,128)S(1)}, u32[]{:S(2)}, u32[]{:S(2)}) collective-permute-start(f32[136,256]{1,0:T(8,128)S(1)} %get-tuple-element.13), channel_id=1, source_target_pairs={{1,0},{2,1},{3,2},{5,4},{6,5},{7,6},{9,8},{10,9},{11,10},{13,12},{... | collective-permute-start | bytes 417800 | tf_op jit(solution)/shard_map/ppermute | solution.py:335
  10.0 1.7 %collective-permute-start.2 = (f32[64,256]{1,0:T(8,128)S(1)}, f32[64,256]{1,0:T(8,128)S(1)}, u32[]{:S(2)}, u32[]{:S(2)}) collective-permute-start(f32[64,256]{1,0:T(8,128)S(1)} %get-tuple-element.14), channel_id=1, source_target_pairs={{0,4},{4,8},{8,12},{12,16},{16,20},{20,24},{24,28},{28,32},{32,36}... | collective-permute-start | bytes 196616 | tf_op jit(solution)/shard_map/ppermute | solution.py:336
  11.7 6.5 %collective-permute-start.3 = (f32[64,256]{1,0:T(8,128)S(1)}, f32[64,256]{1,0:T(8,128)S(1)}, u32[]{:S(2)}, u32[]{:S(2)}) collective-permute-start(f32[64,256]{1,0:T(8,128)S(1)} %get-tuple-element.15), channel_id=1, source_target_pairs={{4,0},{8,4},{12,8},{16,12},{20,16},{24,20},{28,24},{32,28},{36,32}... | collective-permute-start | bytes 196616 | tf_op jit(solution)/shard_map/ppermute | solution.py:337
  18.2 0.8 copy-done.7
  19.0 0.8 copy-done.8
  19.7 0.6 ground.1
  20.3 0.0 copy-start.2
  20.3 0.0 copy-start.3
  20.4 0.0 copy-start.4
  20.4 0.0 copy-start.5
  20.4 0.0 copy-start.6
  20.4 0.1 add_convert_fusion.flag
  20.5 2.4 %inner.1 = (f32[1088,128]{1,0:T(8,128)S(1)}, f32[8,256]{1,0:T(8,128)S(1)}, f32[8,256]{1,0:T(8,128)S(1)}) custom-call(s32[2]{0:T(128)S(1)} %add_convert_fusion.flag, f32[4,32,16,256]{3,2,1,0:T(8,128)S(1)} %copy-done.1, f32[136,256]{1,0:T(8,128)S(1)} %collective-permute-done.low, f32[136,256]{1,0:T(8,128)S(1)} %collective-permute-done.1.high, ...), custom_call_target="tpu_custom_call" | custom-call | flops 10000000 | bytes 6000000 | tf_op jit(solution)/shard_map/inner/pallas_call | solution.py:344
  22.9 25.2 %all_to_all.10 = f32[64,17,1,128]{3,2,1,0:T(1,128)S(1)} all-to-all(f32[64,17,1,128]{3,2,1,0:T(1,128)S(1)} %bitcast.9), channel_id=1, replica_groups=mesh['y'=4,'x'=2,'z'=8,'hx'=2,'core'=2] {'y','z','x'}, dimensions={0} | all-to-all | bytes 1114112 | tf_op jit(solution)/shard_map/all_to_all | solution.py:354
  48.1 2.1 %filter.1 = f32[1024,128]{1,0:T(8,128)} custom-call(bf16[2,128,544]{2,1,0:T(8,128)(2,1)S(1)} %copy-done.3, bf16[2,128,544]{2,1,0:T(8,128)(2,1)S(1)} %copy-done.2, bf16[2,128,512]{2,1,0:T(8,128)(2,1)S(1)} %copy-done.5, bf16[2,128,512]{2,1,0:T(8,128)(2,1)S(1)} %copy-done.4, f32[2,64,128]{2,1,0:T(8,128)S(1)} %copy-done.6, s32[1,64]{1,0:T(1,128)S(1)} %bitcast.10, ...), custom_call_target="tpu_custom_call" | custom-call | tf_op jit(solution)/shard_map/filter/pallas_call | solution.py:367
  50.2 5.8 %all-to-all-start.1 = ((f32[64,16,128]{2,1,0:T(8,128)}), f32[64,16,128]{2,1,0:T(8,128)S(1)}, u32[]{:S(2)}, u32[]{:S(2)}) async-start(f32[64,16,128]{2,1,0:T(8,128)} %bitcast.5), calls=%async_computation.1 | async-start | bytes 1048576 | tf_op jit(solution)/shard_map/all_to_all | solution.py:370
  55.9 1.1 %collective-permute-start.4 = (f32[8,256]{1,0:T(8,128)S(1)}, f32[8,256]{1,0:T(8,128)S(1)}, u32[]{:S(2)}, u32[]{:S(2)}) collective-permute-start(f32[8,256]{1,0:T(8,128)S(1)} %get-tuple-element.16), channel_id=1, source_target_pairs={{0,4},{4,8},{8,12},{12,16},{16,20},{20,24},{24,28},{28,32},{32,36}... | collective-permute-start | bytes 24584 | tf_op jit(solution)/shard_map/ppermute | solution.py:355
  57.0 4.7 %collective-permute-start.5 = (f32[8,256]{1,0:T(8,128)S(1)}, f32[8,256]{1,0:T(8,128)S(1)}, u32[]{:S(2)}, u32[]{:S(2)}) collective-permute-start(f32[8,256]{1,0:T(8,128)S(1)} %get-tuple-element.17), channel_id=1, source_target_pairs={{4,0},{8,4},{12,8},{16,12},{20,16},{24,20},{28,24},{32,28},{36,32}... | collective-permute-start | bytes 24584 | tf_op jit(solution)/shard_map/ppermute | solution.py:356
  61.7 8.9 %collective-permute-done.4.left_corner = f32[8,256]{1,0:T(8,128)S(1)} collective-permute-done((f32[8,256]{1,0:T(8,128)S(1)}, f32[8,256]{1,0:T(8,128)S(1)}, u32[]{:S(2)}, u32[]{:S(2)}) %collective-permute-start.4) | collective-permute-done | bytes 8224 | tf_op jit(solution)/shard_map/ppermute | solution.py:355
  70.7 4.8 %outer.1.stepped = f32[4,32,16,256]{3,2,1,0:T(8,128)} custom-call(s32[2]{0:T(128)S(1)} %add_convert_fusion.flag, f32[4,32,16,256]{3,2,1,0:T(8,128)S(1)} %copy-done.1, f32[136,256]{1,0:T(8,128)S(1)} %collective-permute-done.low, f32[136,256]{1,0:T(8,128)S(1)} %collective-permute-done.1.high, f32[64,256]{1,0:T(8,128)S(1)} %collective-permute-done.2.left, ...), custom_call_target="tpu_custom_call" | custom-call | flops 20000000 | bytes 20000000 | tf_op jit(solution)/shard_map/outer/pallas_call | solution.py:357
  75.5 2.1 %merge.1 = f32[4,32,16,256]{3,2,1,0:T(8,128)} custom-call(f32[4,32,16,256]{3,2,1,0:T(8,128)} %outer.1.stepped, f32[1024,128]{1,0:T(8,128)S(1)} %bitcast.8), custom_call_target="tpu_custom_call", output_to_operand_aliasing={{}: (0, {})} | custom-call | tf_op jit(solution)/shard_map/merge/pallas_call | solution.py:371
  (22 shorter events, 0.0 us)
Async XLA Ops:
  0.0 1.6 %copy-start = (f32[4,32,16,256]{3,2,1,0:T(8,128)S(1)}, f32[4,32,16,256]{3,2,1,0:T(8,128)}, u32[]{:S(2)}) copy-start(f32[4,32,16,256]{3,2,1,0:T(8,128)} %state.7) | copy-start | bytes 6291460
  1.6 16.6 %copy-start.1 = (f32[4,32,16,256]{3,2,1,0:T(8,128)S(1)}, f32[4,32,16,256]{3,2,1,0:T(8,128)}, u32[]{:S(2)}) copy-start(f32[4,32,16,256]{3,2,1,0:T(8,128)} %state.7) | copy-start | bytes 6291460
  1.6 16.6 %copy-start.10 = (f32[8]{0:T(128)S(1)}, f32[8]{0:T(128)}, u32[]{:S(2)}) copy-start(f32[8]{0:T(128)} %resistance.1) | copy-start | bytes 100
  1.6 16.6 %copy-start.11 = (f32[8]{0:T(128)S(1)}, f32[8]{0:T(128)}, u32[]{:S(2)}) copy-start(f32[8]{0:T(128)} %relax.1) | copy-start | bytes 100
  1.9 18.6 %collective-permute-start = (f32[136,256]{1,0:T(8,128)S(1)}, f32[136,256]{1,0:T(8,128)S(1)}, u32[]{:S(2)}, u32[]{:S(2)}) collective-permute-start(f32[136,256]{1,0:T(8,128)S(1)} %get-tuple-element.12), channel_id=1, source_target_pairs={{0,1},{1,2},{2,3},{4,5},{5,6},{6,7},{8,9},{9,10},{10,11},{12,13},{... | collective-permute-start | bytes 417800 | tf_op jit(solution)/shard_map/ppermute | solution.py:334
  8.0 12.5 %collective-permute-start.1 = (f32[136,256]{1,0:T(8,128)S(1)}, f32[136,256]{1,0:T(8,128)S(1)}, u32[]{:S(2)}, u32[]{:S(2)}) collective-permute-start(f32[136,256]{1,0:T(8,128)S(1)} %get-tuple-element.13), channel_id=1, source_target_pairs={{1,0},{2,1},{3,2},{5,4},{6,5},{7,6},{9,8},{10,9},{11,10},{13,12},{... | collective-permute-start | bytes 417800 | tf_op jit(solution)/shard_map/ppermute | solution.py:335
  10.0 10.5 %collective-permute-start.2 = (f32[64,256]{1,0:T(8,128)S(1)}, f32[64,256]{1,0:T(8,128)S(1)}, u32[]{:S(2)}, u32[]{:S(2)}) collective-permute-start(f32[64,256]{1,0:T(8,128)S(1)} %get-tuple-element.14), channel_id=1, source_target_pairs={{0,4},{4,8},{8,12},{12,16},{16,20},{20,24},{24,28},{28,32},{32,36}... | collective-permute-start | bytes 196616 | tf_op jit(solution)/shard_map/ppermute | solution.py:336
  11.7 8.8 %collective-permute-start.3 = (f32[64,256]{1,0:T(8,128)S(1)}, f32[64,256]{1,0:T(8,128)S(1)}, u32[]{:S(2)}, u32[]{:S(2)}) collective-permute-start(f32[64,256]{1,0:T(8,128)S(1)} %get-tuple-element.15), channel_id=1, source_target_pairs={{4,0},{8,4},{12,8},{16,12},{20,16},{24,20},{28,24},{32,28},{36,32}... | collective-permute-start | bytes 196616 | tf_op jit(solution)/shard_map/ppermute | solution.py:337
  18.2 0.8 copy-start.7
  19.0 0.8 copy-start.8
  20.3 27.7 %copy-start.2 = (bf16[2,128,544]{2,1,0:T(8,128)(2,1)S(1)}, bf16[2,128,544]{2,1,0:T(8,128)(2,1)}, u32[]{:S(2)}) copy-start(bf16[2,128,544]{2,1,0:T(8,128)(2,1)} %constant.23.clone.there_small) | copy-start | bytes 835588
  20.3 27.7 %copy-start.3 = (bf16[2,128,544]{2,1,0:T(8,128)(2,1)S(1)}, bf16[2,128,544]{2,1,0:T(8,128)(2,1)}, u32[]{:S(2)}) copy-start(bf16[2,128,544]{2,1,0:T(8,128)(2,1)} %constant.22.clone.there) | copy-start | bytes 835588
  20.4 27.7 %copy-start.4 = (bf16[2,128,512]{2,1,0:T(8,128)(2,1)S(1)}, bf16[2,128,512]{2,1,0:T(8,128)(2,1)}, u32[]{:S(2)}) copy-start(bf16[2,128,512]{2,1,0:T(8,128)(2,1)} %constant.25.clone.back_small) | copy-start | bytes 786436
  20.4 27.7 %copy-start.5 = (bf16[2,128,512]{2,1,0:T(8,128)(2,1)S(1)}, bf16[2,128,512]{2,1,0:T(8,128)(2,1)}, u32[]{:S(2)}) copy-start(bf16[2,128,512]{2,1,0:T(8,128)(2,1)} %constant.24.clone.back) | copy-start | bytes 786436
  20.4 27.7 %copy-start.6 = (f32[2,64,128]{2,1,0:T(8,128)S(1)}, f32[2,64,128]{2,1,0:T(8,128)}, u32[]{:S(2)}) copy-start(f32[2,64,128]{2,1,0:T(8,128)} %constant.26.clone.turn) | copy-start | bytes 196612
  20.4 27.7 %copy-start.9 = (s32[64]{0:T(128)S(1)}, s32[64]{0:T(128)}, u32[]{:S(2)}) copy-start(s32[64]{0:T(128)} %param.16) | copy-start | bytes 772
  50.2 25.3 %all-to-all-start.1 = ((f32[64,16,128]{2,1,0:T(8,128)}), f32[64,16,128]{2,1,0:T(8,128)S(1)}, u32[]{:S(2)}, u32[]{:S(2)}) async-start(f32[64,16,128]{2,1,0:T(8,128)} %bitcast.5), calls=%async_computation.1 | async-start | bytes 1048576 | tf_op jit(solution)/shard_map/all_to_all | solution.py:370
  55.9 14.7 %collective-permute-start.4 = (f32[8,256]{1,0:T(8,128)S(1)}, f32[8,256]{1,0:T(8,128)S(1)}, u32[]{:S(2)}, u32[]{:S(2)}) collective-permute-start(f32[8,256]{1,0:T(8,128)S(1)} %get-tuple-element.16), channel_id=1, source_target_pairs={{0,4},{4,8},{8,12},{12,16},{16,20},{20,24},{24,28},{28,32},{32,36}... | collective-permute-start | bytes 24584 | tf_op jit(solution)/shard_map/ppermute | solution.py:355
  57.0 13.6 %collective-permute-start.5 = (f32[8,256]{1,0:T(8,128)S(1)}, f32[8,256]{1,0:T(8,128)S(1)}, u32[]{:S(2)}, u32[]{:S(2)}) collective-permute-start(f32[8,256]{1,0:T(8,128)S(1)} %get-tuple-element.17), channel_id=1, source_target_pairs={{4,0},{8,4},{12,8},{16,12},{20,16},{24,20},{28,24},{32,28},{36,32}... | collective-permute-start | bytes 24584 | tf_op jit(solution)/shard_map/ppermute | solution.py:356

commit v3 on v2

--- a/solution.py
+++ b/solution.py
@@ -100,7 +100,7 @@
 AZ_ROWS = 64
 
 
-def pack_kernel(state, up, down, to_left, to_right):
+def pack_kernel(flag, state, ht_first, ht_then, az_first, az_then, up, down, to_left, to_right):
     inv_r, half_arc = radial_rates(NR)
     zero = jnp.zeros((1, NR), jnp.float32)
     for out, edge, inside, sign in ((up, HTS - 1, HTS - 2, 1.0), (down, 0, 1, -1.0)):
@@ -123,6 +123,13 @@
         out[32:48] = p - DT * rate
         out[48:64] = v + (DT * sign) * half_arc * state[0, inside]
 
+    for odd, one, two, ahead, behind in (
+        (flag[2] == 1, ht_first, ht_then, up, down),
+        (flag[3] == 1, az_first, az_then, to_right, to_left),
+    ):
+        one[...] = jnp.where(odd, behind[...], ahead[...])
+        two[...] = jnp.where(odd, ahead[...], behind[...])
+
 
 def ground_kernel(resistance, relax, state, zone, aux, ground):
     ids, q = zone[...], aux[...]
@@ -131,6 +138,11 @@
     ground[0] = twice * (p0 - q) - w0
     ground[1] = twice
     ground[2] = q + DT * lookup(ids, relax) * (p0 - q)
+
+
+def unswap(flag, place, first, then, behind, ahead):
+    behind[...] = jnp.where(flag[place] == 1, first[...], then[...])
+    ahead[...] = jnp.where(flag[place] == 1, then[...], first[...])
 
 
 def two_stages(width, flag, state, low, high, left, right, ground, mid, ghost):
@@ -200,7 +212,11 @@
     return (0.5 * DT) * (0.5 * DT) * radial_rates(width)[1]
 
 
-def inner_kernel(flag, state, low, high, left, right, ground, packed, to_left, to_right, mid, ghost):
+def inner_kernel(
+    flag, state, ht_first, ht_then, az_first, az_then, ground, packed, low, high, left, right, to_left, to_right, mid, ghost
+):
+    unswap(flag, 2, ht_first, ht_then, low, high)
+    unswap(flag, 3, az_first, az_then, left, right)
     near = lax.broadcasted_iota(jnp.int32, (HTS, 128), 1) < NI
     height = lax.broadcasted_iota(jnp.int32, (HTS, 128), 0)
     second = two_stages(128, flag, state, low, high, left, right, ground, mid, ghost)
@@ -236,20 +252,13 @@
         out[...] = jnp.concatenate([w_low, w_high, v_low, v_high, jnp.zeros((4, NR), jnp.float32)], 0)
 
 
-def outer_kernel(flag, state, low, high, left, right, ground, left_corner, right_corner, stepped, mid, ghost):
+def outer_kernel(flag, state, low, high, left, right, ground, stepped, mid, ghost):
     second = two_stages(NR, flag, state, low, high, left, right, ground, mid, ghost)
 
     @pl.loop(0, ROWS, unroll=2)
     def _(j):
         for i, value in enumerate(second(j)):
             stepped[i, j] = value
-
-    weight = corner_weight(NR)
-    for j, corner, sign in ((0, left_corner, -1.0), (ROWS - 1, right_corner, 1.0)):
-        for i, k in ((2, 0), (3, 2)):
-            stepped[i, j, 0:1] = stepped[i, j, 0:1] - (sign * weight) * corner[k : k + 1]
-            end = slice(HTS - 1, HTS)
-            stepped[i, j, end] = stepped[i, j, end] + (sign * weight) * corner[k + 1 : k + 2]
 
 
 def filter_kernel(there, there_small, back, back_small, turn, cutoff, x_ref, o_ref):
@@ -278,18 +287,35 @@
     o_ref[n:] = outs[0] - outs[1]
 
 
-def merge_kernel(stepped, back, out, rows, tile, beside, sems):
+def merge_kernel(stepped, back, left_corner, right_corner, out, rows, tile, beside, edges, sems, edge_sems):
     near = lax.broadcasted_iota(jnp.int32, (HTS, 128), 1) < NI
+    height = lax.broadcasted_iota(jnp.int32, (HTS, NR), 0)
     loads = [
         pltpu.make_async_copy(stepped.at[i, :, :, pl.ds(0, 128)], beside.at[i], sems.at[0, i]) for i in range(COMPS)
     ]
-    for copy in loads:
+    places = [(k, i, j) for k, (i, j) in enumerate(((2, 0), (2, ROWS - 1), (3, 0), (3, ROWS - 1)))]
+    edge_loads = [
+        pltpu.make_async_copy(stepped.at[i, j, :, pl.ds(128, 128)], edges.at[k], edge_sems.at[0, k]) for k, i, j in places
+    ]
+    for copy in loads + edge_loads:
         copy.start()
+
+    weight = corner_weight(NR)
+    owed = {}
+    for k, i, j in places:
+        corner, sign = (left_corner, -1.0) if j == 0 else (right_corner, 1.0)
+        at = 2 * (i - 2)
+        below, above = (-sign * weight) * corner[at : at + 1], (sign * weight) * corner[at + 1 : at + 2]
+        owed[i, j] = jnp.where(height == HTS - 1, above, jnp.where(height == 0, below, 0.0))
+
     for i in range(COMPS * HTS):
         rows[pl.ds(i // HTS * HTS * HALF + i % HTS, HALF, stride=HTS), :] = back[i * HALF : (i + 1) * HALF]
     stores = []
     for i in range(COMPS):
         loads[i].wait()
+        for j in (0, ROWS - 1):
+            if i >= 2:
+                beside[i, j] = beside[i, j] + owed[i, j][:, 0:128]
         for l in range(HALF):
             at = (i * HALF + l) * HTS
             both = rows[at : at + HTS]
@@ -297,6 +323,11 @@
             tile[i, l + HALF] = jnp.where(near, pltpu.roll(both, NI, 1), beside[i, l + HALF])
         stores.append(pltpu.make_async_copy(tile.at[i], out.at[i, :, :, pl.ds(0, 128)], sems.at[1, i]))
         stores[i].start()
+    for k, i, j in places:
+        edge_loads[k].wait()
+        edges[k] = edges[k] + owed[i, j][:, 128:NR]
+        stores.append(pltpu.make_async_copy(edges.at[k], out.at[i, j, :, pl.ds(128, 128)], edge_sems.at[1, k]))
+        stores[-1].start()
     for copy in stores:
         copy.wait()
 
@@ -304,7 +335,7 @@
 def per_device(state, zone_id, ground_aux, resistance, relax_rate, cutoff):
     f32 = jnp.float32
     ht = lax.axis_index(HT)
-    flags = jnp.stack([ht == 0, ht == 3]).astype(jnp.int32)
+    flags = jnp.stack([ht == 0, ht == 3, lax.axis_index("core") == 1, lax.axis_index("z") % 2 == 1]).astype(jnp.int32)
 
     vmem = pl.BlockSpec(memory_space=pltpu.VMEM)
     smem = pl.BlockSpec(memory_space=pltpu.SMEM)
@@ -316,13 +347,15 @@
     def shapes(*dims):
         return tuple(jax.ShapeDtypeStruct(d, f32) for d in dims)
 
-    up, down, to_left, to_right = call(
+    ht_message, az_message = (HT_ROWS, NR), (AZ_ROWS, NR)
+    ht_first, ht_then, az_first, az_then = call(
         pack_kernel,
-        out_shape=shapes((HT_ROWS, NR), (HT_ROWS, NR), (AZ_ROWS, NR), (AZ_ROWS, NR)),
-        in_specs=[vmem],
+        out_shape=shapes(ht_message, ht_message, az_message, az_message),
+        in_specs=[smem, vmem],
         out_specs=(vmem,) * 4,
+        scratch_shapes=[pltpu.VMEM(m, f32) for m in (ht_message, ht_message, az_message, az_message)],
         name="pack",
-    )(state)
+    )(flags, state)
     ground = call(
         ground_kernel,
         out_shape=shapes((3, ROWS, NR))[0],
@@ -330,40 +363,45 @@
         out_specs=vmem,
         name="ground",
     )(resistance, relax_rate, state, zone_id, ground_aux)
-    to_next, to_last = [(i, (i + 1) % SECTORS) for i in range(SECTORS)], [((i + 1) % SECTORS, i) for i in range(SECTORS)]
-    low = lax.ppermute(up, HT, [(i, i + 1) for i in range(3)])
-    high = lax.ppermute(down, HT, [(i + 1, i) for i in range(3)])
-    left = lax.ppermute(to_right, AZ, to_next)
-    right = lax.ppermute(to_left, AZ, to_last)
-
-    operands = (flags, state, low, high, left, right, ground)
+    def swap(x, axes, size, start, closed):
+        pairs = [(i % size, (i + 1) % size) for i in range(start, size if closed else size - 1, 2)]
+        return lax.ppermute(x, axes, pairs + [(b, a) for a, b in pairs])
+
+    swaps = (
+        swap(ht_first, HT, 4, 0, False),
+        swap(ht_then, HT, 4, 1, False),
+        swap(az_first, AZ, SECTORS, 0, True),
+        swap(az_then, AZ, SECTORS, 1, True),
+    )
 
     def scratch(width):
         return [pltpu.VMEM((COMPS, ROWS + 2, HTS, width), f32), pltpu.VMEM((8, ROWS, width), f32)]
 
-    packed, to_left, to_right = call(
+    packed, low, high, left, right, to_left, to_right = call(
         inner_kernel,
         mib=12,
-        out_shape=shapes((COMPS * HTS * LONG, 128), (8, NR), (8, NR)),
+        out_shape=shapes(
+            (COMPS * HTS * LONG, 128), ht_message, ht_message, az_message, az_message, (8, NR), (8, NR)
+        ),
         in_specs=[smem] + [vmem] * 6,
-        out_specs=(vmem,) * 3,
+        out_specs=(vmem,) * 7,
         scratch_shapes=scratch(128),
         cost_estimate=pl.CostEstimate(flops=10**7, bytes_accessed=6 * 10**6, transcendentals=0),
         name="inner",
-    )(*operands)
+    )(flags, state, *swaps, ground)
     circle = lax.all_to_all(packed.reshape(SECTORS, LONG, 1, 128), SPREAD, 0, 0, tiled=True)
-    left_corner = lax.ppermute(to_right, AZ, to_next)
-    right_corner = lax.ppermute(to_left, AZ, to_last)
+    left_corner = lax.ppermute(to_right, AZ, [(i, (i + 1) % SECTORS) for i in range(SECTORS)])
+    right_corner = lax.ppermute(to_left, AZ, [((i + 1) % SECTORS, i) for i in range(SECTORS)])
     stepped = call(
         outer_kernel,
         mib=16,
         out_shape=shapes((COMPS, ROWS, HTS, NR))[0],
-        in_specs=[smem] + [vmem] * 8,
+        in_specs=[smem] + [vmem] * 6,
         out_specs=vmem,
         scratch_shapes=scratch(NR),
         cost_estimate=pl.CostEstimate(flops=2 * 10**7, bytes_accessed=2 * 10**7, transcendentals=0),
         name="outer",
-    )(*operands, left_corner, right_corner)
+    )(flags, state, low, high, left, right, ground)
     kept = call(
         filter_kernel, out_shape=shapes((NA // 2, 128))[0], in_specs=[vmem] * 7, out_specs=vmem, name="filter"
     )(*map(jnp.asarray, mode_tables()), cutoff.reshape(1, NI), circle.reshape(SECTORS * LONG, 128))
@@ -371,17 +409,19 @@
     return call(
         merge_kernel,
         out_shape=jax.ShapeDtypeStruct(stepped.shape, f32),
-        in_specs=[anywhere, vmem],
+        in_specs=[anywhere] + [vmem] * 3,
         out_specs=anywhere,
         scratch_shapes=[
             pltpu.VMEM((COMPS * HTS * HALF, 128), f32),
             pltpu.VMEM((COMPS, ROWS, HTS, 128), f32),
             pltpu.VMEM((COMPS, ROWS, HTS, 128), f32),
+            pltpu.VMEM((4, HTS, 128), f32),
             pltpu.SemaphoreType.DMA((2, COMPS)),
+            pltpu.SemaphoreType.DMA((2, 4)),
         ],
         input_output_aliases={0: 0},
         name="merge",
-    )(stepped, back.reshape(COMPS * HTS * HALF, 128))
+    )(stepped, back.reshape(COMPS * HTS * HALF, 128), left_corner, right_corner)
 
 
 def solution(mesh):

time: 78 us -> 74.1 us (0.950)
  the two profiles are of different devices: /device:TPU:1 before, /device:TPU:32 now
where the time goes in v3:
time: 74.1 us; the launch traced here: 73.2 us
  blocking collectives  32.2 us (43%)
  starting transfers between devices  14.6 us (20%)
  Pallas kernels  12.9 us (17%)
  waiting for transfers between devices  10.9 us (15%)
  local copies, waits for them, and re-layouts  2.4 us (3%)
    all_to_all x1, blocking collectives, per_device(): lax.all_to_all(packed.reshape(SECTORS, LONG, 1, 128), SPREAD, 0, 0, tiled...  32.2 us
    all_to_all x1, starting transfers between devices, per_device(): lax.all_to_all(kept.reshape(SECTORS, HALF, 128), SPREAD, 0, 0, tiled=True)  7.8 us
    all_to_all x1, waiting for transfers between devices, per_device(): lax.all_to_all(kept.reshape(SECTORS, HALF, 128), SPREAD, 0, 0, tiled=True)  4.96 us
    pallas_call x1, Pallas kernels, per_device(): call(outer_kernel, mib=16, out_shape=shapes((COMPS, ROWS, HTS, NR))[0], i...  4.8 us
    ppermute x4, starting transfers between devices, swap(): return lax.ppermute(x, axes, pairs + [(b, a) for a, b in pairs])  4.68 us
    ppermute x1, waiting for transfers between devices, per_device(): lax.ppermute(to_right, AZ, [(i, (i + 1) % SECTORS) for i in range(SECTORS)])  3.83 us
    unnamed x24, local copies, waits for them, and re-layouts  2.4 us
    pallas_call x1, Pallas kernels, per_device(): call(inner_kernel, mib=12, out_shape=shapes((COMPS * HTS * LONG, 128), ht...  2.4 us
  transfers between devices with their start and end apart: 7, of which 4 were waited for; matrix products, arithmetic and copies ran while one was open for 0% of the time, Pallas kernels for 7%

profile of v3, /device:TPU:32, one launch (start us, length us, event | category | flops | bytes accessed | tf_op | source)
XLA Modules:
  0.0 73.2 jit_solution(12886266281502668760)
XLA Ops:
  0.0 0.1 add_convert_fusion.flag
  0.1 1.6 %copy-done = f32[4,32,16,256]{3,2,1,0:T(8,128)S(1)} copy-done((f32[4,32,16,256]{3,2,1,0:T(8,128)S(1)}, f32[4,32,16,256]{3,2,1,0:T(8,128)}, u32[]{:S(2)}) %copy-start) | copy-done | bytes 2097176
  1.7 0.8 %pack.1 = (f32[136,256]{1,0:T(8,128)S(1)}, f32[136,256]{1,0:T(8,128)S(1)}, f32[64,256]{1,0:T(8,128)S(1)}, f32[64,256]{1,0:T(8,128)S(1)}) custom-call(s32[4]{0:T(128)S(1)} %add_convert_fusion.flag, f32[4,32,16,256]{3,2,1,0:T(8,128)S(1)} %copy-done), custom_call_target="tpu_custom_call" | custom-call | tf_op jit(solution)/shard_map/pack/pallas_call | solution.py:351
  2.5 0.1 collective-permute-start
  2.6 0.7 collective-permute-start.1
  3.3 1.9 %collective-permute-start.2 = (f32[64,256]{1,0:T(8,128)S(1)}, f32[64,256]{1,0:T(8,128)S(1)}, u32[]{:S(2)}, u32[]{:S(2)}) collective-permute-start(f32[64,256]{1,0:T(8,128)S(1)} %get-tuple-element.18), channel_id=1, source_target_pairs={{0,4},{8,12},{16,20},{24,28},{32,36},{40,44},{48,52},{56,60},{64,6... | collective-permute-start | bytes 196616 | tf_op jit(solution)/shard_map/ppermute | solution.py:368
  5.2 2.0 %collective-permute-start.3 = (f32[64,256]{1,0:T(8,128)S(1)}, f32[64,256]{1,0:T(8,128)S(1)}, u32[]{:S(2)}, u32[]{:S(2)}) collective-permute-start(f32[64,256]{1,0:T(8,128)S(1)} %get-tuple-element.19), channel_id=1, source_target_pairs={{4,8},{12,16},{20,24},{28,32},{36,40},{44,48},{52,56},{60,64},{68,... | collective-permute-start | bytes 196616 | tf_op jit(solution)/shard_map/ppermute | solution.py:368
  7.2 0.7 %copy-done.8 = f32[32,256]{1,0:T(8,128)S(1)} copy-done((f32[32,256]{1,0:T(8,128)S(1)}, f32[32,256]{1,0:T(8,128)}, u32[]{:S(2)}) %copy-start.8) | copy-done | bytes 32792
  8.0 0.6 ground.1
  8.6 0.0 copy-start.2
  8.6 0.0 copy-start.3
  8.6 0.0 copy-start.4
  8.7 0.8 %collective-permute-done.3.az_then = f32[64,256]{1,0:T(8,128)S(1)} collective-permute-done((f32[64,256]{1,0:T(8,128)S(1)}, f32[64,256]{1,0:T(8,128)S(1)}, u32[]{:S(2)}, u32[]{:S(2)}) %collective-permute-start.3) | collective-permute-done | bytes 65568 | tf_op jit(solution)/shard_map/ppermute | solution.py:368
  9.5 2.4 %inner.1 = (f32[1088,128]{1,0:T(8,128)S(1)}, f32[136,256]{1,0:T(8,128)S(1)}, f32[136,256]{1,0:T(8,128)S(1)}, f32[64,256]{1,0:T(8,128)S(1)}, f32[64,256]{1,0:T(8,...) custom-call(s32[4]{0:T(128)S(1)} %add_convert_fusion.flag, f32[4,32,16,256]{3,2,1,0:T(8,128)S(1)} %copy-done.1, ...), custom_call_target="tpu_custom_call" | custom-call | flops 10000000 | bytes 6000000 | tf_op jit(solution)/shard_map/inner/pallas_call | solution.py:380
  11.9 32.2 %all_to_all.10 = f32[64,17,1,128]{3,2,1,0:T(1,128)S(1)} all-to-all(f32[64,17,1,128]{3,2,1,0:T(1,128)S(1)} %bitcast.11), channel_id=1, replica_groups=mesh['y'=4,'x'=2,'z'=8,'hx'=2,'core'=2] {'y','z','x'}, dimensions={0} | all-to-all | bytes 1114112 | tf_op jit(solution)/shard_map/all_to_all | solution.py:392
  44.1 2.1 %filter.1 = f32[1024,128]{1,0:T(8,128)} custom-call(bf16[2,128,544]{2,1,0:T(8,128)(2,1)S(1)} %copy-done.3, bf16[2,128,544]{2,1,0:T(8,128)(2,1)S(1)} %copy-done.2, bf16[2,128,512]{2,1,0:T(8,128)(2,1)S(1)} %copy-done.5, bf16[2,128,512]{2,1,0:T(8,128)(2,1)S(1)} %copy-done.4, f32[2,64,128]{2,1,0:T(8,128)S(1)} %copy-done.6, s32[1,64]{1,0:T(1,128)S(1)} %bitcast.12, ...), custom_call_target="tpu_custom_call" | custom-call | tf_op jit(solution)/shard_map/filter/pallas_call | solution.py:405
  46.2 7.8 %all-to-all-start.1 = ((f32[64,16,128]{2,1,0:T(8,128)}), f32[64,16,128]{2,1,0:T(8,128)S(1)}, u32[]{:S(2)}, u32[]{:S(2)}) async-start(f32[64,16,128]{2,1,0:T(8,128)} %bitcast.7), calls=%async_computation.1 | async-start | bytes 1048576 | tf_op jit(solution)/shard_map/all_to_all | solution.py:408
  54.0 1.5 %collective-permute-start.4 = (f32[8,256]{1,0:T(8,128)S(1)}, f32[8,256]{1,0:T(8,128)S(1)}, u32[]{:S(2)}, u32[]{:S(2)}) collective-permute-start(f32[8,256]{1,0:T(8,128)S(1)} %get-tuple-element.25), channel_id=1, source_target_pairs={{0,4},{4,8},{8,12},{12,16},{16,20},{20,24},{24,28},{28,32},{32,36}... | collective-permute-start | bytes 24584 | tf_op jit(solution)/shard_map/ppermute | solution.py:393
  55.5 0.6 collective-permute-start.5
  56.1 4.8 %outer.1.stepped = f32[4,32,16,256]{3,2,1,0:T(8,128)} custom-call(s32[4]{0:T(128)S(1)} %add_convert_fusion.flag, f32[4,32,16,256]{3,2,1,0:T(8,128)S(1)} %copy-done.1, f32[136,256]{1,0:T(8,128)S(1)} %get-tuple-element.20.low, f32[136,256]{1,0:T(8,128)S(1)} %get-tuple-element.21.high, f32[64,256]{1,0:T(8,128)S(1)} %get-tuple-element.22.left, ...), custom_call_target="tpu_custom_call" | custom-call | flops 20000000 | bytes 20000000 | tf_op jit(solution)/shard_map/outer/pallas_call | solution.py:395
  60.9 3.8 %collective-permute-done.4.left_corner = f32[8,256]{1,0:T(8,128)S(1)} collective-permute-done((f32[8,256]{1,0:T(8,128)S(1)}, f32[8,256]{1,0:T(8,128)S(1)}, u32[]{:S(2)}, u32[]{:S(2)}) %collective-permute-start.4) | collective-permute-done | bytes 8224 | tf_op jit(solution)/shard_map/ppermute | solution.py:393
  64.7 1.3 %collective-permute-done.5.right_corner = f32[8,256]{1,0:T(8,128)S(1)} collective-permute-done((f32[8,256]{1,0:T(8,128)S(1)}, f32[8,256]{1,0:T(8,128)S(1)}, u32[]{:S(2)}, u32[]{:S(2)}) %collective-permute-start.5) | collective-permute-done | bytes 8224 | tf_op jit(solution)/shard_map/ppermute | solution.py:394
  66.1 5.0 %all-to-all-done.1 = f32[64,16,128]{2,1,0:T(8,128)S(1)} async-done(((f32[64,16,128]{2,1,0:T(8,128)}), f32[64,16,128]{2,1,0:T(8,128)S(1)}, u32[]{:S(2)}, u32[]{:S(2)}) %all-to-all-start.1) | async-done | bytes 524320 | tf_op jit(solution)/shard_map/all_to_all | solution.py:408
  71.0 2.2 %merge.1 = f32[4,32,16,256]{3,2,1,0:T(8,128)} custom-call(f32[4,32,16,256]{3,2,1,0:T(8,128)} %outer.1.stepped, f32[1024,128]{1,0:T(8,128)S(1)} %bitcast.10, f32[8,256]{1,0:T(8,128)S(1)} %collective-permute-done.4.left_corner, f32[8,256]{1,0:T(8,128)S(1)} %collective-permute-done.5.right_corner), custom_call_target="tpu_custom_call", output_to_operand_aliasing={{}: (0, {})} | custom-call | tf_op jit(solution)/shard_map/merge/pallas_call | solution.py:409
  (22 shorter events, 0.1 us)
Async XLA Ops:
  0.0 7.2 %copy-start.11 = (f32[8]{0:T(128)S(1)}, f32[8]{0:T(128)}, u32[]{:S(2)}) copy-start(f32[8]{0:T(128)} %relax.1) | copy-start | bytes 100
  0.0 7.2 %copy-start.10 = (f32[8]{0:T(128)S(1)}, f32[8]{0:T(128)}, u32[]{:S(2)}) copy-start(f32[8]{0:T(128)} %resistance.1) | copy-start | bytes 100
  0.0 7.2 %copy-start.7 = (s32[32,256]{1,0:T(8,128)S(1)}, s32[32,256]{1,0:T(8,128)}, u32[]{:S(2)}) copy-start(s32[32,256]{1,0:T(8,128)} %zone.1) | copy-start | bytes 98308
  0.1 1.6 %copy-start = (f32[4,32,16,256]{3,2,1,0:T(8,128)S(1)}, f32[4,32,16,256]{3,2,1,0:T(8,128)}, u32[]{:S(2)}) copy-start(f32[4,32,16,256]{3,2,1,0:T(8,128)} %state.7) | copy-start | bytes 6291460
  1.7 5.5 %copy-start.1 = (f32[4,32,16,256]{3,2,1,0:T(8,128)S(1)}, f32[4,32,16,256]{3,2,1,0:T(8,128)}, u32[]{:S(2)}) copy-start(f32[4,32,16,256]{3,2,1,0:T(8,128)} %state.7) | copy-start | bytes 6291460
  2.5 7.0 %collective-permute-start = (f32[136,256]{1,0:T(8,128)S(1)}, f32[136,256]{1,0:T(8,128)S(1)}, u32[]{:S(2)}, u32[]{:S(2)}) collective-permute-start(f32[136,256]{1,0:T(8,128)S(1)} %get-tuple-element.16), channel_id=1, source_target_pairs={{0,1},{2,3},{1,0},{3,2},{4,5},{6,7},{5,4},{7,6},{8,9},{10,11},{9,8... | collective-permute-start | bytes 417800 | tf_op jit(solution)/shard_map/ppermute | solution.py:368
  2.6 6.9 %collective-permute-start.1 = (f32[136,256]{1,0:T(8,128)S(1)}, f32[136,256]{1,0:T(8,128)S(1)}, u32[]{:S(2)}, u32[]{:S(2)}) collective-permute-start(f32[136,256]{1,0:T(8,128)S(1)} %get-tuple-element.17), channel_id=1, source_target_pairs={{1,2},{2,1},{5,6},{6,5},{9,10},{10,9},{13,14},{14,13},{17,18},{18,... | collective-permute-start | bytes 417800 | tf_op jit(solution)/shard_map/ppermute | solution.py:368
  3.3 5.4 %collective-permute-start.2 = (f32[64,256]{1,0:T(8,128)S(1)}, f32[64,256]{1,0:T(8,128)S(1)}, u32[]{:S(2)}, u32[]{:S(2)}) collective-permute-start(f32[64,256]{1,0:T(8,128)S(1)} %get-tuple-element.18), channel_id=1, source_target_pairs={{0,4},{8,12},{16,20},{24,28},{32,36},{40,44},{48,52},{56,60},{64,6... | collective-permute-start | bytes 196616 | tf_op jit(solution)/shard_map/ppermute | solution.py:368
  5.2 4.3 %collective-permute-start.3 = (f32[64,256]{1,0:T(8,128)S(1)}, f32[64,256]{1,0:T(8,128)S(1)}, u32[]{:S(2)}, u32[]{:S(2)}) collective-permute-start(f32[64,256]{1,0:T(8,128)S(1)} %get-tuple-element.19), channel_id=1, source_target_pairs={{4,8},{12,16},{20,24},{28,32},{36,40},{44,48},{52,56},{60,64},{68,... | collective-permute-start | bytes 196616 | tf_op jit(solution)/shard_map/ppermute | solution.py:368
  7.2 0.8 %copy-start.8 = (f32[32,256]{1,0:T(8,128)S(1)}, f32[32,256]{1,0:T(8,128)}, u32[]{:S(2)}) copy-start(f32[32,256]{1,0:T(8,128)} %aux.1) | copy-start | bytes 98308
  8.6 35.5 %copy-start.2 = (bf16[2,128,544]{2,1,0:T(8,128)(2,1)S(1)}, bf16[2,128,544]{2,1,0:T(8,128)(2,1)}, u32[]{:S(2)}) copy-start(bf16[2,128,544]{2,1,0:T(8,128)(2,1)} %constant.40.clone.there_small) | copy-start | bytes 835588
  8.6 35.5 %copy-start.3 = (bf16[2,128,544]{2,1,0:T(8,128)(2,1)S(1)}, bf16[2,128,544]{2,1,0:T(8,128)(2,1)}, u32[]{:S(2)}) copy-start(bf16[2,128,544]{2,1,0:T(8,128)(2,1)} %constant.39.clone.there) | copy-start | bytes 835588
  8.6 35.4 %copy-start.4 = (bf16[2,128,512]{2,1,0:T(8,128)(2,1)S(1)}, bf16[2,128,512]{2,1,0:T(8,128)(2,1)}, u32[]{:S(2)}) copy-start(bf16[2,128,512]{2,1,0:T(8,128)(2,1)} %constant.42.clone.back_small) | copy-start | bytes 786436
  8.6 35.4 %copy-start.5 = (bf16[2,128,512]{2,1,0:T(8,128)(2,1)S(1)}, bf16[2,128,512]{2,1,0:T(8,128)(2,1)}, u32[]{:S(2)}) copy-start(bf16[2,128,512]{2,1,0:T(8,128)(2,1)} %constant.41.clone.back) | copy-start | bytes 786436
  8.7 35.4 %copy-start.6 = (f32[2,64,128]{2,1,0:T(8,128)S(1)}, f32[2,64,128]{2,1,0:T(8,128)}, u32[]{:S(2)}) copy-start(f32[2,64,128]{2,1,0:T(8,128)} %constant.43.clone.turn) | copy-start | bytes 196612
  8.7 35.4 %copy-start.9 = (s32[64]{0:T(128)S(1)}, s32[64]{0:T(128)}, u32[]{:S(2)}) copy-start(s32[64]{0:T(128)} %param.16) | copy-start | bytes 772
  46.2 24.8 %all-to-all-start.1 = ((f32[64,16,128]{2,1,0:T(8,128)}), f32[64,16,128]{2,1,0:T(8,128)S(1)}, u32[]{:S(2)}, u32[]{:S(2)}) async-start(f32[64,16,128]{2,1,0:T(8,128)} %bitcast.7), calls=%async_computation.1 | async-start | bytes 1048576 | tf_op jit(solution)/shard_map/all_to_all | solution.py:408
  54.0 10.7 %collective-permute-start.4 = (f32[8,256]{1,0:T(8,128)S(1)}, f32[8,256]{1,0:T(8,128)S(1)}, u32[]{:S(2)}, u32[]{:S(2)}) collective-permute-start(f32[8,256]{1,0:T(8,128)S(1)} %get-tuple-element.25), channel_id=1, source_target_pairs={{0,4},{4,8},{8,12},{12,16},{16,20},{20,24},{24,28},{28,32},{32,36}... | collective-permute-start | bytes 24584 | tf_op jit(solution)/shard_map/ppermute | solution.py:393
  55.5 10.5 %collective-permute-start.5 = (f32[8,256]{1,0:T(8,128)S(1)}, f32[8,256]{1,0:T(8,128)S(1)}, u32[]{:S(2)}, u32[]{:S(2)}) collective-permute-start(f32[8,256]{1,0:T(8,128)S(1)} %get-tuple-element.26), channel_id=1, source_target_pairs={{4,0},{8,4},{12,8},{16,12},{20,16},{24,20},{28,24},{32,28},{36,32}... | collective-permute-start | bytes 24584 | tf_op jit(solution)/shard_map/ppermute | solution.py:394

commit v4 on v3

--- a/solution.py
+++ b/solution.py
@@ -96,11 +96,27 @@
     return out
 
 
+def odd_slab():
+    return lax.axis_index("core") == 1
+
+
+def odd_sector():
+    return lax.rem(lax.axis_index("z"), 2) == 1
+
+
+def lowest_slab():
+    return lax.axis_index("hx") * 2 + lax.axis_index("core") == 0
+
+
+def highest_slab():
+    return lax.axis_index("hx") * 2 + lax.axis_index("core") == 3
+
+
 HT_ROWS = 136
 AZ_ROWS = 64
 
 
-def pack_kernel(flag, state, ht_first, ht_then, az_first, az_then, up, down, to_left, to_right):
+def pack_kernel(state, az_then, ht_then, az_first, ht_first, up, down, to_left, to_right):
     inv_r, half_arc = radial_rates(NR)
     zero = jnp.zeros((1, NR), jnp.float32)
     for out, edge, inside, sign in ((up, HTS - 1, HTS - 2, 1.0), (down, 0, 1, -1.0)):
@@ -124,8 +140,8 @@
         out[48:64] = v + (DT * sign) * half_arc * state[0, inside]
 
     for odd, one, two, ahead, behind in (
-        (flag[2] == 1, ht_first, ht_then, up, down),
-        (flag[3] == 1, az_first, az_then, to_right, to_left),
+        (odd_slab(), ht_first, ht_then, up, down),
+        (odd_sector(), az_first, az_then, to_right, to_left),
     ):
         one[...] = jnp.where(odd, behind[...], ahead[...])
         two[...] = jnp.where(odd, ahead[...], behind[...])
@@ -140,13 +156,13 @@
     ground[2] = q + DT * lookup(ids, relax) * (p0 - q)
 
 
-def unswap(flag, place, first, then, behind, ahead):
-    behind[...] = jnp.where(flag[place] == 1, first[...], then[...])
-    ahead[...] = jnp.where(flag[place] == 1, then[...], first[...])
-
-
-def two_stages(width, flag, state, low, high, left, right, ground, mid, ghost):
-    on_ground, on_top = flag[0] == 1, flag[1] == 1
+def unswap(odd, first, then, behind, ahead):
+    behind[...] = jnp.where(odd, first[...], then[...])
+    ahead[...] = jnp.where(odd, then[...], first[...])
+
+
+def two_stages(width, state, low, high, left, right, ground, mid, ghost):
+    on_ground, on_top = lowest_slab(), highest_slab()
     inv_r, half_arc = radial_rates(width)
     cols = slice(0, width)
     turn = DT * half_arc
@@ -213,13 +229,13 @@
 
 
 def inner_kernel(
-    flag, state, ht_first, ht_then, az_first, az_then, ground, packed, low, high, left, right, to_left, to_right, mid, ghost
+    state, az_then, ht_then, az_first, ht_first, ground, packed, low, high, left, right, to_left, to_right, mid, ghost
 ):
-    unswap(flag, 2, ht_first, ht_then, low, high)
-    unswap(flag, 3, az_first, az_then, left, right)
+    unswap(odd_slab(), ht_first, ht_then, low, high)
+    unswap(odd_sector(), az_first, az_then, left, right)
     near = lax.broadcasted_iota(jnp.int32, (HTS, 128), 1) < NI
     height = lax.broadcasted_iota(jnp.int32, (HTS, 128), 0)
-    second = two_stages(128, flag, state, low, high, left, right, ground, mid, ghost)
+    second = two_stages(128, state, low, high, left, right, ground, mid, ghost)
 
     def emit(r, one, two):
         for i in range(COMPS):
@@ -234,7 +250,7 @@
 
     def beyond(row):
         at, end = 32 + row * (ROWS - 1), row * (ROWS - 1)
-        w_low = jnp.where(flag[0] == 1, ground[0, end : end + 1], low[at : at + 1])
+        w_low = jnp.where(lowest_slab(), ground[0, end : end + 1], low[at : at + 1])
         return (w_low, high[at : at + 1]), (low[128 + row : 129 + row], high[128 + row : 129 + row])
 
     def owed(row, sign):
@@ -252,8 +268,8 @@
         out[...] = jnp.concatenate([w_low, w_high, v_low, v_high, jnp.zeros((4, NR), jnp.float32)], 0)
 
 
-def outer_kernel(flag, state, low, high, left, right, ground, stepped, mid, ghost):
-    second = two_stages(NR, flag, state, low, high, left, right, ground, mid, ghost)
+def outer_kernel(state, low, high, left, right, ground, stepped, mid, ghost):
+    second = two_stages(NR, state, low, high, left, right, ground, mid, ghost)
 
     @pl.loop(0, ROWS, unroll=2)
     def _(j):
@@ -334,9 +350,6 @@
 
 def per_device(state, zone_id, ground_aux, resistance, relax_rate, cutoff):
     f32 = jnp.float32
-    ht = lax.axis_index(HT)
-    flags = jnp.stack([ht == 0, ht == 3, lax.axis_index("core") == 1, lax.axis_index("z") % 2 == 1]).astype(jnp.int32)
-
     vmem = pl.BlockSpec(memory_space=pltpu.VMEM)
     smem = pl.BlockSpec(memory_space=pltpu.SMEM)
     anywhere = pl.BlockSpec(memory_space=pl.ANY)
@@ -348,14 +361,14 @@
         return tuple(jax.ShapeDtypeStruct(d, f32) for d in dims)
 
     ht_message, az_message = (HT_ROWS, NR), (AZ_ROWS, NR)
-    ht_first, ht_then, az_first, az_then = call(
+    az_then, ht_then, az_first, ht_first = call(
         pack_kernel,
-        out_shape=shapes(ht_message, ht_message, az_message, az_message),
-        in_specs=[smem, vmem],
+        out_shape=shapes(az_message, ht_message, az_message, ht_message),
+        in_specs=[vmem],
         out_specs=(vmem,) * 4,
         scratch_shapes=[pltpu.VMEM(m, f32) for m in (ht_message, ht_message, az_message, az_message)],
         name="pack",
-    )(flags, state)
+    )(state)
     ground = call(
         ground_kernel,
         out_shape=shapes((3, ROWS, NR))[0],
@@ -367,12 +380,10 @@
         pairs = [(i % size, (i + 1) % size) for i in range(start, size if closed else size - 1, 2)]
         return lax.ppermute(x, axes, pairs + [(b, a) for a, b in pairs])
 
-    swaps = (
-        swap(ht_first, HT, 4, 0, False),
-        swap(ht_then, HT, 4, 1, False),
-        swap(az_first, AZ, SECTORS, 0, True),
-        swap(az_then, AZ, SECTORS, 1, True),
-    )
+    az_then = swap(az_then, AZ, SECTORS, 1, True)
+    ht_then = swap(ht_then, HT, 4, 1, False)
+    az_first = swap(az_first, AZ, SECTORS, 0, True)
+    ht_first = swap(ht_first, HT, 4, 0, False)
 
     def scratch(width):
         return [pltpu.VMEM((COMPS, ROWS + 2, HTS, width), f32), pltpu.VMEM((8, ROWS, width), f32)]
@@ -383,12 +394,12 @@
         out_shape=shapes(
             (COMPS * HTS * LONG, 128), ht_message, ht_message, az_message, az_message, (8, NR), (8, NR)
         ),
-        in_specs=[smem] + [vmem] * 6,
+        in_specs=[vmem] * 6,
         out_specs=(vmem,) * 7,
         scratch_shapes=scratch(128),
         cost_estimate=pl.CostEstimate(flops=10**7, bytes_accessed=6 * 10**6, transcendentals=0),
         name="inner",
-    )(flags, state, *swaps, ground)
+    )(state, az_then, ht_then, az_first, ht_first, ground)
     circle = lax.all_to_all(packed.reshape(SECTORS, LONG, 1, 128), SPREAD, 0, 0, tiled=True)
     left_corner = lax.ppermute(to_right, AZ, [(i, (i + 1) % SECTORS) for i in range(SECTORS)])
     right_corner = lax.ppermute(to_left, AZ, [((i + 1) % SECTORS, i) for i in range(SECTORS)])
@@ -396,12 +407,12 @@
         outer_kernel,
         mib=16,
         out_shape=shapes((COMPS, ROWS, HTS, NR))[0],
-        in_specs=[smem] + [vmem] * 6,
+        in_specs=[vmem] * 6,
         out_specs=vmem,
         scratch_shapes=scratch(NR),
         cost_estimate=pl.CostEstimate(flops=2 * 10**7, bytes_accessed=2 * 10**7, transcendentals=0),
         name="outer",
-    )(flags, state, low, high, left, right, ground)
+    )(state, low, high, left, right, ground)
     kept = call(
         filter_kernel, out_shape=shapes((NA // 2, 128))[0], in_specs=[vmem] * 7, out_specs=vmem, name="filter"
     )(*map(jnp.asarray, mode_tables()), cutoff.reshape(1, NI), circle.reshape(SECTORS * LONG, 128))

time: 74.1 us -> 72.7 us (0.981)
  starting transfers between devices: 14.6 us -> 22.7 us
  blocking collectives: 32.2 us -> 24.5 us
  Pallas kernels: 12.9 us -> 11.3 us
  waiting for transfers between devices: 10.9 us -> 9.48 us
  local copies, waits for them, and re-layouts: 2.4 us -> 3.16 us
    ppermute x4, starting transfers between devices: 4.68 us -> 13.7 us  [swap(): return lax.ppermute(x, axes, pairs + [(b, a) for a, b in pairs])]
    all_to_all x1, blocking collectives: 32.2 us -> 24.5 us  [per_device(): lax.all_to_all(packed.reshape(SECTORS, LONG, 1, 128), SPREAD, 0, 0, tiled...]
    all_to_all x1, starting transfers between devices: 7.8 us -> 6.87 us  [per_device(): lax.all_to_all(kept.reshape(SECTORS, HALF, 128), SPREAD, 0, 0, tiled=True)]
    ppermute x1, waiting for transfers between devices: 3.83 us -> 2.95 us  [per_device(): lax.ppermute(to_right, AZ, [(i, (i + 1) % SECTORS) for i in range(SECTORS)])]
    ppermute x4, waiting for transfers between devices: 0.79 us -> 0.02 us  [swap(): return lax.ppermute(x, axes, pairs + [(b, a) for a, b in pairs])]
    unnamed x24, local copies, waits for them, and re-layouts: 2.4 us -> 3.16 us
  transfers between devices with their start and end apart: 7 -> 7, of which waited for: 4 -> 3; matrix products, arithmetic and copies ran while one was open for 0% -> 0% of each run, Pallas kernels for 7% -> 7%
where the time goes in v4:
time: 72.7 us; the launch traced here: 71.2 us
  blocking collectives  24.5 us (34%)
  starting transfers between devices  22.7 us (31%)
  Pallas kernels  11.3 us (16%)
  waiting for transfers between devices  9.48 us (13%)
  local copies, waits for them, and re-layouts  3.16 us (4%)
    all_to_all x1, blocking collectives, per_device(): lax.all_to_all(packed.reshape(SECTORS, LONG, 1, 128), SPREAD, 0, 0, tiled...  24.5 us
    ppermute x4, starting transfers between devices, swap(): return lax.ppermute(x, axes, pairs + [(b, a) for a, b in pairs])  13.7 us
    all_to_all x1, starting transfers between devices, per_device(): lax.all_to_all(kept.reshape(SECTORS, HALF, 128), SPREAD, 0, 0, tiled=True)  6.87 us
    all_to_all x1, waiting for transfers between devices, per_device(): lax.all_to_all(kept.reshape(SECTORS, HALF, 128), SPREAD, 0, 0, tiled=True)  5.07 us
    pallas_call x1, Pallas kernels, per_device(): call(outer_kernel, mib=16, out_shape=shapes((COMPS, ROWS, HTS, NR))[0], i...  4.28 us
    unnamed x24, local copies, waits for them, and re-layouts  3.16 us
    ppermute x1, waiting for transfers between devices, per_device(): lax.ppermute(to_right, AZ, [(i, (i + 1) % SECTORS) for i in range(SECTORS)])  2.95 us
    pallas_call x1, Pallas kernels, per_device(): call(merge_kernel, out_shape=jax.ShapeDtypeStruct(stepped.shape, f32), in...  2.21 us
  transfers between devices with their start and end apart: 7, of which 3 were waited for; matrix products, arithmetic and copies ran while one was open for 0% of the time, Pallas kernels for 7%

profile of v4, /device:TPU:32, one launch (start us, length us, event | category | flops | bytes accessed | tf_op | source)
XLA Modules:
  0.0 71.2 jit_solution(3705391185298318845)
XLA Ops:
  0.0 1.6 %copy-done = f32[4,32,16,256]{3,2,1,0:T(8,128)S(1)} copy-done((f32[4,32,16,256]{3,2,1,0:T(8,128)S(1)}, f32[4,32,16,256]{3,2,1,0:T(8,128)}, u32[]{:S(2)}) %copy-start) | copy-done | bytes 2097176
  1.6 0.3 pack.1
  1.9 0.8 %collective-permute-start.1 = (f32[136,256]{1,0:T(8,128)S(1)}, f32[136,256]{1,0:T(8,128)S(1)}, u32[]{:S(2)}, u32[]{:S(2)}) collective-permute-start(f32[136,256]{1,0:T(8,128)S(1)} %get-tuple-element.17), channel_id=1, source_target_pairs={{1,2},{2,1},{5,6},{6,5},{9,10},{10,9},{13,14},{14,13},{17,18},{18,... | collective-permute-start | bytes 417800 | tf_op jit(solution)/shard_map/ppermute | solution.py:381
  2.7 4.5 %collective-permute-start.3 = (f32[136,256]{1,0:T(8,128)S(1)}, f32[136,256]{1,0:T(8,128)S(1)}, u32[]{:S(2)}, u32[]{:S(2)}) collective-permute-start(f32[136,256]{1,0:T(8,128)S(1)} %get-tuple-element.19), channel_id=1, source_target_pairs={{0,1},{2,3},{1,0},{3,2},{4,5},{6,7},{5,4},{7,6},{8,9},{10,11},{9,8... | collective-permute-start | bytes 417800 | tf_op jit(solution)/shard_map/ppermute | solution.py:381
  7.2 1.9 %collective-permute-start = (f32[64,256]{1,0:T(8,128)S(1)}, f32[64,256]{1,0:T(8,128)S(1)}, u32[]{:S(2)}, u32[]{:S(2)}) collective-permute-start(f32[64,256]{1,0:T(8,128)S(1)} %get-tuple-element.16), channel_id=1, source_target_pairs={{4,8},{12,16},{20,24},{28,32},{36,40},{44,48},{52,56},{60,64},{68,... | collective-permute-start | bytes 196616 | tf_op jit(solution)/shard_map/ppermute | solution.py:381
  9.1 6.5 %collective-permute-start.2 = (f32[64,256]{1,0:T(8,128)S(1)}, f32[64,256]{1,0:T(8,128)S(1)}, u32[]{:S(2)}, u32[]{:S(2)}) collective-permute-start(f32[64,256]{1,0:T(8,128)S(1)} %get-tuple-element.18), channel_id=1, source_target_pairs={{0,4},{8,12},{16,20},{24,28},{32,36},{40,44},{48,52},{56,60},{64,6... | collective-permute-start | bytes 196616 | tf_op jit(solution)/shard_map/ppermute | solution.py:381
  15.6 0.8 %copy-done.7 = s32[32,256]{1,0:T(8,128)S(1)} copy-done((s32[32,256]{1,0:T(8,128)S(1)}, s32[32,256]{1,0:T(8,128)}, u32[]{:S(2)}) %copy-start.7) | copy-done | bytes 32792
  16.4 0.8 %copy-done.8 = f32[32,256]{1,0:T(8,128)S(1)} copy-done((f32[32,256]{1,0:T(8,128)S(1)}, f32[32,256]{1,0:T(8,128)}, u32[]{:S(2)}) %copy-start.8) | copy-done | bytes 32792
  17.1 0.6 ground.1
  17.7 0.0 copy-start.2
  17.7 0.0 copy-start.3
  17.8 0.0 copy-start.4
  17.8 0.0 collective-permute-done.2.az_first
  17.9 1.9 %inner.1 = (f32[1088,128]{1,0:T(8,128)S(1)}, f32[136,256]{1,0:T(8,128)S(1)}, f32[136,256]{1,0:T(8,128)S(1)}, f32[64,256]{1,0:T(8,128)S(1)}, f32[64,256]{1,0:T(8,...) custom-call(f32[4,32,16,256]{3,2,1,0:T(8,128)S(1)} %copy-done.1, f32[64,256]{1,0:T(8,128)S(1)} %collective-permute-done.az_then, ...), custom_call_target="tpu_custom_call" | custom-call | flops 10000000 | bytes 6000000 | tf_op jit(solution)/shard_map/inner/pallas_call | solution.py:391
  19.7 24.5 %all_to_all.10 = f32[64,17,1,128]{3,2,1,0:T(1,128)S(1)} all-to-all(f32[64,17,1,128]{3,2,1,0:T(1,128)S(1)} %bitcast.7), channel_id=1, replica_groups=mesh['y'=4,'x'=2,'z'=8,'hx'=2,'core'=2] {'y','z','x'}, dimensions={0} | all-to-all | bytes 1114112 | tf_op jit(solution)/shard_map/all_to_all | solution.py:403
  44.2 2.1 %filter.1 = f32[1024,128]{1,0:T(8,128)} custom-call(bf16[2,128,544]{2,1,0:T(8,128)(2,1)S(1)} %copy-done.3, bf16[2,128,544]{2,1,0:T(8,128)(2,1)S(1)} %copy-done.2, bf16[2,128,512]{2,1,0:T(8,128)(2,1)S(1)} %copy-done.5, bf16[2,128,512]{2,1,0:T(8,128)(2,1)S(1)} %copy-done.4, f32[2,64,128]{2,1,0:T(8,128)S(1)} %copy-done.6, s32[1,64]{1,0:T(1,128)S(1)} %bitcast.8, ...), custom_call_target="tpu_custom_call" | custom-call | tf_op jit(solution)/shard_map/filter/pallas_call | solution.py:416
  46.3 6.9 %all-to-all-start.1 = ((f32[64,16,128]{2,1,0:T(8,128)}), f32[64,16,128]{2,1,0:T(8,128)S(1)}, u32[]{:S(2)}, u32[]{:S(2)}) async-start(f32[64,16,128]{2,1,0:T(8,128)} %bitcast.3), calls=%async_computation.1 | async-start | bytes 1048576 | tf_op jit(solution)/shard_map/all_to_all | solution.py:419
  53.2 1.5 %collective-permute-start.4 = (f32[8,256]{1,0:T(8,128)S(1)}, f32[8,256]{1,0:T(8,128)S(1)}, u32[]{:S(2)}, u32[]{:S(2)}) collective-permute-start(f32[8,256]{1,0:T(8,128)S(1)} %get-tuple-element.25), channel_id=1, source_target_pairs={{0,4},{4,8},{8,12},{12,16},{16,20},{20,24},{24,28},{28,32},{32,36}... | collective-permute-start | bytes 24584 | tf_op jit(solution)/shard_map/ppermute | solution.py:404
  54.7 0.6 collective-permute-start.5
  55.3 4.3 %outer.1.stepped = f32[4,32,16,256]{3,2,1,0:T(8,128)} custom-call(f32[4,32,16,256]{3,2,1,0:T(8,128)S(1)} %copy-done.1, f32[136,256]{1,0:T(8,128)S(1)} %get-tuple-element.20.low, f32[136,256]{1,0:T(8,128)S(1)} %get-tuple-element.21.high, f32[64,256]{1,0:T(8,128)S(1)} %get-tuple-element.22.left, f32[64,256]{1,0:T(8,128)S(1)} %get-tuple-element.23.right, ...), custom_call_target="tpu_custom_call" | custom-call | flops 20000000 | bytes 20000000 | tf_op jit(solution)/shard_map/outer/pallas_call | solution.py:406
  59.6 2.9 %collective-permute-done.4.left_corner = f32[8,256]{1,0:T(8,128)S(1)} collective-permute-done((f32[8,256]{1,0:T(8,128)S(1)}, f32[8,256]{1,0:T(8,128)S(1)}, u32[]{:S(2)}, u32[]{:S(2)}) %collective-permute-start.4) | collective-permute-done | bytes 8224 | tf_op jit(solution)/shard_map/ppermute | solution.py:404
  62.5 1.4 %collective-permute-done.5.right_corner = f32[8,256]{1,0:T(8,128)S(1)} collective-permute-done((f32[8,256]{1,0:T(8,128)S(1)}, f32[8,256]{1,0:T(8,128)S(1)}, u32[]{:S(2)}, u32[]{:S(2)}) %collective-permute-start.5) | collective-permute-done | bytes 8224 | tf_op jit(solution)/shard_map/ppermute | solution.py:405
  64.0 5.1 %all-to-all-done.1 = f32[64,16,128]{2,1,0:T(8,128)S(1)} async-done(((f32[64,16,128]{2,1,0:T(8,128)}), f32[64,16,128]{2,1,0:T(8,128)S(1)}, u32[]{:S(2)}, u32[]{:S(2)}) %all-to-all-start.1) | async-done | bytes 524320 | tf_op jit(solution)/shard_map/all_to_all | solution.py:419
  69.0 2.2 %merge.1 = f32[4,32,16,256]{3,2,1,0:T(8,128)} custom-call(f32[4,32,16,256]{3,2,1,0:T(8,128)} %outer.1.stepped, f32[1024,128]{1,0:T(8,128)S(1)} %bitcast.6, f32[8,256]{1,0:T(8,128)S(1)} %collective-permute-done.4.left_corner, f32[8,256]{1,0:T(8,128)S(1)} %collective-permute-done.5.right_corner), custom_call_target="tpu_custom_call", output_to_operand_aliasing={{}: (0, {})} | custom-call | tf_op jit(solution)/shard_map/merge/pallas_call | solution.py:420
  (21 shorter events, 0.0 us)
Async XLA Ops:
  0.0 1.6 %copy-start = (f32[4,32,16,256]{3,2,1,0:T(8,128)S(1)}, f32[4,32,16,256]{3,2,1,0:T(8,128)}, u32[]{:S(2)}) copy-start(f32[4,32,16,256]{3,2,1,0:T(8,128)} %state.7) | copy-start | bytes 6291460
  1.6 14.0 %copy-start.10 = (f32[8]{0:T(128)S(1)}, f32[8]{0:T(128)}, u32[]{:S(2)}) copy-start(f32[8]{0:T(128)} %resistance.1) | copy-start | bytes 100
  1.6 14.0 %copy-start.11 = (f32[8]{0:T(128)S(1)}, f32[8]{0:T(128)}, u32[]{:S(2)}) copy-start(f32[8]{0:T(128)} %relax.1) | copy-start | bytes 100
  1.6 16.3 %copy-start.1 = (f32[4,32,16,256]{3,2,1,0:T(8,128)S(1)}, f32[4,32,16,256]{3,2,1,0:T(8,128)}, u32[]{:S(2)}) copy-start(f32[4,32,16,256]{3,2,1,0:T(8,128)} %state.7) | copy-start | bytes 6291460
  1.9 16.0 %collective-permute-start.1 = (f32[136,256]{1,0:T(8,128)S(1)}, f32[136,256]{1,0:T(8,128)S(1)}, u32[]{:S(2)}, u32[]{:S(2)}) collective-permute-start(f32[136,256]{1,0:T(8,128)S(1)} %get-tuple-element.17), channel_id=1, source_target_pairs={{1,2},{2,1},{5,6},{6,5},{9,10},{10,9},{13,14},{14,13},{17,18},{18,... | collective-permute-start | bytes 417800 | tf_op jit(solution)/shard_map/ppermute | solution.py:381
  2.7 15.2 %collective-permute-start.3 = (f32[136,256]{1,0:T(8,128)S(1)}, f32[136,256]{1,0:T(8,128)S(1)}, u32[]{:S(2)}, u32[]{:S(2)}) collective-permute-start(f32[136,256]{1,0:T(8,128)S(1)} %get-tuple-element.19), channel_id=1, source_target_pairs={{0,1},{2,3},{1,0},{3,2},{4,5},{6,7},{5,4},{7,6},{8,9},{10,11},{9,8... | collective-permute-start | bytes 417800 | tf_op jit(solution)/shard_map/ppermute | solution.py:381
  7.2 10.7 %collective-permute-start = (f32[64,256]{1,0:T(8,128)S(1)}, f32[64,256]{1,0:T(8,128)S(1)}, u32[]{:S(2)}, u32[]{:S(2)}) collective-permute-start(f32[64,256]{1,0:T(8,128)S(1)} %get-tuple-element.16), channel_id=1, source_target_pairs={{4,8},{12,16},{20,24},{28,32},{36,40},{44,48},{52,56},{60,64},{68,... | collective-permute-start | bytes 196616 | tf_op jit(solution)/shard_map/ppermute | solution.py:381
  9.1 8.8 %collective-permute-start.2 = (f32[64,256]{1,0:T(8,128)S(1)}, f32[64,256]{1,0:T(8,128)S(1)}, u32[]{:S(2)}, u32[]{:S(2)}) collective-permute-start(f32[64,256]{1,0:T(8,128)S(1)} %get-tuple-element.18), channel_id=1, source_target_pairs={{0,4},{8,12},{16,20},{24,28},{32,36},{40,44},{48,52},{56,60},{64,6... | collective-permute-start | bytes 196616 | tf_op jit(solution)/shard_map/ppermute | solution.py:381
  15.6 0.8 %copy-start.7 = (s32[32,256]{1,0:T(8,128)S(1)}, s32[32,256]{1,0:T(8,128)}, u32[]{:S(2)}) copy-start(s32[32,256]{1,0:T(8,128)} %zone.1) | copy-start | bytes 98308
  16.4 0.8 %copy-start.8 = (f32[32,256]{1,0:T(8,128)S(1)}, f32[32,256]{1,0:T(8,128)}, u32[]{:S(2)}) copy-start(f32[32,256]{1,0:T(8,128)} %aux.1) | copy-start | bytes 98308
  17.7 26.5 %copy-start.2 = (bf16[2,128,544]{2,1,0:T(8,128)(2,1)S(1)}, bf16[2,128,544]{2,1,0:T(8,128)(2,1)}, u32[]{:S(2)}) copy-start(bf16[2,128,544]{2,1,0:T(8,128)(2,1)} %constant.11.clone.there_small) | copy-start | bytes 835588
  17.7 26.5 %copy-start.3 = (bf16[2,128,544]{2,1,0:T(8,128)(2,1)S(1)}, bf16[2,128,544]{2,1,0:T(8,128)(2,1)}, u32[]{:S(2)}) copy-start(bf16[2,128,544]{2,1,0:T(8,128)(2,1)} %constant.10.clone.there) | copy-start | bytes 835588
  17.8 26.4 %copy-start.4 = (bf16[2,128,512]{2,1,0:T(8,128)(2,1)S(1)}, bf16[2,128,512]{2,1,0:T(8,128)(2,1)}, u32[]{:S(2)}) copy-start(bf16[2,128,512]{2,1,0:T(8,128)(2,1)} %constant.13.clone.back_small) | copy-start | bytes 786436
  17.8 26.4 %copy-start.5 = (bf16[2,128,512]{2,1,0:T(8,128)(2,1)S(1)}, bf16[2,128,512]{2,1,0:T(8,128)(2,1)}, u32[]{:S(2)}) copy-start(bf16[2,128,512]{2,1,0:T(8,128)(2,1)} %constant.12.clone.back) | copy-start | bytes 786436
  17.8 26.4 %copy-start.6 = (f32[2,64,128]{2,1,0:T(8,128)S(1)}, f32[2,64,128]{2,1,0:T(8,128)}, u32[]{:S(2)}) copy-start(f32[2,64,128]{2,1,0:T(8,128)} %constant.14.clone.turn) | copy-start | bytes 196612
  17.8 26.4 %copy-start.9 = (s32[64]{0:T(128)S(1)}, s32[64]{0:T(128)}, u32[]{:S(2)}) copy-start(s32[64]{0:T(128)} %param.16) | copy-start | bytes 772
  46.3 22.7 %all-to-all-start.1 = ((f32[64,16,128]{2,1,0:T(8,128)}), f32[64,16,128]{2,1,0:T(8,128)S(1)}, u32[]{:S(2)}, u32[]{:S(2)}) async-start(f32[64,16,128]{2,1,0:T(8,128)} %bitcast.3), calls=%async_computation.1 | async-start | bytes 1048576 | tf_op jit(solution)/shard_map/all_to_all | solution.py:419
  53.2 9.3 %collective-permute-start.4 = (f32[8,256]{1,0:T(8,128)S(1)}, f32[8,256]{1,0:T(8,128)S(1)}, u32[]{:S(2)}, u32[]{:S(2)}) collective-permute-start(f32[8,256]{1,0:T(8,128)S(1)} %get-tuple-element.25), channel_id=1, source_target_pairs={{0,4},{4,8},{8,12},{12,16},{16,20},{20,24},{24,28},{28,32},{32,36}... | collective-permute-start | bytes 24584 | tf_op jit(solution)/shard_map/ppermute | solution.py:404
  54.7 9.2 %collective-permute-start.5 = (f32[8,256]{1,0:T(8,128)S(1)}, f32[8,256]{1,0:T(8,128)S(1)}, u32[]{:S(2)}, u32[]{:S(2)}) collective-permute-start(f32[8,256]{1,0:T(8,128)S(1)} %get-tuple-element.26), channel_id=1, source_target_pairs={{4,0},{8,4},{12,8},{16,12},{20,16},{24,20},{28,24},{32,28},{36,32}... | collective-permute-start | bytes 24584 | tf_op jit(solution)/shard_map/ppermute | solution.py:405

commit v5 on v4

--- a/solution.py
+++ b/solution.py
@@ -23,35 +23,33 @@
 DT = 0.4
 
 AZ = ("y", "x", "z")
-SPREAD = ("y", "z", "x")
+SPREAD = ("z", "y")
+PEERS = 32
+SETS = COMPS * HTS // PEERS
 HT = ("hx", "core")
 
 
-def sector_of_chunk():
-    y, z, x = np.meshgrid(np.arange(4), np.arange(8), np.arange(2), indexing="ij")
-    return ((y * 2 + x) * 8 + z).reshape(-1)
-
-
 def mode_tables():
-    first = sector_of_chunk()[: SECTORS // 2, None] * ROWS
+    z, y = np.meshgrid(np.arange(8), np.arange(2), indexing="ij")
+    first = (y * 16 + z).reshape(-1, 1) * ROWS
     there = (first - 1 + np.arange(LONG)[None, :]).reshape(-1)
     back = (first + np.arange(HALF)[None, :]).reshape(-1)
-    tables = []
+    tables, turns = [], np.zeros((2, 2, MODES // 2, 128), np.float32)
     for parity in range(2):
         modes = np.arange(parity, MODES, 2)
         waves = []
         for azimuth in (there, back):
             phase = (modes[:, None] * azimuth[None, :] % NA) * (2.0 * math.pi / NA)
             waves.append(np.concatenate([np.cos(phase), np.sin(phase)], 0))
-        more = np.zeros((MODES // 2, 128))
-        for k, by in enumerate((LONG, HALF)):
-            turn = (modes * by % NA) * (2.0 * math.pi / NA)
-            more[:, 2 * k] = np.cos(turn)
-            more[:, 2 * k + 1] = np.sin(turn)
-        more[:, 4] = np.where(modes == 0, 1.0, 2.0) / NA
-        tables.append((*waves, more))
-    there, back, turns = [np.stack(t).astype(np.float32) for t in zip(*tables)]
-    return (*split(there), *split(back), turns)
+        for x in range(2):
+            for k, by in enumerate((0, LONG, 0, HALF)):
+                turn = (modes * (by + x * 8 * ROWS) % NA) * (2.0 * math.pi / NA)
+                turns[x, parity, :, 2 * k] = np.cos(turn)
+                turns[x, parity, :, 2 * k + 1] = np.sin(turn)
+            turns[x, parity, :, 8] = np.where(modes == 0, 1.0, 2.0) / NA
+        tables.append(waves)
+    there, back = [np.stack(t).astype(np.float32) for t in zip(*tables)]
+    return split(there), split(back), turns
 
 
 def split(x):
@@ -114,6 +112,7 @@
 
 HT_ROWS = 136
 AZ_ROWS = 64
+AZ_LONG = 144
 
 
 def pack_kernel(state, az_then, ht_then, az_first, ht_first, up, down, to_left, to_right):
@@ -141,10 +140,11 @@
 
     for odd, one, two, ahead, behind in (
         (odd_slab(), ht_first, ht_then, up, down),
-        (odd_sector(), az_first, az_then, to_right, to_left),
+        (odd_sector(), az_first, az_then.at[0:AZ_ROWS], to_right, to_left),
     ):
         one[...] = jnp.where(odd, behind[...], ahead[...])
         two[...] = jnp.where(odd, ahead[...], behind[...])
+    az_then[AZ_ROWS:AZ_LONG] = jnp.zeros((AZ_LONG - AZ_ROWS, NR), jnp.float32)
 
 
 def ground_kernel(resistance, relax, state, zone, aux, ground):
@@ -232,7 +232,7 @@
     state, az_then, ht_then, az_first, ht_first, ground, packed, low, high, left, right, to_left, to_right, mid, ghost
 ):
     unswap(odd_slab(), ht_first, ht_then, low, high)
-    unswap(odd_sector(), az_first, az_then, left, right)
+    unswap(odd_sector(), az_first, az_then.at[0:AZ_ROWS], left, right)
     near = lax.broadcasted_iota(jnp.int32, (HTS, 128), 1) < NI
     height = lax.broadcasted_iota(jnp.int32, (HTS, 128), 0)
     second = two_stages(128, state, low, high, left, right, ground, mid, ghost)
@@ -277,30 +277,63 @@
             stepped[i, j] = value
 
 
-def filter_kernel(there, there_small, back, back_small, turn, cutoff, x_ref, o_ref):
-    n, m = NA // 4, SECTORS // 2 * LONG
-    first, second = x_ref[:m], x_ref[m:]
+def turns_of(turn, x, parity, way):
+    near = lax.broadcasted_iota(jnp.int32, (MODES // 2, 128), 1) < NI
+    return [
+        jnp.where(near, turn[x, parity, :, k : k + 1], turn[x, parity, :, k + 2 : k + 3])
+        for k in (4 * way, 4 * way + 1)
+    ]
+
+
+def analysis_kernel(wave, wave_small, turn, circle, sums, folded):
+    for z in range(8):
+        for y in range(2):
+            for q in range(SETS):
+                one, two = [circle[pl.ds(((4 * z + k) * SETS + q) * LONG, LONG), :] for k in (y, y + 2)]
+                at = pl.ds((2 * z + y) * LONG, LONG)
+                folded[0, q, at, :] = one + two
+                folded[1, q, at, :] = one - two
+    x = lax.axis_index("x")
+    h = MODES // 2
+    near = lax.broadcasted_iota(jnp.int32, (h, 128), 1) < NI
+    for parity in range(2):
+        cs, sn = turns_of(turn, x, parity, 0)
+        found = []
+        for q in range(SETS):
+            coef = product((wave[parity], wave_small[parity]), split(folded[parity, q]), ((1,), (0,)))
+            a, b = coef[:h], coef[h:]
+            found.append([t + pltpu.roll(t, NI, 1) for t in (a * cs - b * sn, a * sn + b * cs)])
+        for k in range(2):
+            at = (2 * parity + k) * h
+            sums[at : at + h] = jnp.where(near, found[0][k], found[1][k])
+
+
+def synthesis_kernel(wave, wave_small, turn, cutoff, mine, other, out):
+    x = lax.axis_index("x")
     h = MODES // 2
     mode = lax.broadcasted_iota(jnp.int32, (h, 128), 0) * 2
     near = lax.broadcasted_iota(jnp.int32, (h, 128), 1) < NI
     limit = jnp.concatenate([cutoff[...], cutoff[...]], 1)
-    outs = []
+    parts = []
     for parity in range(2):
-        folded = first + second if parity == 0 else first - second
-        cs, sn, cs_back, sn_back, weight = [turn[parity, :, k : k + 1] for k in range(5)]
-        coef = product((there[parity], there_small[parity]), split(folded), ((1,), (0,)))
-        a, b = coef[:h], coef[h:]
-        a_all = jnp.where(near, a, a * cs - b * sn)
-        b_all = jnp.where(near, b, a * sn + b * cs)
-        keep = jnp.where(mode + parity < limit, weight, 0.0)
-        a_all = (a_all + pltpu.roll(a_all, NI, 1)) * keep
-        b_all = (b_all + pltpu.roll(b_all, NI, 1)) * keep
-        a_back = jnp.where(near, a_all, a_all * cs_back + b_all * sn_back)
-        b_back = jnp.where(near, b_all, b_all * cs_back - a_all * sn_back)
-        both = jnp.concatenate([a_back, b_back], 0)
-        outs.append(product((back[parity], back_small[parity]), split(both), ((0,), (0,))))
-    o_ref[:n] = outs[0] + outs[1]
-    o_ref[n:] = outs[0] - outs[1]
+        cs, sn = turns_of(turn, x, parity, 1)
+        keep = jnp.where(mode + parity < limit, turn[x, parity, :, 8:9], 0.0)
+        a, b = [
+            (mine[at : at + h] + other[at : at + h]) * keep for at in (2 * parity * h, (2 * parity + 1) * h)
+        ]
+        a_far, b_far = pltpu.roll(a, NI, 1), pltpu.roll(b, NI, 1)
+        for q in range(SETS):
+            a_all, b_all = [jnp.where(near == (q == 0), t, far) for t, far in ((a, a_far), (b, b_far))]
+            both = jnp.concatenate([a_all * cs + b_all * sn, b_all * cs - a_all * sn], 0)
+            parts.append(product((wave[parity], wave_small[parity]), split(both), ((0,), (0,))))
+    for q in range(SETS):
+        even, odd = parts[q], parts[SETS + q]
+        for z in range(8):
+            for y in range(2):
+                at = slice((2 * z + y) * HALF, (2 * z + y + 1) * HALF)
+                for k, value in ((y, even[at] + odd[at]), (y + 2, even[at] - odd[at])):
+                    to = ((4 * z + k) * SETS + q) * HALF
+                    out[to : to + HALF] = value
 
 
 def merge_kernel(stepped, back, left_corner, right_corner, out, rows, tile, beside, edges, sems, edge_sems):
@@ -363,7 +396,7 @@
     ht_message, az_message = (HT_ROWS, NR), (AZ_ROWS, NR)
     az_then, ht_then, az_first, ht_first = call(
         pack_kernel,
-        out_shape=shapes(az_message, ht_message, az_message, ht_message),
+        out_shape=shapes((AZ_LONG, NR), ht_message, az_message, ht_message),
         in_specs=[vmem],
         out_specs=(vmem,) * 4,
         scratch_shapes=[pltpu.VMEM(m, f32) for m in (ht_message, ht_message, az_message, az_message)],
@@ -400,7 +433,7 @@
         cost_estimate=pl.CostEstimate(flops=10**7, bytes_accessed=6 * 10**6, transcendentals=0),
         name="inner",
     )(state, az_then, ht_then, az_first, ht_first, ground)
-    circle = lax.all_to_all(packed.reshape(SECTORS, LONG, 1, 128), SPREAD, 0, 0, tiled=True)
+    circle = lax.all_to_all(packed.reshape(PEERS, SETS * LONG, 1, 128), SPREAD, 0, 0, tiled=True)
     left_corner = lax.ppermute(to_right, AZ, [(i, (i + 1) % SECTORS) for i in range(SECTORS)])
     right_corner = lax.ppermute(to_left, AZ, [((i + 1) % SECTORS, i) for i in range(SECTORS)])
     stepped = call(
@@ -413,10 +446,24 @@
         cost_estimate=pl.CostEstimate(flops=2 * 10**7, bytes_accessed=2 * 10**7, transcendentals=0),
         name="outer",
     )(state, low, high, left, right, ground)
+    there, back, turns = jax.tree.map(jnp.asarray, mode_tables())
+    sums = call(
+        analysis_kernel,
+        out_shape=shapes((2 * MODES, 128))[0],
+        in_specs=[vmem] * 4,
+        out_specs=vmem,
+        scratch_shapes=[pltpu.VMEM((2, SETS, PEERS // 2 * LONG, 128), f32)],
+        name="analysis",
+    )(*there, turns, circle.reshape(PEERS * SETS * LONG, 128))
+    other = lax.ppermute(sums, "x", [(0, 1), (1, 0)])
     kept = call(
-        filter_kernel, out_shape=shapes((NA // 2, 128))[0], in_specs=[vmem] * 7, out_specs=vmem, name="filter"
-    )(*map(jnp.asarray, mode_tables()), cutoff.reshape(1, NI), circle.reshape(SECTORS * LONG, 128))
-    back = lax.all_to_all(kept.reshape(SECTORS, HALF, 128), SPREAD, 0, 0, tiled=True)
+        synthesis_kernel,
+        out_shape=shapes((PEERS * SETS * HALF, 128))[0],
+        in_specs=[vmem] * 6,
+        out_specs=vmem,
+        name="synthesis",
+    )(*back, turns, cutoff.reshape(1, NI), sums, other)
+    back = lax.all_to_all(kept.reshape(PEERS, SETS * HALF, 128), SPREAD, 0, 0, tiled=True)
     return call(
         merge_kernel,
         out_shape=jax.ShapeDtypeStruct(stepped.shape, f32),

time: 72.7 us -> 73.2 us (level); the launches traced: 71.2 us -> 72.7 us
  waiting for transfers between devices: 9.48 us -> 13.8 us
  blocking collectives: 24.5 us -> 22.4 us
    ppermute x0 -> x1, waiting for transfers between devices: none -> 4.62 us  [per_device(): other = lax.ppermute(sums, 'x', [(0, 1), (1, 0)])]
    all_to_all x1, blocking collectives: 24.5 us -> 22.4 us  [per_device(): lax.all_to_all(packed.reshape(PEERS, SETS * LONG, 1, 128), SPREAD, 0, 0,...]
    all_to_all x1, starting transfers between devices: 6.87 us -> 5.26 us  [per_device(): lax.all_to_all(kept.reshape(PEERS, SETS * HALF, 128), SPREAD, 0, 0, tiled...]
    ppermute x1, waiting for transfers between devices: 2.95 us -> 2.04 us  [per_device(): lax.ppermute(to_right, AZ, [(i, (i + 1) % SECTORS) for i in range(SECTORS)])]
    pallas_call x2 -> x3, Pallas kernels: 2.35 us -> 2.26 us  [the longest x1 1.42 us: per_device(): call(synthesis_kernel, out_shape=shapes((PEERS * SETS * HALF, 128))[0], i...]
  transfers between devices with their start and end apart: 7 -> 8, of which waited for: 3 -> 5; matrix products, arithmetic and copies ran while one was open for 0% -> 0% of each run, Pallas kernels for 7% -> 7%
where the time goes in v5:
time: 73.2 us; the launch traced here: 72.7 us
  blocking collectives  22.4 us (31%)
  starting transfers between devices  22.1 us (30%)
  waiting for transfers between devices  13.8 us (19%)
  Pallas kernels  11.2 us (15%)
  local copies, waits for them, and re-layouts  3.16 us (4%)
    all_to_all x1, blocking collectives, per_device(): lax.all_to_all(packed.reshape(PEERS, SETS * LONG, 1, 128), SPREAD, 0, 0,...  22.4 us
    ppermute x4, starting transfers between devices, swap(): return lax.ppermute(x, axes, pairs + [(b, a) for a, b in pairs])  14.3 us
    all_to_all x1, starting transfers between devices, per_device(): lax.all_to_all(kept.reshape(PEERS, SETS * HALF, 128), SPREAD, 0, 0, tiled...  5.26 us
    all_to_all x1, waiting for transfers between devices, per_device(): lax.all_to_all(kept.reshape(PEERS, SETS * HALF, 128), SPREAD, 0, 0, tiled...  5.24 us
    ppermute x1, waiting for transfers between devices, per_device(): other = lax.ppermute(sums, 'x', [(0, 1), (1, 0)])  4.62 us
    pallas_call x1, Pallas kernels, per_device(): call(outer_kernel, mib=16, out_shape=shapes((COMPS, ROWS, HTS, NR))[0], i...  4.28 us
    unnamed x24, local copies, waits for them, and re-layouts  3.16 us
    pallas_call x1, Pallas kernels, per_device(): call(merge_kernel, out_shape=jax.ShapeDtypeStruct(stepped.shape, f32), in...  2.21 us
  transfers between devices with their start and end apart: 8, of which 5 were waited for; matrix products, arithmetic and copies ran while one was open for 0% of the time, Pallas kernels for 7%

profile of v5, /device:TPU:32, one launch (start us, length us, event | category | flops | bytes accessed | tf_op | source)
XLA Modules:
  0.0 72.7 jit_solution(16103373395079903738)
XLA Ops:
  0.0 1.6 %copy-done = f32[4,32,16,256]{3,2,1,0:T(8,128)S(1)} copy-done((f32[4,32,16,256]{3,2,1,0:T(8,128)S(1)}, f32[4,32,16,256]{3,2,1,0:T(8,128)}, u32[]{:S(2)}) %copy-start) | copy-done | bytes 2097176
  1.6 0.3 pack.1
  1.9 2.0 %collective-permute-start = (f32[144,256]{1,0:T(8,128)S(1)}, f32[144,256]{1,0:T(8,128)S(1)}, u32[]{:S(2)}, u32[]{:S(2)}) collective-permute-start(f32[144,256]{1,0:T(8,128)S(1)} %get-tuple-element.16), channel_id=1, source_target_pairs={{4,8},{12,16},{20,24},{28,32},{36,40},{44,48},{52,56},{60,64},{68,... | collective-permute-start | bytes 442376 | tf_op jit(solution)/shard_map/ppermute | solution.py:414
  3.9 0.7 collective-permute-start.1
  4.5 4.5 %collective-permute-start.3 = (f32[136,256]{1,0:T(8,128)S(1)}, f32[136,256]{1,0:T(8,128)S(1)}, u32[]{:S(2)}, u32[]{:S(2)}) collective-permute-start(f32[136,256]{1,0:T(8,128)S(1)} %get-tuple-element.19), channel_id=1, source_target_pairs={{0,1},{2,3},{1,0},{3,2},{4,5},{6,7},{5,4},{7,6},{8,9},{10,11},{9,8... | collective-permute-start | bytes 417800 | tf_op jit(solution)/shard_map/ppermute | solution.py:414
  9.0 7.1 %collective-permute-start.2 = (f32[64,256]{1,0:T(8,128)S(1)}, f32[64,256]{1,0:T(8,128)S(1)}, u32[]{:S(2)}, u32[]{:S(2)}) collective-permute-start(f32[64,256]{1,0:T(8,128)S(1)} %get-tuple-element.18), channel_id=1, source_target_pairs={{0,4},{8,12},{16,20},{24,28},{32,36},{40,44},{48,52},{56,60},{64,6... | collective-permute-start | bytes 196616 | tf_op jit(solution)/shard_map/ppermute | solution.py:414
  16.2 0.8 %copy-done.7 = s32[32,256]{1,0:T(8,128)S(1)} copy-done((s32[32,256]{1,0:T(8,128)S(1)}, s32[32,256]{1,0:T(8,128)}, u32[]{:S(2)}) %copy-start.7) | copy-done | bytes 32792
  16.9 0.8 %copy-done.8 = f32[32,256]{1,0:T(8,128)S(1)} copy-done((f32[32,256]{1,0:T(8,128)S(1)}, f32[32,256]{1,0:T(8,128)}, u32[]{:S(2)}) %copy-start.8) | copy-done | bytes 32792
  17.7 0.6 ground.1
  18.4 0.1 collective-permute-done.2.az_first
  18.5 1.9 %inner.1 = (f32[1088,128]{1,0:T(8,128)S(1)}, f32[136,256]{1,0:T(8,128)S(1)}, f32[136,256]{1,0:T(8,128)S(1)}, f32[64,256]{1,0:T(8,128)S(1)}, f32[64,256]{1,0:T(8,...) custom-call(f32[4,32,16,256]{3,2,1,0:T(8,128)S(1)} %copy-done.1, f32[144,256]{1,0:T(8,128)S(1)} %collective-permute-done.az_then, ...), custom_call_target="tpu_custom_call" | custom-call | flops 10000000 | bytes 6000000 | tf_op jit(solution)/shard_map/inner/pallas_call | solution.py:424
  20.4 22.4 %all_to_all.10 = f32[32,34,1,128]{3,2,1,0:T(1,128)S(1)} all-to-all(f32[32,34,1,128]{3,2,1,0:T(1,128)S(1)} %bitcast.7), channel_id=1, replica_groups=mesh['y'=4,'x'=2,'z'=8,'hx'=2,'core'=2] {'z','y'}, dimensions={0} | all-to-all | bytes 1114112 | tf_op jit(solution)/shard_map/all_to_all | solution.py:436
  42.8 0.6 analysis.1.mine
  43.3 0.4 collective-permute-start.4
  43.8 4.6 %collective-permute-done.4.other = f32[256,128]{1,0:T(8,128)S(1)} collective-permute-done((f32[256,128]{1,0:T(8,128)S(1)}, f32[256,128]{1,0:T(8,128)S(1)}, u32[]{:S(2)}, u32[]{:S(2)}) %collective-permute-start.4) | collective-permute-done | bytes 131104 | tf_op jit(solution)/shard_map/ppermute | solution.py:458
  48.4 1.4 %synthesis.1 = f32[1024,128]{1,0:T(8,128)} custom-call(bf16[2,128,256]{2,1,0:T(8,128)(2,1)S(1)} %copy-done.6, bf16[2,128,256]{2,1,0:T(8,128)(2,1)S(1)} %copy-done.5, f32[2,2,64,128]{3,2,1,0:T(8,128)S(1)} %copy-done.2, s32[1,64]{1,0:T(1,128)S(1)} %bitcast.8, f32[256,128]{1,0:T(8,128)S(1)} %analysis.1.mine, f32[256,128]{1,0:T(8,128)S(1)} %collective-permute-done.4.other), custom_call_target="tpu_custom_call" | custom-call | tf_op jit(solution)/shard_map/synthesis/pallas_call | solution.py:459
  49.8 5.3 %all-to-all-start.1 = ((f32[32,32,128]{2,1,0:T(8,128)}), f32[32,32,128]{2,1,0:T(8,128)S(1)}, u32[]{:S(2)}, u32[]{:S(2)}) async-start(f32[32,32,128]{2,1,0:T(8,128)} %bitcast.3), calls=%async_computation.1 | async-start | bytes 1048576 | tf_op jit(solution)/shard_map/all_to_all | solution.py:466
  55.1 1.5 %collective-permute-start.5 = (f32[8,256]{1,0:T(8,128)S(1)}, f32[8,256]{1,0:T(8,128)S(1)}, u32[]{:S(2)}, u32[]{:S(2)}) collective-permute-start(f32[8,256]{1,0:T(8,128)S(1)} %get-tuple-element.25), channel_id=1, source_target_pairs={{0,4},{4,8},{8,12},{12,16},{16,20},{20,24},{24,28},{28,32},{32,36}... | collective-permute-start | bytes 24584 | tf_op jit(solution)/shard_map/ppermute | solution.py:437
  56.6 0.6 collective-permute-start.6
  57.2 4.3 %outer.1.stepped = f32[4,32,16,256]{3,2,1,0:T(8,128)} custom-call(f32[4,32,16,256]{3,2,1,0:T(8,128)S(1)} %copy-done.1, f32[136,256]{1,0:T(8,128)S(1)} %get-tuple-element.20.low, f32[136,256]{1,0:T(8,128)S(1)} %get-tuple-element.21.high, f32[64,256]{1,0:T(8,128)S(1)} %get-tuple-element.22.left, f32[64,256]{1,0:T(8,128)S(1)} %get-tuple-element.23.right, ...), custom_call_target="tpu_custom_call" | custom-call | flops 20000000 | bytes 20000000 | tf_op jit(solution)/shard_map/outer/pallas_call | solution.py:439
  61.5 2.0 %collective-permute-done.5.left_corner = f32[8,256]{1,0:T(8,128)S(1)} collective-permute-done((f32[8,256]{1,0:T(8,128)S(1)}, f32[8,256]{1,0:T(8,128)S(1)}, u32[]{:S(2)}, u32[]{:S(2)}) %collective-permute-start.5) | collective-permute-done | bytes 8224 | tf_op jit(solution)/shard_map/ppermute | solution.py:437
  63.5 1.8 %collective-permute-done.6.right_corner = f32[8,256]{1,0:T(8,128)S(1)} collective-permute-done((f32[8,256]{1,0:T(8,128)S(1)}, f32[8,256]{1,0:T(8,128)S(1)}, u32[]{:S(2)}, u32[]{:S(2)}) %collective-permute-start.6) | collective-permute-done | bytes 8224 | tf_op jit(solution)/shard_map/ppermute | solution.py:438
  65.3 5.2 %all-to-all-done.1 = f32[32,32,128]{2,1,0:T(8,128)S(1)} async-done(((f32[32,32,128]{2,1,0:T(8,128)}), f32[32,32,128]{2,1,0:T(8,128)S(1)}, u32[]{:S(2)}, u32[]{:S(2)}) %all-to-all-start.1) | async-done | bytes 524320 | tf_op jit(solution)/shard_map/all_to_all | solution.py:466
  70.5 2.2 %merge.1 = f32[4,32,16,256]{3,2,1,0:T(8,128)} custom-call(f32[4,32,16,256]{3,2,1,0:T(8,128)} %outer.1.stepped, f32[1024,128]{1,0:T(8,128)S(1)} %bitcast.6, f32[8,256]{1,0:T(8,128)S(1)} %collective-permute-done.5.left_corner, f32[8,256]{1,0:T(8,128)S(1)} %collective-permute-done.6.right_corner), custom_call_target="tpu_custom_call", output_to_operand_aliasing={{}: (0, {})} | custom-call | tf_op jit(solution)/shard_map/merge/pallas_call | solution.py:467
  (24 shorter events, 0.1 us)
Async XLA Ops:
  0.0 1.6 %copy-start = (f32[4,32,16,256]{3,2,1,0:T(8,128)S(1)}, f32[4,32,16,256]{3,2,1,0:T(8,128)}, u32[]{:S(2)}) copy-start(f32[4,32,16,256]{3,2,1,0:T(8,128)} %state.7) | copy-start | bytes 6291460
  1.6 14.6 %copy-start.10 = (f32[8]{0:T(128)S(1)}, f32[8]{0:T(128)}, u32[]{:S(2)}) copy-start(f32[8]{0:T(128)} %resistance.1) | copy-start | bytes 100
  1.6 14.6 %copy-start.11 = (f32[8]{0:T(128)S(1)}, f32[8]{0:T(128)}, u32[]{:S(2)}) copy-start(f32[8]{0:T(128)} %relax.1) | copy-start | bytes 100
  1.6 16.9 %copy-start.1 = (f32[4,32,16,256]{3,2,1,0:T(8,128)S(1)}, f32[4,32,16,256]{3,2,1,0:T(8,128)}, u32[]{:S(2)}) copy-start(f32[4,32,16,256]{3,2,1,0:T(8,128)} %state.7) | copy-start | bytes 6291460
  1.9 16.6 %collective-permute-start = (f32[144,256]{1,0:T(8,128)S(1)}, f32[144,256]{1,0:T(8,128)S(1)}, u32[]{:S(2)}, u32[]{:S(2)}) collective-permute-start(f32[144,256]{1,0:T(8,128)S(1)} %get-tuple-element.16), channel_id=1, source_target_pairs={{4,8},{12,16},{20,24},{28,32},{36,40},{44,48},{52,56},{60,64},{68,... | collective-permute-start | bytes 442376 | tf_op jit(solution)/shard_map/ppermute | solution.py:414
  3.9 14.6 %collective-permute-start.1 = (f32[136,256]{1,0:T(8,128)S(1)}, f32[136,256]{1,0:T(8,128)S(1)}, u32[]{:S(2)}, u32[]{:S(2)}) collective-permute-start(f32[136,256]{1,0:T(8,128)S(1)} %get-tuple-element.17), channel_id=1, source_target_pairs={{1,2},{2,1},{5,6},{6,5},{9,10},{10,9},{13,14},{14,13},{17,18},{18,... | collective-permute-start | bytes 417800 | tf_op jit(solution)/shard_map/ppermute | solution.py:414
  4.5 14.0 %collective-permute-start.3 = (f32[136,256]{1,0:T(8,128)S(1)}, f32[136,256]{1,0:T(8,128)S(1)}, u32[]{:S(2)}, u32[]{:S(2)}) collective-permute-start(f32[136,256]{1,0:T(8,128)S(1)} %get-tuple-element.19), channel_id=1, source_target_pairs={{0,1},{2,3},{1,0},{3,2},{4,5},{6,7},{5,4},{7,6},{8,9},{10,11},{9,8... | collective-permute-start | bytes 417800 | tf_op jit(solution)/shard_map/ppermute | solution.py:414
  9.0 9.5 %collective-permute-start.2 = (f32[64,256]{1,0:T(8,128)S(1)}, f32[64,256]{1,0:T(8,128)S(1)}, u32[]{:S(2)}, u32[]{:S(2)}) collective-permute-start(f32[64,256]{1,0:T(8,128)S(1)} %get-tuple-element.18), channel_id=1, source_target_pairs={{0,4},{8,12},{16,20},{24,28},{32,36},{40,44},{48,52},{56,60},{64,6... | collective-permute-start | bytes 196616 | tf_op jit(solution)/shard_map/ppermute | solution.py:414
  16.1 0.8 %copy-start.7 = (s32[32,256]{1,0:T(8,128)S(1)}, s32[32,256]{1,0:T(8,128)}, u32[]{:S(2)}) copy-start(s32[32,256]{1,0:T(8,128)} %zone.1) | copy-start | bytes 98308
  16.9 0.8 %copy-start.8 = (f32[32,256]{1,0:T(8,128)S(1)}, f32[32,256]{1,0:T(8,128)}, u32[]{:S(2)}) copy-start(f32[32,256]{1,0:T(8,128)} %aux.1) | copy-start | bytes 98308
  18.3 24.5 %copy-start.2 = (f32[2,2,64,128]{3,2,1,0:T(8,128)S(1)}, f32[2,2,64,128]{3,2,1,0:T(8,128)}, u32[]{:S(2)}) copy-start(f32[2,2,64,128]{3,2,1,0:T(8,128)} %constant.14.clone.turn) | copy-start | bytes 393220
  18.3 24.5 %copy-start.3 = (bf16[2,128,272]{2,1,0:T(8,128)(2,1)S(1)}, bf16[2,128,272]{2,1,0:T(8,128)(2,1)}, u32[]{:S(2)}) copy-start(bf16[2,128,272]{2,1,0:T(8,128)(2,1)} %constant.11.clone.wave_small) | copy-start | bytes 417796
  18.3 24.5 %copy-start.4 = (bf16[2,128,272]{2,1,0:T(8,128)(2,1)S(1)}, bf16[2,128,272]{2,1,0:T(8,128)(2,1)}, u32[]{:S(2)}) copy-start(bf16[2,128,272]{2,1,0:T(8,128)(2,1)} %constant.10.clone.wave) | copy-start | bytes 417796
  18.3 30.1 %copy-start.5 = (bf16[2,128,256]{2,1,0:T(8,128)(2,1)S(1)}, bf16[2,128,256]{2,1,0:T(8,128)(2,1)}, u32[]{:S(2)}) copy-start(bf16[2,128,256]{2,1,0:T(8,128)(2,1)} %constant.13.clone.wave_small) | copy-start | bytes 393220
  18.3 30.1 %copy-start.6 = (bf16[2,128,256]{2,1,0:T(8,128)(2,1)S(1)}, bf16[2,128,256]{2,1,0:T(8,128)(2,1)}, u32[]{:S(2)}) copy-start(bf16[2,128,256]{2,1,0:T(8,128)(2,1)} %constant.12.clone.wave) | copy-start | bytes 393220
  18.3 30.1 %copy-start.9 = (s32[64]{0:T(128)S(1)}, s32[64]{0:T(128)}, u32[]{:S(2)}) copy-start(s32[64]{0:T(128)} %param.16) | copy-start | bytes 772
  43.3 5.1 %collective-permute-start.4 = (f32[256,128]{1,0:T(8,128)S(1)}, f32[256,128]{1,0:T(8,128)S(1)}, u32[]{:S(2)}, u32[]{:S(2)}) collective-permute-start(f32[256,128]{1,0:T(8,128)S(1)} %analysis.1.mine), channel_id=1, source_target_pairs={{0,32},{32,0},{1,33},{33,1},{2,34},{34,2},{3,35},{35,3},{4,36},{36... | collective-permute-start | bytes 393224 | tf_op jit(solution)/shard_map/ppermute | solution.py:458
  49.8 20.7 %all-to-all-start.1 = ((f32[32,32,128]{2,1,0:T(8,128)}), f32[32,32,128]{2,1,0:T(8,128)S(1)}, u32[]{:S(2)}, u32[]{:S(2)}) async-start(f32[32,32,128]{2,1,0:T(8,128)} %bitcast.3), calls=%async_computation.1 | async-start | bytes 1048576 | tf_op jit(solution)/shard_map/all_to_all | solution.py:466
  55.1 8.4 %collective-permute-start.5 = (f32[8,256]{1,0:T(8,128)S(1)}, f32[8,256]{1,0:T(8,128)S(1)}, u32[]{:S(2)}, u32[]{:S(2)}) collective-permute-start(f32[8,256]{1,0:T(8,128)S(1)} %get-tuple-element.25), channel_id=1, source_target_pairs={{0,4},{4,8},{8,12},{12,16},{16,20},{20,24},{24,28},{28,32},{32,36}... | collective-permute-start | bytes 24584 | tf_op jit(solution)/shard_map/ppermute | solution.py:437
  56.6 8.7 %collective-permute-start.6 = (f32[8,256]{1,0:T(8,128)S(1)}, f32[8,256]{1,0:T(8,128)S(1)}, u32[]{:S(2)}, u32[]{:S(2)}) collective-permute-start(f32[8,256]{1,0:T(8,128)S(1)} %get-tuple-element.26), channel_id=1, source_target_pairs={{4,0},{8,4},{12,8},{16,12},{20,16},{24,20},{28,24},{32,28},{36,32}... | collective-permute-start | bytes 24584 | tf_op jit(solution)/shard_map/ppermute | solution.py:438

commit v6 on v1

--- a/solution.py
+++ b/solution.py
@@ -16,6 +16,8 @@
 SECTORS = 64
 ROWS = NA // SECTORS
 HALF = ROWS // 2
+LONG = HALF + 2
+TURN_AT = SECTORS // 2 * LONG
 HTS = 16
 NR = 256
 COMPS = 4
@@ -32,19 +34,22 @@
 
 
 def mode_tables():
-    azimuth = (sector_of_chunk()[: SECTORS // 2, None] * ROWS + np.arange(HALF)[None, :]).reshape(-1)
-    tables = []
+    first = sector_of_chunk()[: SECTORS // 2, None] * ROWS
+    azimuth = (first - 2 + np.arange(LONG)[None, :]).reshape(-1)
+    out = np.zeros((2, 2, MODES, TURN_AT + 64), jnp.bfloat16)
     for parity in range(2):
         modes = np.arange(parity, MODES, 2)
         phase = (modes[:, None] * azimuth[None, :] % NA) * (2.0 * math.pi / NA)
-        turn = (modes * HALF % NA) * (2.0 * math.pi / NA)
-        more = np.zeros((MODES // 2, 128))
-        more[:, 0] = np.cos(turn)
-        more[:, 1] = np.sin(turn)
-        more[:, 2] = np.where(modes == 0, 1.0, 2.0) / NA
-        tables.append((np.concatenate([np.cos(phase), np.sin(phase)], 0), more))
-    waves, turns = [np.stack(t).astype(np.float32) for t in zip(*tables)]
-    return (*split(waves), turns)
+        out[0, parity, :, :TURN_AT], out[1, parity, :, :TURN_AT] = split(np.concatenate([np.cos(phase), np.sin(phase)], 0))
+        turn = (modes * LONG % NA) * (2.0 * math.pi / NA)
+        for k, value in enumerate((np.cos(turn), np.sin(turn))):
+            rest = value.astype(np.float32)
+            for part in range(3):
+                large = rest.astype(jnp.bfloat16)
+                out[0, parity, : MODES // 2, TURN_AT + 3 * k + part] = large
+                rest = rest - large.astype(np.float32)
+        out[0, parity, : MODES // 2, TURN_AT + 6] = np.where(modes == 0, 1.0, 2.0) / NA
+    return out
 
 
 def split(x):
@@ -89,11 +94,28 @@
     return out
 
 
+def odd_slab():
+    return lax.axis_index("core") == 1
+
+
+def odd_sector():
+    return lax.rem(lax.axis_index("z"), 2) == 1
+
+
+def lowest_slab():
+    return lax.axis_index("hx") * 2 + lax.axis_index("core") == 0
+
+
+def highest_slab():
+    return lax.axis_index("hx") * 2 + lax.axis_index("core") == 3
+
+
 HT_ROWS = 136
 AZ_ROWS = 72
-
-
-def pack_kernel(state, up, down):
+AZ_AHEAD = 288
+
+
+def pack_kernel(state, to_right, ht_then, ht_first, up, down):
     inv_r, half_arc = radial_rates(NR)
     zero = jnp.zeros((1, NR), jnp.float32)
     for out, edge, inside, sign in ((up, HTS - 1, HTS - 2, 1.0), (down, 0, 1, -1.0)):
@@ -107,6 +129,24 @@
         out[128:129] = v[0:1]
         out[129:130] = v[ROWS - 1 : ROWS]
         out[130:HT_ROWS] = jnp.zeros((HT_ROWS - 130, NR), jnp.float32)
+    odd = odd_slab()
+    ht_first[...] = jnp.where(odd, down[...], up[...])
+    ht_then[...] = jnp.where(odd, up[...], down[...])
+
+    no_row = jnp.zeros((1, 128), jnp.float32)
+    edge_message(to_right, state, ROWS - 1, ROWS - 2, 1.0, no_row, no_row)
+    to_right[64:AZ_AHEAD] = jnp.zeros((AZ_AHEAD - 64, 128), jnp.float32)
+
+
+def edge_message(out, state, j, inside, sign, w_low, w_high):
+    width = w_low.shape[1]
+    inv_r, half_arc = radial_rates(width)
+    p, u, v, w = [state[i, j, :, 0:width] for i in range(4)]
+    v_in, p_in = state[2, inside, :, 0:width], state[0, inside, :, 0:width]
+    out[0:16] = p
+    out[16:32] = v
+    out[32:48] = p - DT * (radial_diff(u) + u * inv_r + row_diff(w, w_low, w_high) - sign * half_arc * v_in)
+    out[48:64] = v + (DT * sign) * half_arc * p_in
 
 
 def ground_kernel(resistance, relax, state, zone, aux, ground):
@@ -118,27 +158,26 @@
     ground[2] = q + DT * lookup(ids, relax) * (p0 - q)
 
 
-def edge_kernel(flag, state, low, high, ground, to_left, to_right):
-    inv_r, half_arc = radial_rates(NR)
-    on_ground = flag[0] == 1
-    for out, j, inside, sign, corner in ((to_right, ROWS - 1, ROWS - 2, 1.0, 129), (to_left, 0, 1, -1.0, 128)):
-        p, u, v, w = [state[i, j] for i in range(4)]
-        w_low = jnp.where(on_ground, ground[0, j : j + 1], low[32 + j : 33 + j])
-        out[0:16] = p
-        out[16:32] = v
-        rate = radial_diff(u) + u * inv_r + row_diff(w, w_low, high[32 + j : 33 + j]) - sign * half_arc * state[2, inside]
-        out[32:48] = p - DT * rate
-        out[48:64] = v + (DT * sign) * half_arc * state[0, inside]
-        out[64:65] = low[corner : corner + 1]
-        out[65:66] = high[corner : corner + 1]
-        out[66:AZ_ROWS] = jnp.zeros((AZ_ROWS - 66, NR), jnp.float32)
-
-
-def two_stages(width, flag, state, low, high, left, right, ground, mid, ghost, emit):
-    on_ground, on_top = flag[0] == 1, flag[1] == 1
+def unswap(odd, first, then, behind, ahead):
+    behind[...] = jnp.where(odd, first[...], then[...])
+    ahead[...] = jnp.where(odd, then[...], first[...])
+
+
+def two_stages(width, state, low, high, left, right, ground, mid, ghost):
+    on_ground, on_top = lowest_slab(), highest_slab()
     inv_r, half_arc = radial_rates(width)
     cols = slice(0, width)
     turn = DT * half_arc
+
+    def beyond(a, b):
+        return jnp.zeros((b - a, width), jnp.float32) if right is None else right[a:b, cols]
+
+    def corners(k):
+        if right is None:
+            return 0.0
+        sub = lax.broadcasted_iota(jnp.int32, (ROWS, width), 0)
+        last = jnp.where(sub == ROWS - 1, -right[k : k + 1, cols], 0.0)
+        return turn * jnp.where(sub == 0, left[k : k + 1, cols], last)
 
     p0, p1, u0, v0, w0, w1 = [plane(state, i, k, width) for i, k in ((0, 0), (0, 1), (1, 0), (2, 0), (3, 0), (3, 1))]
     p15, w15 = plane(state, 0, HTS - 1, width), plane(state, 3, HTS - 1, width)
@@ -146,18 +185,11 @@
     bw = jnp.where(on_ground, ground[0, :, cols], low[32:64, cols])
     ghost[0], ghost[1], ghost[2], ghost[3] = bp, bw, high[0:32, cols], high[32:64, cols]
 
-    sub = lax.broadcasted_iota(jnp.int32, (ROWS, width), 0)
-
-    def corners(k):
-        return turn * jnp.where(
-            sub == 0, left[k : k + 1, cols], jnp.where(sub == ROWS - 1, -right[k : k + 1, cols], 0.0)
-        )
-
     top_p = high[64:96, cols] + (0.5 * DT) * w15 + corners(65)
     top_w = high[96:128, cols] + (0.5 * DT) * p15
     low_p = low[64:96, cols] - (0.5 * DT) * w0 + corners(64)
     low_w = low[96:128, cols] - (0.5 * DT) * p0
-    v_diff = 2.0 * row_diff(v0, left[16:17, cols], right[16:17, cols]) * half_arc
+    v_diff = 2.0 * row_diff(v0, left[16:17, cols], beyond(16, 17)) * half_arc
     mid_p0 = p0 - DT * (radial_diff(u0) + u0 * inv_r + v_diff + 0.5 * (w1 - bw))
     mid_w0 = w0 - (0.5 * DT) * (p1 - bp)
     ghost[4] = jnp.where(on_ground, mid_p0, low_p)
@@ -167,8 +199,8 @@
 
     mid[0, 0] = left[32:48, cols] - turn * state[2, 0, :, cols]
     mid[2, 0] = left[48:64, cols] - turn * state[0, 0, :, cols]
-    mid[0, ROWS + 1] = right[32:48, cols] + turn * state[2, ROWS - 1, :, cols]
-    mid[2, ROWS + 1] = right[48:64, cols] + turn * state[0, ROWS - 1, :, cols]
+    mid[0, ROWS + 1] = beyond(32, 48) + turn * state[2, ROWS - 1, :, cols]
+    mid[2, ROWS + 1] = beyond(48, 64) + turn * state[0, ROWS - 1, :, cols]
 
     def rates(p, u, v_diff, p_diff, w, j, first):
         p_low, w_low, p_high, w_high = [ghost[first + i, pl.ds(j, 1)] for i in range(4)]
@@ -186,7 +218,7 @@
 
     first(0, state[0, 1, :, cols] - left[0:16, cols], state[2, 1, :, cols] - left[16:32, cols])
     end = ROWS - 2
-    first(ROWS - 1, right[0:16, cols] - state[0, end, :, cols], right[16:32, cols] - state[2, end, :, cols])
+    first(ROWS - 1, beyond(0, 16) - state[0, end, :, cols], beyond(16, 32) - state[2, end, :, cols])
 
     @pl.loop(1, ROWS - 1, unroll=5)
     def _(j):
@@ -201,34 +233,110 @@
         found = rates(p, u, mid[2, j + 2] - mid[2, j], mid[0, j + 2] - mid[0, j], w, j, 4)
         return [0.5 * (state[i, j, :, cols] + m - DT * r) for i, (m, r) in enumerate(zip((p, u, v, w), found))]
 
-    @pl.loop(0, HALF, unroll=2)
-    def _(l):
-        emit(l, second(l), second(l + HALF))
-
-
-def inner_kernel(flag, state, low, high, left, right, ground, packed, mid, ghost):
+    return second
+
+
+def corner_weight(width):
+    return (0.5 * DT) * (0.5 * DT) * radial_rates(width)[1]
+
+
+def inner_kernel(state, left, ht_then, ht_first, ground, packed, low, high, mid, ghost):
+    unswap(odd_slab(), ht_first, ht_then, low, high)
     near = lax.broadcasted_iota(jnp.int32, (HTS, 128), 1) < NI
-
-    def emit(l, one, two):
+    height = lax.broadcasted_iota(jnp.int32, (HTS, 128), 0)
+    second = two_stages(128, state, low, high, left, None, ground, mid, ghost)
+    on_ground = lowest_slab()
+
+    def emit(r, one, two):
         for i in range(COMPS):
             both = jnp.where(near, one[i], pltpu.roll(two[i], NI, 1))
-            packed[pl.ds(i * HTS * HALF + l, HTS, stride=HALF), :] = both
-
-    two_stages(128, flag, state, low, high, left, right, ground, mid, ghost, emit)
-
-
-def outer_kernel(flag, state, low, high, left, right, ground, stepped, mid, ghost):
-    def emit(l, one, two):
-        for i in range(COMPS):
-            stepped[i, l] = one[i]
-            stepped[i, l + HALF] = two[i]
-
-    two_stages(NR, flag, state, low, high, left, right, ground, mid, ghost, emit)
-
-
-def filter_kernel(large, small, turn, cutoff, x_ref, o_ref):
-    n = NA // 4
-    first, second = x_ref[:n], x_ref[n:]
+            packed[pl.ds(i * HTS * LONG + r, HTS, stride=LONG), :] = both
+
+    @pl.loop(0, HALF - 2, unroll=2)
+    def _(l):
+        emit(l + 2, second(l), second(l + LONG))
+
+    turn = DT * radial_rates(128)[1]
+    none = jnp.zeros((HTS, 128), jnp.float32)
+
+    p0, v0 = state[0, 0, :, 0:128], state[2, 0, :, 0:128]
+    own_p, own_v = mid[0, 1] - turn * left[16:32], mid[2, 1] - turn * left[0:16]
+    far_p = -turn * v0
+    far_low = jnp.where(on_ground, far_p[0:1], -turn * low[128:129, 0:128])
+    far_high = -turn * high[128:129, 0:128]
+    last = [
+        0.5 * (far_p - turn * own_v),
+        (-0.5 * DT) * radial_diff(far_p),
+        (-0.5 * turn) * (p0 + own_p),
+        (-0.5 * DT) * row_diff(far_p, far_low, far_high),
+    ]
+    before = [0.5 * turn * turn * p0, none, 0.5 * turn * turn * v0, none]
+
+    weight = 0.5 * DT * turn * 0.5
+
+    end = ROWS - 1
+    at_ground = jnp.logical_and(on_ground, height == 0)
+    owed = [jnp.where(at_ground, ground[1, end : end + 1, 0:128], 0.0), none]
+    factor = jnp.where(at_ground, (-0.25 * DT) * turn * v0, 0.0)
+    for below, above in ((w_below(low, ground, end), high[32 + end : 33 + end]), (low[129:130], high[129:130])):
+        below, above = weight * below[:, 0:128], -weight * above[:, 0:128]
+        owed.append(jnp.where(height == HTS - 1, above, jnp.where(height == 0, below, 0.0)))
+
+    emit(0, before, second(HALF))
+    emit(1, last, second(HALF + 1))
+    emit(HALF, second(HALF - 2), owed)
+    emit(HALF + 1, second(HALF - 1), [factor] + [none] * 3)
+
+
+def w_below(low, ground, j):
+    return jnp.where(lowest_slab(), ground[0, j : j + 1], low[32 + j : 33 + j])
+
+
+def edge_kernel(state, ht_then, ht_first, ground, after, to_left, to_right, low, high):
+    unswap(odd_slab(), ht_first, ht_then, low, high)
+    end = ROWS - 1
+    for out, j, inside, sign, corner in ((to_right, end, end - 1, 1.0, 129), (to_left, 0, 1, -1.0, 128)):
+        edge_message(out, state, j, inside, sign, w_below(low, ground, j), high[32 + j : 33 + j])
+        out[64:65] = low[corner : corner + 1]
+        out[65:66] = high[corner : corner + 1]
+        out[66:AZ_ROWS] = jnp.zeros((AZ_ROWS - 66, NR), jnp.float32)
+
+
+def outer_kernel(state, ht_then, ht_first, left, right, ground, stepped, low, high, mid, ghost):
+    unswap(odd_slab(), ht_first, ht_then, low, high)
+    second = two_stages(NR, state, low, high, left, right, ground, mid, ghost)
+
+    @pl.loop(0, ROWS, unroll=2)
+    def _(j):
+        for i, value in enumerate(second(j)):
+            stepped[i, j] = value
+
+
+def ground_terms(circle):
+    near = lax.broadcasted_iota(jnp.int32, (1, 128), 1) < NI
+    sectors = sector_of_chunk().tolist()
+
+    def row(chunk, r):
+        return pl.ds(chunk * LONG + r, 1)
+
+    for k, sector in enumerate(sectors):
+        last = sectors.index((sector - 1) % SECTORS)
+        term = circle[row(last, HALF), :] * circle[row(k, HALF + 1), :]
+        circle[row(k, 1), :] = circle[row(k, 1), :] + jnp.where(near, pltpu.roll(term, NI, 1), 0.0)
+    for k in range(SECTORS):
+        for r in (HALF, HALF + 1):
+            circle[row(k, r), :] = jnp.where(near, circle[row(k, r), :], 0.0)
+
+
+def filter_kernel(table, cutoff, x_ref, left, right, o_ref, circle):
+    m = SECTORS // 2 * LONG
+    circle[...] = x_ref[...]
+
+    @pl.when(lax.axis_index("y") * 16 + lax.axis_index("z") * 2 + lax.axis_index("x") == 0)
+    def _():
+        ground_terms(circle)
+
+    first, second = circle[:m], circle[m:]
     h = MODES // 2
     mode = lax.broadcasted_iota(jnp.int32, (h, 128), 0) * 2
     near = lax.broadcasted_iota(jnp.int32, (h, 128), 1) < NI
@@ -236,8 +344,10 @@
     outs = []
     for parity in range(2):
         folded = first + second if parity == 0 else first - second
-        waves = large[parity], small[parity]
-        cs, sn, weight = [turn[parity, :, k : k + 1] for k in range(3)]
+        waves = table[0, parity, :, :TURN_AT], table[1, parity, :, :TURN_AT]
+        parts = table[0, parity, :h, TURN_AT : TURN_AT + 64].astype(jnp.float32)
+        cs, sn = [parts[:, k : k + 1] + parts[:, k + 1 : k + 2] + parts[:, k + 2 : k + 3] for k in (0, 3)]
+        weight = parts[:, 6:7]
         coef = product(waves, split(folded), ((1,), (0,)))
         a, b = coef[:h], coef[h:]
         a_all = jnp.where(near, a, a * cs - b * sn)
@@ -247,10 +357,16 @@
         b_all = (b_all + pltpu.roll(b_all, NI, 1)) * keep
         a_back = jnp.where(near, a_all, a_all * cs + b_all * sn)
         b_back = jnp.where(near, b_all, b_all * cs - a_all * sn)
-        back = jnp.concatenate([a_back, b_back], 0)
-        outs.append(product(waves, split(back), ((0,), (0,))))
-    o_ref[:n] = outs[0] + outs[1]
-    o_ref[n:] = outs[0] - outs[1]
+        both = jnp.concatenate([a_back, b_back], 0)
+        outs.append(product(waves, split(both), ((0,), (0,))))
+    for half in range(2):
+        circle[half * m : (half + 1) * m] = outs[0] + outs[1] if half == 0 else outs[0] - outs[1]
+    row_near = lax.broadcasted_iota(jnp.int32, (HALF, 128), 1) < NI
+    for k in range(SECTORS):
+        at = k * LONG
+        o_ref[k * HALF : (k + 1) * HALF] = jnp.where(
+            row_near, circle[at + 2 : at + 2 + HALF], circle[at : at + HALF]
+        )
 
 
 def merge_kernel(stepped, back, out, rows, tile, beside, sems):
@@ -278,9 +394,6 @@
 
 def per_device(state, zone_id, ground_aux, resistance, relax_rate, cutoff):
     f32 = jnp.float32
-    ht = lax.axis_index(HT)
-    flags = jnp.stack([ht == 0, ht == 3]).astype(jnp.int32)
-
     vmem = pl.BlockSpec(memory_space=pltpu.VMEM)
     smem = pl.BlockSpec(memory_space=pltpu.SMEM)
     anywhere = pl.BlockSpec(memory_space=pl.ANY)
@@ -291,11 +404,15 @@
     def shapes(*dims):
         return tuple(jax.ShapeDtypeStruct(d, f32) for d in dims)
 
-    up, down = call(
-        pack_kernel, out_shape=shapes((HT_ROWS, NR), (HT_ROWS, NR)), in_specs=[vmem], out_specs=(vmem, vmem), name="pack"
+    ht_message, az_message = (HT_ROWS, NR), (AZ_ROWS, NR)
+    to_right, ht_then, ht_first = call(
+        pack_kernel,
+        out_shape=shapes((AZ_AHEAD, 128), ht_message, ht_message),
+        in_specs=[vmem],
+        out_specs=(vmem,) * 3,
+        scratch_shapes=[pltpu.VMEM(ht_message, f32)] * 2,
+        name="pack",
     )(state)
-    low = lax.ppermute(up, HT, [(i, i + 1) for i in range(3)])
-    high = lax.ppermute(down, HT, [(i + 1, i) for i in range(3)])
     ground = call(
         ground_kernel,
         out_shape=shapes((3, ROWS, NR))[0],
@@ -303,45 +420,58 @@
         out_specs=vmem,
         name="ground",
     )(resistance, relax_rate, state, zone_id, ground_aux)
-    to_left, to_right = call(
-        edge_kernel,
-        out_shape=shapes((AZ_ROWS, NR), (AZ_ROWS, NR)),
-        in_specs=[smem] + [vmem] * 4,
-        out_specs=(vmem, vmem),
-        name="edge",
-    )(flags, state, low, high, ground)
-    left = lax.ppermute(to_right, AZ, [(i, (i + 1) % SECTORS) for i in range(SECTORS)])
-    right = lax.ppermute(to_left, AZ, [((i + 1) % SECTORS, i) for i in range(SECTORS)])
-
-    operands = (flags, state, low, high, left, right, ground)
+    def swap(x, start):
+        pairs = [(i, i + 1) for i in range(start, 3, 2)]
+        return lax.ppermute(x, HT, pairs + [(b, a) for a, b in pairs])
+
+    rightward = [(i, (i + 1) % SECTORS) for i in range(SECTORS)]
+    leftward = [(b, a) for a, b in rightward]
+    ahead = lax.ppermute(to_right, AZ, rightward)
+    ht_then, ht_first = swap(ht_then, 1), swap(ht_first, 0)
 
     def scratch(width):
         return [pltpu.VMEM((COMPS, ROWS + 2, HTS, width), f32), pltpu.VMEM((8, ROWS, width), f32)]
 
+    halos = [pltpu.VMEM(ht_message, f32)] * 2
     packed = call(
         inner_kernel,
         mib=12,
-        out_shape=shapes((COMPS * HTS * HALF, 128))[0],
-        in_specs=[smem] + [vmem] * 6,
+        out_shape=shapes((COMPS * HTS * LONG, 128))[0],
+        in_specs=[vmem] * 5,
         out_specs=vmem,
-        scratch_shapes=scratch(128),
+        scratch_shapes=halos + scratch(128),
         cost_estimate=pl.CostEstimate(flops=10**7, bytes_accessed=6 * 10**6, transcendentals=0),
         name="inner",
-    )(*operands)
-    circle = lax.all_to_all(packed.reshape(SECTORS, HALF, 128), SPREAD, 0, 0, tiled=True)
+    )(state, ahead, ht_then, ht_first, ground)
+    to_left, to_right = call(
+        edge_kernel,
+        out_shape=shapes(az_message, az_message),
+        in_specs=[vmem] * 4 + [anywhere],
+        out_specs=(vmem,) * 2,
+        scratch_shapes=halos,
+        name="edge",
+    )(state, ht_then, ht_first, ground, packed)
+    circle = lax.all_to_all(packed.reshape(SECTORS, LONG, 1, 128), SPREAD, 0, 0, tiled=True)
+    left = lax.ppermute(to_right, AZ, rightward)
+    right = lax.ppermute(to_left, AZ, leftward)
     stepped = call(
         outer_kernel,
         mib=16,
         out_shape=shapes((COMPS, ROWS, HTS, NR))[0],
-        in_specs=[smem] + [vmem] * 6,
+        in_specs=[vmem] * 6,
         out_specs=vmem,
-        scratch_shapes=scratch(NR),
+        scratch_shapes=halos + scratch(NR),
         cost_estimate=pl.CostEstimate(flops=2 * 10**7, bytes_accessed=2 * 10**7, transcendentals=0),
         name="outer",
-    )(*operands)
+    )(state, ht_then, ht_first, left, right, ground)
     kept = call(
-        filter_kernel, out_shape=shapes((NA // 2, 128))[0], in_specs=[vmem] * 5, out_specs=vmem, name="filter"
-    )(*map(jnp.asarray, mode_tables()), cutoff.reshape(1, NI), circle.reshape(NA // 2, 128))
+        filter_kernel,
+        out_shape=shapes((NA // 2, 128))[0],
+        in_specs=[vmem] * 3 + [anywhere] * 2,
+        out_specs=vmem,
+        scratch_shapes=[pltpu.VMEM((SECTORS * LONG, 128), f32)],
+        name="filter",
+    )(jnp.asarray(mode_tables()), cutoff.reshape(1, NI), circle.reshape(SECTORS * LONG, 128), left, right)
     back = lax.all_to_all(kept.reshape(SECTORS, HALF, 128), SPREAD, 0, 0, tiled=True)
     return call(
         merge_kernel,

time: 80.3 us -> 75.5 us (0.940)
  the two profiles are of different devices: /device:TPU:1 before, /device:TPU:32 now
where the time goes in v6:
time: 75.5 us; the launch traced here: 74.7 us
  waiting for transfers between devices  29.8 us (39%)
  starting transfers between devices  28.1 us (37%)
  Pallas kernels  12.6 us (17%)
  local copies, waits for them, and re-layouts  4.21 us (6%)
    ppermute x1, waiting for transfers between devices, per_device(): left = lax.ppermute(to_right, AZ, rightward)  13.1 us
    all_to_all x1, waiting for transfers between devices, per_device(): lax.all_to_all(kept.reshape(SECTORS, HALF, 128), SPREAD, 0, 0, tiled=True)  12.7 us
    all_to_all x1, starting transfers between devices, per_device(): lax.all_to_all(packed.reshape(SECTORS, LONG, 1, 128), SPREAD, 0, 0, tiled...  11 us
    all_to_all x1, starting transfers between devices, per_device(): lax.all_to_all(kept.reshape(SECTORS, HALF, 128), SPREAD, 0, 0, tiled=True)  7.85 us
    ppermute x2, starting transfers between devices, swap(): return lax.ppermute(x, HT, pairs + [(b, a) for a, b in pairs])  5.12 us
    pallas_call x1, Pallas kernels, per_device(): call(outer_kernel, mib=16, out_shape=shapes((COMPS, ROWS, HTS, NR))[0], i...  4.29 us
    unnamed x16, local copies, waits for them, and re-layouts  4.21 us
    all_to_all x1, waiting for transfers between devices, per_device(): lax.all_to_all(packed.reshape(SECTORS, LONG, 1, 128), SPREAD, 0, 0, tiled...  3.05 us
  transfers between devices with their start and end apart: 7, of which 4 were waited for; matrix products, arithmetic and copies ran while one was open for 0% of the time, Pallas kernels for 7%

profile of v6, /device:TPU:32, one launch (start us, length us, event | category | flops | bytes accessed | tf_op | source)
XLA Modules:
  0.0 74.7 jit_solution(15374745427802573933)
XLA Ops:
  0.0 1.6 %copy-done = f32[4,32,16,256]{3,2,1,0:T(8,128)S(1)} copy-done((f32[4,32,16,256]{3,2,1,0:T(8,128)S(1)}, f32[4,32,16,256]{3,2,1,0:T(8,128)}, u32[]{:S(2)}) %copy-start) | copy-done | bytes 2097176
  1.6 0.3 pack.1
  1.9 2.0 %collective-permute-start.2 = (f32[288,128]{1,0:T(8,128)S(1)}, f32[288,128]{1,0:T(8,128)S(1)}, u32[]{:S(2)}, u32[]{:S(2)}) collective-permute-start(f32[288,128]{1,0:T(8,128)S(1)} %get-tuple-element.12), channel_id=1, source_target_pairs={{0,4},{4,8},{8,12},{12,16},{16,20},{20,24},{24,28},{28,32},{32,36}... | collective-permute-start | bytes 442376 | tf_op jit(solution)/shard_map/ppermute | solution.py:429
  3.9 0.7 collective-permute-start
  4.5 4.5 %collective-permute-start.1 = (f32[136,256]{1,0:T(8,128)S(1)}, f32[136,256]{1,0:T(8,128)S(1)}, u32[]{:S(2)}, u32[]{:S(2)}) collective-permute-start(f32[136,256]{1,0:T(8,128)S(1)} %get-tuple-element.11), channel_id=1, source_target_pairs={{0,1},{2,3},{1,0},{3,2},{4,5},{6,7},{5,4},{7,6},{8,9},{10,11},{9,8... | collective-permute-start | bytes 417800 | tf_op jit(solution)/shard_map/ppermute | solution.py:425
  9.0 0.8 %copy-done.3 = s32[32,256]{1,0:T(8,128)S(1)} copy-done((s32[32,256]{1,0:T(8,128)S(1)}, s32[32,256]{1,0:T(8,128)}, u32[]{:S(2)}) %copy-start.3) | copy-done | bytes 32792
  9.7 0.8 %copy-done.4 = f32[32,256]{1,0:T(8,128)S(1)} copy-done((f32[32,256]{1,0:T(8,128)S(1)}, f32[32,256]{1,0:T(8,128)}, u32[]{:S(2)}) %copy-start.4) | copy-done | bytes 32792
  10.5 0.6 ground.1
  11.1 0.0 collective-permute-done.ht_then
  11.1 0.0 collective-permute-done.1.ht_first
  11.2 3.0 %inner.1.after = f32[1152,128]{1,0:T(8,128)} custom-call(f32[4,32,16,256]{3,2,1,0:T(8,128)S(1)} %copy-done.1, f32[288,128]{1,0:T(8,128)S(1)} %collective-permute-done.2.left, f32[136,256]{1,0:T(8,128)S(1)} %collective-permute-done.ht_then, f32[136,256]{1,0:T(8,128)S(1)} %collective-permute-done.1.ht_first, f32[3,32,256]{2,1,0:T(8,128)S(1)} %ground.1), custom_call_target="tpu_custom_call" | custom-call | flops 10000000 | bytes 6000000 | tf_op jit(solution)/shard_map/inner/pallas_call | solution.py:436
  14.1 11.0 %all-to-all-start = ((f32[64,18,1,128]{3,2,1,0:T(1,128)}), f32[64,18,1,128]{3,2,1,0:T(1,128)S(1)}, u32[]{:S(2)}, u32[]{:S(2)}) async-start(f32[64,18,1,128]{3,2,1,0:T(1,128)} %bitcast.1), calls=%async_computation | async-start | bytes 1179648 | tf_op jit(solution)/shard_map/all_to_all | solution.py:454
  25.2 0.1 edge.1
  25.3 1.5 %collective-permute-start.3 = (f32[72,256]{1,0:T(8,128)S(1)}, f32[72,256]{1,0:T(8,128)S(1)}, u32[]{:S(2)}, u32[]{:S(2)}) collective-permute-start(f32[72,256]{1,0:T(8,128)S(1)} %get-tuple-element.13), channel_id=1, source_target_pairs={{0,4},{4,8},{8,12},{12,16},{16,20},{20,24},{24,28},{28,32},{32,36}... | collective-permute-start | bytes 221192 | tf_op jit(solution)/shard_map/ppermute | solution.py:455
  26.8 0.6 collective-permute-start.4
  27.4 13.1 %collective-permute-done.3.left = f32[72,256]{1,0:T(8,128)S(1)} collective-permute-done((f32[72,256]{1,0:T(8,128)S(1)}, f32[72,256]{1,0:T(8,128)S(1)}, u32[]{:S(2)}, u32[]{:S(2)}) %collective-permute-start.3) | collective-permute-done | bytes 73760 | tf_op jit(solution)/shard_map/ppermute | solution.py:455
  40.5 1.0 %collective-permute-done.4.right = f32[72,256]{1,0:T(8,128)S(1)} collective-permute-done((f32[72,256]{1,0:T(8,128)S(1)}, f32[72,256]{1,0:T(8,128)S(1)}, u32[]{:S(2)}, u32[]{:S(2)}) %collective-permute-start.4) | collective-permute-done | bytes 73760 | tf_op jit(solution)/shard_map/ppermute | solution.py:456
  41.4 3.0 %all-to-all-done = f32[64,18,1,128]{3,2,1,0:T(1,128)S(1)} async-done(((f32[64,18,1,128]{3,2,1,0:T(1,128)}), f32[64,18,1,128]{3,2,1,0:T(1,128)S(1)}, u32[]{:S(2)}, u32[]{:S(2)}) %all-to-all-start) | async-done | bytes 589856 | tf_op jit(solution)/shard_map/all_to_all | solution.py:454
  44.5 1.1 %copy-done.2 = bf16[2,2,128,640]{3,2,1,0:T(8,128)(2,1)S(1)} copy-done((bf16[2,2,128,640]{3,2,1,0:T(8,128)(2,1)S(1)}, bf16[2,2,128,640]{3,2,1,0:T(8,128)(2,1)}, u32[]{:S(2)}) %copy-start.2) | copy-done | bytes 655384
  45.6 2.2 %filter.1 = f32[1024,128]{1,0:T(8,128)} custom-call(bf16[2,2,128,640]{3,2,1,0:T(8,128)(2,1)S(1)} %copy-done.2, s32[1,64]{1,0:T(1,128)S(1)} %bitcast.7, f32[1152,128]{1,0:T(8,128)S(1)} %bitcast.5, f32[72,256]{1,0:T(8,128)S(1)} %collective-permute-done.3.left, f32[72,256]{1,0:T(8,128)S(1)} %collective-permute-done.4.right), custom_call_target="tpu_custom_call" | custom-call | tf_op jit(solution)/shard_map/filter/pallas_call | solution.py:467
  47.8 7.8 %all-to-all-start.1 = ((f32[64,16,128]{2,1,0:T(8,128)}), f32[64,16,128]{2,1,0:T(8,128)S(1)}, u32[]{:S(2)}, u32[]{:S(2)}) async-start(f32[64,16,128]{2,1,0:T(8,128)} %bitcast.3), calls=%async_computation.1 | async-start | bytes 1048576 | tf_op jit(solution)/shard_map/all_to_all | solution.py:475
  55.6 4.3 %outer.1.stepped = f32[4,32,16,256]{3,2,1,0:T(8,128)} custom-call(f32[4,32,16,256]{3,2,1,0:T(8,128)S(1)} %copy-done.1, f32[136,256]{1,0:T(8,128)S(1)} %collective-permute-done.ht_then, f32[136,256]{1,0:T(8,128)S(1)} %collective-permute-done.1.ht_first, f32[72,256]{1,0:T(8,128)S(1)} %collective-permute-done.3.left, ...), custom_call_target="tpu_custom_call" | custom-call | flops 20000000 | bytes 20000000 | tf_op jit(solution)/shard_map/outer/pallas_call | solution.py:457
  59.9 12.7 %all-to-all-done.1 = f32[64,16,128]{2,1,0:T(8,128)S(1)} async-done(((f32[64,16,128]{2,1,0:T(8,128)}), f32[64,16,128]{2,1,0:T(8,128)S(1)}, u32[]{:S(2)}, u32[]{:S(2)}) %all-to-all-start.1) | async-done | bytes 524320 | tf_op jit(solution)/shard_map/all_to_all | solution.py:475
  72.6 2.1 %merge.1 = f32[4,32,16,256]{3,2,1,0:T(8,128)} custom-call(f32[4,32,16,256]{3,2,1,0:T(8,128)} %outer.1.stepped, f32[1024,128]{1,0:T(8,128)S(1)} %bitcast.6), custom_call_target="tpu_custom_call", output_to_operand_aliasing={{}: (0, {})} | custom-call | tf_op jit(solution)/shard_map/merge/pallas_call | solution.py:476
  (13 shorter events, 0.0 us)
Async XLA Ops:
  0.0 1.6 %copy-start = (f32[4,32,16,256]{3,2,1,0:T(8,128)S(1)}, f32[4,32,16,256]{3,2,1,0:T(8,128)}, u32[]{:S(2)}) copy-start(f32[4,32,16,256]{3,2,1,0:T(8,128)} %state.9) | copy-start | bytes 6291460
  1.6 7.4 %copy-start.6 = (f32[8]{0:T(128)S(1)}, f32[8]{0:T(128)}, u32[]{:S(2)}) copy-start(f32[8]{0:T(128)} %resistance.1) | copy-start | bytes 100
  1.6 7.4 %copy-start.7 = (f32[8]{0:T(128)S(1)}, f32[8]{0:T(128)}, u32[]{:S(2)}) copy-start(f32[8]{0:T(128)} %relax.1) | copy-start | bytes 100
  1.6 9.6 %copy-start.1 = (f32[4,32,16,256]{3,2,1,0:T(8,128)S(1)}, f32[4,32,16,256]{3,2,1,0:T(8,128)}, u32[]{:S(2)}) copy-start(f32[4,32,16,256]{3,2,1,0:T(8,128)} %state.9) | copy-start | bytes 6291460
  1.9 9.3 %collective-permute-start.2 = (f32[288,128]{1,0:T(8,128)S(1)}, f32[288,128]{1,0:T(8,128)S(1)}, u32[]{:S(2)}, u32[]{:S(2)}) collective-permute-start(f32[288,128]{1,0:T(8,128)S(1)} %get-tuple-element.12), channel_id=1, source_target_pairs={{0,4},{4,8},{8,12},{12,16},{16,20},{20,24},{24,28},{28,32},{32,36}... | collective-permute-start | bytes 442376 | tf_op jit(solution)/shard_map/ppermute | solution.py:429
  3.9 7.3 %collective-permute-start = (f32[136,256]{1,0:T(8,128)S(1)}, f32[136,256]{1,0:T(8,128)S(1)}, u32[]{:S(2)}, u32[]{:S(2)}) collective-permute-start(f32[136,256]{1,0:T(8,128)S(1)} %get-tuple-element.10), channel_id=1, source_target_pairs={{1,2},{2,1},{5,6},{6,5},{9,10},{10,9},{13,14},{14,13},{17,18},{18,... | collective-permute-start | bytes 417800 | tf_op jit(solution)/shard_map/ppermute | solution.py:425
  4.5 6.6 %collective-permute-start.1 = (f32[136,256]{1,0:T(8,128)S(1)}, f32[136,256]{1,0:T(8,128)S(1)}, u32[]{:S(2)}, u32[]{:S(2)}) collective-permute-start(f32[136,256]{1,0:T(8,128)S(1)} %get-tuple-element.11), channel_id=1, source_target_pairs={{0,1},{2,3},{1,0},{3,2},{4,5},{6,7},{5,4},{7,6},{8,9},{10,11},{9,8... | collective-permute-start | bytes 417800 | tf_op jit(solution)/shard_map/ppermute | solution.py:425
  9.0 0.8 %copy-start.3 = (s32[32,256]{1,0:T(8,128)S(1)}, s32[32,256]{1,0:T(8,128)}, u32[]{:S(2)}) copy-start(s32[32,256]{1,0:T(8,128)} %zone.1) | copy-start | bytes 98308
  9.7 0.8 %copy-start.4 = (f32[32,256]{1,0:T(8,128)S(1)}, f32[32,256]{1,0:T(8,128)}, u32[]{:S(2)}) copy-start(f32[32,256]{1,0:T(8,128)} %aux.1) | copy-start | bytes 98308
  14.1 30.4 %copy-start.5 = (s32[64]{0:T(128)S(1)}, s32[64]{0:T(128)}, u32[]{:S(2)}) copy-start(s32[64]{0:T(128)} %param.12) | copy-start | bytes 772
  14.1 30.4 %all-to-all-start = ((f32[64,18,1,128]{3,2,1,0:T(1,128)}), f32[64,18,1,128]{3,2,1,0:T(1,128)S(1)}, u32[]{:S(2)}, u32[]{:S(2)}) async-start(f32[64,18,1,128]{3,2,1,0:T(1,128)} %bitcast.1), calls=%async_computation | async-start | bytes 1179648 | tf_op jit(solution)/shard_map/all_to_all | solution.py:454
  25.3 15.2 %collective-permute-start.3 = (f32[72,256]{1,0:T(8,128)S(1)}, f32[72,256]{1,0:T(8,128)S(1)}, u32[]{:S(2)}, u32[]{:S(2)}) collective-permute-start(f32[72,256]{1,0:T(8,128)S(1)} %get-tuple-element.13), channel_id=1, source_target_pairs={{0,4},{4,8},{8,12},{12,16},{16,20},{20,24},{24,28},{28,32},{32,36}... | collective-permute-start | bytes 221192 | tf_op jit(solution)/shard_map/ppermute | solution.py:455
  26.8 14.6 %collective-permute-start.4 = (f32[72,256]{1,0:T(8,128)S(1)}, f32[72,256]{1,0:T(8,128)S(1)}, u32[]{:S(2)}, u32[]{:S(2)}) collective-permute-start(f32[72,256]{1,0:T(8,128)S(1)} %get-tuple-element.14), channel_id=1, source_target_pairs={{4,0},{8,4},{12,8},{16,12},{20,16},{24,20},{28,24},{32,28},{36,32}... | collective-permute-start | bytes 221192 | tf_op jit(solution)/shard_map/ppermute | solution.py:456
  44.5 1.1 %copy-start.2 = (bf16[2,2,128,640]{3,2,1,0:T(8,128)(2,1)S(1)}, bf16[2,2,128,640]{3,2,1,0:T(8,128)(2,1)}, u32[]{:S(2)}) copy-start(bf16[2,2,128,640]{3,2,1,0:T(8,128)(2,1)} %constant.2.clone.table) | copy-start | bytes 1966084
  47.8 24.8 %all-to-all-start.1 = ((f32[64,16,128]{2,1,0:T(8,128)}), f32[64,16,128]{2,1,0:T(8,128)S(1)}, u32[]{:S(2)}, u32[]{:S(2)}) async-start(f32[64,16,128]{2,1,0:T(8,128)} %bitcast.3), calls=%async_computation.1 | async-start | bytes 1048576 | tf_op jit(solution)/shard_map/all_to_all | solution.py:475

commit v7 on v6

--- a/solution.py
+++ b/solution.py
@@ -111,11 +111,10 @@
 
 
 HT_ROWS = 136
-AZ_ROWS = 72
-AZ_AHEAD = 288
-
-
-def pack_kernel(state, to_right, ht_then, ht_first, up, down):
+AZ_ROWS = 64
+
+
+def pack_kernel(state, to_right, to_left, ht_then, ht_first, up, down):
     inv_r, half_arc = radial_rates(NR)
     zero = jnp.zeros((1, NR), jnp.float32)
     for out, edge, inside, sign in ((up, HTS - 1, HTS - 2, 1.0), (down, 0, 1, -1.0)):
@@ -133,9 +132,8 @@
     ht_first[...] = jnp.where(odd, down[...], up[...])
     ht_then[...] = jnp.where(odd, up[...], down[...])
 
-    no_row = jnp.zeros((1, 128), jnp.float32)
-    edge_message(to_right, state, ROWS - 1, ROWS - 2, 1.0, no_row, no_row)
-    to_right[64:AZ_AHEAD] = jnp.zeros((AZ_AHEAD - 64, 128), jnp.float32)
+    edge_message(to_right, state, ROWS - 1, ROWS - 2, 1.0, zero, zero)
+    edge_message(to_left, state, 0, 1, -1.0, zero, zero)
 
 
 def edge_message(out, state, j, inside, sign, w_low, w_high):
@@ -163,21 +161,14 @@
     ahead[...] = jnp.where(odd, then[...], first[...])
 
 
-def two_stages(width, state, low, high, left, right, ground, mid, ghost):
+def two_stages(width, state, low, high, left, ground, mid, ghost):
     on_ground, on_top = lowest_slab(), highest_slab()
     inv_r, half_arc = radial_rates(width)
     cols = slice(0, width)
     turn = DT * half_arc
 
     def beyond(a, b):
-        return jnp.zeros((b - a, width), jnp.float32) if right is None else right[a:b, cols]
-
-    def corners(k):
-        if right is None:
-            return 0.0
-        sub = lax.broadcasted_iota(jnp.int32, (ROWS, width), 0)
-        last = jnp.where(sub == ROWS - 1, -right[k : k + 1, cols], 0.0)
-        return turn * jnp.where(sub == 0, left[k : k + 1, cols], last)
+        return jnp.zeros((b - a, width), jnp.float32)
 
     p0, p1, u0, v0, w0, w1 = [plane(state, i, k, width) for i, k in ((0, 0), (0, 1), (1, 0), (2, 0), (3, 0), (3, 1))]
     p15, w15 = plane(state, 0, HTS - 1, width), plane(state, 3, HTS - 1, width)
@@ -185,9 +176,9 @@
     bw = jnp.where(on_ground, ground[0, :, cols], low[32:64, cols])
     ghost[0], ghost[1], ghost[2], ghost[3] = bp, bw, high[0:32, cols], high[32:64, cols]
 
-    top_p = high[64:96, cols] + (0.5 * DT) * w15 + corners(65)
+    top_p = high[64:96, cols] + (0.5 * DT) * w15
     top_w = high[96:128, cols] + (0.5 * DT) * p15
-    low_p = low[64:96, cols] - (0.5 * DT) * w0 + corners(64)
+    low_p = low[64:96, cols] - (0.5 * DT) * w0
     low_w = low[96:128, cols] - (0.5 * DT) * p0
     v_diff = 2.0 * row_diff(v0, left[16:17, cols], beyond(16, 17)) * half_arc
     mid_p0 = p0 - DT * (radial_diff(u0) + u0 * inv_r + v_diff + 0.5 * (w1 - bw))
@@ -240,11 +231,17 @@
     return (0.5 * DT) * (0.5 * DT) * radial_rates(width)[1]
 
 
-def inner_kernel(state, left, ht_then, ht_first, ground, packed, low, high, mid, ghost):
+def corner_weight(width):
+    return (0.5 * DT) * (0.5 * DT) * radial_rates(width)[1]
+
+
+def inner_kernel(
+    state, left, ht_then, ht_first, ground, packed, left_corner, right_corner, low, high, mid, ghost
+):
     unswap(odd_slab(), ht_first, ht_then, low, high)
     near = lax.broadcasted_iota(jnp.int32, (HTS, 128), 1) < NI
     height = lax.broadcasted_iota(jnp.int32, (HTS, 128), 0)
-    second = two_stages(128, state, low, high, left, None, ground, mid, ghost)
+    second = two_stages(128, state, low, high, left, ground, mid, ghost)
     on_ground = lowest_slab()
 
     def emit(r, one, two):
@@ -260,7 +257,7 @@
     none = jnp.zeros((HTS, 128), jnp.float32)
 
     p0, v0 = state[0, 0, :, 0:128], state[2, 0, :, 0:128]
-    own_p, own_v = mid[0, 1] - turn * left[16:32], mid[2, 1] - turn * left[0:16]
+    own_p, own_v = mid[0, 1] - turn * left[16:32, 0:128], mid[2, 1] - turn * left[0:16, 0:128]
     far_p = -turn * v0
     far_low = jnp.where(on_ground, far_p[0:1], -turn * low[128:129, 0:128])
     far_high = -turn * high[128:129, 0:128]
@@ -272,7 +269,7 @@
     ]
     before = [0.5 * turn * turn * p0, none, 0.5 * turn * turn * v0, none]
 
-    weight = 0.5 * DT * turn * 0.5
+    weight = corner_weight(128)
 
     end = ROWS - 1
     at_ground = jnp.logical_and(on_ground, height == 0)
@@ -287,24 +284,18 @@
     emit(HALF, second(HALF - 2), owed)
     emit(HALF + 1, second(HALF - 1), [factor] + [none] * 3)
 
+    for out, j, corner in ((left_corner, 0, 128), (right_corner, end, 129)):
+        rows = [w_below(low, ground, j), high[32 + j : 33 + j], low[corner : corner + 1], high[corner : corner + 1]]
+        out[...] = jnp.concatenate(rows + [jnp.zeros((4, NR), jnp.float32)], 0)
+
 
 def w_below(low, ground, j):
     return jnp.where(lowest_slab(), ground[0, j : j + 1], low[32 + j : 33 + j])
 
 
-def edge_kernel(state, ht_then, ht_first, ground, after, to_left, to_right, low, high):
+def outer_kernel(state, ht_then, ht_first, left, ground, stepped, low, high, mid, ghost):
     unswap(odd_slab(), ht_first, ht_then, low, high)
-    end = ROWS - 1
-    for out, j, inside, sign, corner in ((to_right, end, end - 1, 1.0, 129), (to_left, 0, 1, -1.0, 128)):
-        edge_message(out, state, j, inside, sign, w_below(low, ground, j), high[32 + j : 33 + j])
-        out[64:65] = low[corner : corner + 1]
-        out[65:66] = high[corner : corner + 1]
-        out[66:AZ_ROWS] = jnp.zeros((AZ_ROWS - 66, NR), jnp.float32)
-
-
-def outer_kernel(state, ht_then, ht_first, left, right, ground, stepped, low, high, mid, ghost):
-    unswap(odd_slab(), ht_first, ht_then, low, high)
-    second = two_stages(NR, state, low, high, left, right, ground, mid, ghost)
+    second = two_stages(NR, state, low, high, left, ground, mid, ghost)
 
     @pl.loop(0, ROWS, unroll=2)
     def _(j):
@@ -328,7 +319,7 @@
             circle[row(k, r), :] = jnp.where(near, circle[row(k, r), :], 0.0)
 
 
-def filter_kernel(table, cutoff, x_ref, left, right, o_ref, circle):
+def filter_kernel(table, cutoff, x_ref, o_ref, circle):
     m = SECTORS // 2 * LONG
     circle[...] = x_ref[...]
 
@@ -369,18 +360,63 @@
         )
 
 
-def merge_kernel(stepped, back, out, rows, tile, beside, sems):
+def edge_terms(right, left_corner, right_corner, ground):
+    height = lax.broadcasted_iota(jnp.int32, (HTS, NR), 0)
+    half_arc = radial_rates(NR)[1]
+    turn, weight = DT * half_arc, corner_weight(NR)
+    on_ground = lowest_slab()
+    end = ROWS - 1
+    p, v, mid_p, mid_v = [right[16 * i : 16 * i + 16] for i in range(4)]
+    far_p = -turn * v
+    wall = (0.25 * DT) * ground[1, end : end + 1] * far_p
+    far_low = jnp.where(on_ground, far_p[0:1], 0.0)
+    terms = {
+        (0, end): 0.5 * (far_p - turn * mid_v) + jnp.where(jnp.logical_and(on_ground, height == 0), wall, 0.0),
+        (1, end): (-0.5 * DT) * radial_diff(far_p),
+        (2, end): (-0.5 * turn) * (p + mid_p),
+        (3, end): (-0.5 * DT) * row_diff(far_p, far_low, jnp.zeros((1, NR), jnp.float32)),
+        (0, end - 1): 0.5 * turn * turn * p,
+        (2, end - 1): 0.5 * turn * turn * v,
+        (2, 0): 0.0,
+        (3, 0): 0.0,
+    }
+    for i, j in ((2, 0), (2, end), (3, 0), (3, end)):
+        corner, sign = (left_corner, -1.0) if j == 0 else (right_corner, 1.0)
+        at = 2 * (i - 2)
+        below, above = (-sign * weight) * corner[at : at + 1], (sign * weight) * corner[at + 1 : at + 2]
+        corner_term = jnp.where(height == HTS - 1, above, jnp.where(height == 0, below, 0.0))
+        terms[i, j] = terms[i, j] + corner_term
+    return terms
+
+
+EDGE_PLACES = 8
+
+
+def merge_kernel(
+    stepped, back, right, left_corner, right_corner, ground, out, rows, tile, beside, edges, sems, edge_sems
+):
     near = lax.broadcasted_iota(jnp.int32, (HTS, 128), 1) < NI
     loads = [
         pltpu.make_async_copy(stepped.at[i, :, :, pl.ds(0, 128)], beside.at[i], sems.at[0, i]) for i in range(COMPS)
     ]
     for copy in loads:
         copy.start()
+    owed = edge_terms(right, left_corner, right_corner, ground)
+    places = [(k, i, j) for k, (i, j) in enumerate(owed)]
+    edge_loads = [
+        pltpu.make_async_copy(stepped.at[i, j, :, pl.ds(128, 128)], edges.at[k], edge_sems.at[0, k]) for k, i, j in places
+    ]
+    for copy in edge_loads:
+        copy.start()
+
     for i in range(COMPS * HTS):
         rows[pl.ds(i // HTS * HTS * HALF + i % HTS, HALF, stride=HTS), :] = back[i * HALF : (i + 1) * HALF]
     stores = []
     for i in range(COMPS):
         loads[i].wait()
+        for k, comp, j in places:
+            if comp == i:
+                beside[i, j] = beside[i, j] + owed[i, j][:, 0:128]
         for l in range(HALF):
             at = (i * HALF + l) * HTS
             both = rows[at : at + HTS]
@@ -388,6 +424,11 @@
             tile[i, l + HALF] = jnp.where(near, pltpu.roll(both, NI, 1), beside[i, l + HALF])
         stores.append(pltpu.make_async_copy(tile.at[i], out.at[i, :, :, pl.ds(0, 128)], sems.at[1, i]))
         stores[i].start()
+    for k, i, j in places:
+        edge_loads[k].wait()
+        edges[k] = edges[k] + owed[i, j][:, 128:NR]
+        stores.append(pltpu.make_async_copy(edges.at[k], out.at[i, j, :, pl.ds(128, 128)], edge_sems.at[1, k]))
+        stores[-1].start()
     for copy in stores:
         copy.wait()
 
@@ -405,11 +446,11 @@
         return tuple(jax.ShapeDtypeStruct(d, f32) for d in dims)
 
     ht_message, az_message = (HT_ROWS, NR), (AZ_ROWS, NR)
-    to_right, ht_then, ht_first = call(
+    to_right, to_left, ht_then, ht_first = call(
         pack_kernel,
-        out_shape=shapes((AZ_AHEAD, 128), ht_message, ht_message),
+        out_shape=shapes(az_message, az_message, ht_message, ht_message),
         in_specs=[vmem],
-        out_specs=(vmem,) * 3,
+        out_specs=(vmem,) * 4,
         scratch_shapes=[pltpu.VMEM(ht_message, f32)] * 2,
         name="pack",
     )(state)
@@ -426,67 +467,60 @@
 
     rightward = [(i, (i + 1) % SECTORS) for i in range(SECTORS)]
     leftward = [(b, a) for a, b in rightward]
-    ahead = lax.ppermute(to_right, AZ, rightward)
+    left, right = lax.ppermute(to_right, AZ, rightward), lax.ppermute(to_left, AZ, leftward)
     ht_then, ht_first = swap(ht_then, 1), swap(ht_first, 0)
 
     def scratch(width):
         return [pltpu.VMEM((COMPS, ROWS + 2, HTS, width), f32), pltpu.VMEM((8, ROWS, width), f32)]
 
     halos = [pltpu.VMEM(ht_message, f32)] * 2
-    packed = call(
+    packed, to_left, to_right = call(
         inner_kernel,
         mib=12,
-        out_shape=shapes((COMPS * HTS * LONG, 128))[0],
+        out_shape=shapes((COMPS * HTS * LONG, 128), (8, NR), (8, NR)),
         in_specs=[vmem] * 5,
-        out_specs=vmem,
+        out_specs=(vmem,) * 3,
         scratch_shapes=halos + scratch(128),
         cost_estimate=pl.CostEstimate(flops=10**7, bytes_accessed=6 * 10**6, transcendentals=0),
         name="inner",
-    )(state, ahead, ht_then, ht_first, ground)
-    to_left, to_right = call(
-        edge_kernel,
-        out_shape=shapes(az_message, az_message),
-        in_specs=[vmem] * 4 + [anywhere],
-        out_specs=(vmem,) * 2,
-        scratch_shapes=halos,
-        name="edge",
-    )(state, ht_then, ht_first, ground, packed)
+    )(state, left, ht_then, ht_first, ground)
     circle = lax.all_to_all(packed.reshape(SECTORS, LONG, 1, 128), SPREAD, 0, 0, tiled=True)
-    left = lax.ppermute(to_right, AZ, rightward)
-    right = lax.ppermute(to_left, AZ, leftward)
+    left_corner, right_corner = lax.ppermute(to_right, AZ, rightward), lax.ppermute(to_left, AZ, leftward)
     stepped = call(
         outer_kernel,
         mib=16,
         out_shape=shapes((COMPS, ROWS, HTS, NR))[0],
-        in_specs=[vmem] * 6,
+        in_specs=[vmem] * 5,
         out_specs=vmem,
         scratch_shapes=halos + scratch(NR),
         cost_estimate=pl.CostEstimate(flops=2 * 10**7, bytes_accessed=2 * 10**7, transcendentals=0),
         name="outer",
-    )(state, ht_then, ht_first, left, right, ground)
+    )(state, ht_then, ht_first, left, ground)
     kept = call(
         filter_kernel,
         out_shape=shapes((NA // 2, 128))[0],
-        in_specs=[vmem] * 3 + [anywhere] * 2,
+        in_specs=[vmem] * 3,
         out_specs=vmem,
         scratch_shapes=[pltpu.VMEM((SECTORS * LONG, 128), f32)],
         name="filter",
-    )(jnp.asarray(mode_tables()), cutoff.reshape(1, NI), circle.reshape(SECTORS * LONG, 128), left, right)
+    )(jnp.asarray(mode_tables()), cutoff.reshape(1, NI), circle.reshape(SECTORS * LONG, 128))
     back = lax.all_to_all(kept.reshape(SECTORS, HALF, 128), SPREAD, 0, 0, tiled=True)
     return call(
         merge_kernel,
         out_shape=jax.ShapeDtypeStruct(stepped.shape, f32),
-        in_specs=[anywhere, vmem],
+        in_specs=[anywhere] + [vmem] * 5,
         out_specs=anywhere,
         scratch_shapes=[
             pltpu.VMEM((COMPS * HTS * HALF, 128), f32),
             pltpu.VMEM((COMPS, ROWS, HTS, 128), f32),
             pltpu.VMEM((COMPS, ROWS, HTS, 128), f32),
+            pltpu.VMEM((EDGE_PLACES, HTS, 128), f32),
             pltpu.SemaphoreType.DMA((2, COMPS)),
+            pltpu.SemaphoreType.DMA((2, EDGE_PLACES)),
         ],
         input_output_aliases={0: 0},
         name="merge",
-    )(stepped, back.reshape(COMPS * HTS * HALF, 128))
+    )(stepped, back.reshape(COMPS * HTS * HALF, 128), right, left_corner, right_corner, ground)
 
 
 def solution(mesh):

time: 75.5 us -> 72.4 us (0.959)
  blocking collectives: 0 us -> 30.1 us
  waiting for transfers between devices: 29.8 us -> 5.44 us
  starting transfers between devices: 28.1 us -> 20.7 us
  local copies, waits for them, and re-layouts: 4.21 us -> 3.13 us
    all_to_all x0 -> x1, blocking collectives: none -> 30.1 us  [per_device(): lax.all_to_all(packed.reshape(SECTORS, LONG, 1, 128), SPREAD, 0, 0, tiled...]
    ppermute x3 -> x4, waiting for transfers between devices: 14.1 us -> 1.89 us  [the longest x2 1.7 us: per_device(): lax.ppermute(to_left, AZ, leftward)]
    all_to_all x1 -> x0, starting transfers between devices: 11 us -> none  [per_device(): lax.all_to_all(packed.reshape(SECTORS, LONG, 1, 128), SPREAD, 0, 0, tiled...]
    all_to_all x1, waiting for transfers between devices: 12.7 us -> 3.55 us  [per_device(): lax.all_to_all(kept.reshape(SECTORS, HALF, 128), SPREAD, 0, 0, tiled=True)]
    ppermute x3 -> x4, starting transfers between devices: 4.1 us -> 8.55 us  [the longest x2 5.07 us: per_device(): lax.ppermute(to_left, AZ, leftward)]
    all_to_all x1 -> x0, waiting for transfers between devices: 3.05 us -> none  [per_device(): lax.all_to_all(packed.reshape(SECTORS, LONG, 1, 128), SPREAD, 0, 0, tiled...]
    unnamed x16, local copies, waits for them, and re-layouts: 4.21 us -> 3.13 us
    all_to_all x1, starting transfers between devices: 7.85 us -> 6.89 us  [per_device(): lax.all_to_all(kept.reshape(SECTORS, HALF, 128), SPREAD, 0, 0, tiled=True)]
where the time goes in v7:
time: 72.4 us; the launch traced here: 71.3 us
  blocking collectives  30.1 us (42%)
  starting transfers between devices  20.7 us (29%)
  Pallas kernels  11.9 us (16%)
  waiting for transfers between devices  5.44 us (8%)
  local copies, waits for them, and re-layouts  3.13 us (4%)
    all_to_all x1, blocking collectives, per_device(): lax.all_to_all(packed.reshape(SECTORS, LONG, 1, 128), SPREAD, 0, 0, tiled...  30.1 us
    all_to_all x1, starting transfers between devices, per_device(): lax.all_to_all(kept.reshape(SECTORS, HALF, 128), SPREAD, 0, 0, tiled=True)  6.89 us
    ppermute x2, starting transfers between devices, swap(): return lax.ppermute(x, HT, pairs + [(b, a) for a, b in pairs])  5.27 us
    ppermute x2, starting transfers between devices, per_device(): lax.ppermute(to_left, AZ, leftward)  5.07 us
    pallas_call x1, Pallas kernels, per_device(): call(outer_kernel, mib=16, out_shape=shapes((COMPS, ROWS, HTS, NR))[0], i...  4.3 us
    all_to_all x1, waiting for transfers between devices, per_device(): lax.all_to_all(kept.reshape(SECTORS, HALF, 128), SPREAD, 0, 0, tiled=True)  3.55 us
    ppermute x2, starting transfers between devices, per_device(): lax.ppermute(to_right, AZ, rightward)  3.49 us
    unnamed x16, local copies, waits for them, and re-layouts  3.13 us
  transfers between devices with their start and end apart: 7, of which 4 were waited for; matrix products, arithmetic and copies ran while one was open for 0% of the time, Pallas kernels for 7%

profile of v7, /device:TPU:32, one launch (start us, length us, event | category | flops | bytes accessed | tf_op | source)
XLA Modules:
  0.0 71.3 jit_solution(16096785539359072182)
XLA Ops:
  0.0 1.6 %copy-done = f32[4,32,16,256]{3,2,1,0:T(8,128)S(1)} copy-done((f32[4,32,16,256]{3,2,1,0:T(8,128)S(1)}, f32[4,32,16,256]{3,2,1,0:T(8,128)}, u32[]{:S(2)}) %copy-start) | copy-done | bytes 2097176
  1.6 0.3 pack.1
  1.9 0.8 %collective-permute-start = (f32[136,256]{1,0:T(8,128)S(1)}, f32[136,256]{1,0:T(8,128)S(1)}, u32[]{:S(2)}, u32[]{:S(2)}) collective-permute-start(f32[136,256]{1,0:T(8,128)S(1)} %get-tuple-element.12), channel_id=1, source_target_pairs={{1,2},{2,1},{5,6},{6,5},{9,10},{10,9},{13,14},{14,13},{17,18},{18,... | collective-permute-start | bytes 417800 | tf_op jit(solution)/shard_map/ppermute | solution.py:466
  2.7 4.5 %collective-permute-start.1 = (f32[136,256]{1,0:T(8,128)S(1)}, f32[136,256]{1,0:T(8,128)S(1)}, u32[]{:S(2)}, u32[]{:S(2)}) collective-permute-start(f32[136,256]{1,0:T(8,128)S(1)} %get-tuple-element.13), channel_id=1, source_target_pairs={{0,1},{2,3},{1,0},{3,2},{4,5},{6,7},{5,4},{7,6},{8,9},{10,11},{9,8... | collective-permute-start | bytes 417800 | tf_op jit(solution)/shard_map/ppermute | solution.py:466
  7.1 1.9 %collective-permute-start.2 = (f32[64,256]{1,0:T(8,128)S(1)}, f32[64,256]{1,0:T(8,128)S(1)}, u32[]{:S(2)}, u32[]{:S(2)}) collective-permute-start(f32[64,256]{1,0:T(8,128)S(1)} %get-tuple-element.14), channel_id=1, source_target_pairs={{0,4},{4,8},{8,12},{12,16},{16,20},{20,24},{24,28},{28,32},{32,36}... | collective-permute-start | bytes 196616 | tf_op jit(solution)/shard_map/ppermute | solution.py:470
  9.1 0.8 %copy-done.3 = s32[32,256]{1,0:T(8,128)S(1)} copy-done((s32[32,256]{1,0:T(8,128)S(1)}, s32[32,256]{1,0:T(8,128)}, u32[]{:S(2)}) %copy-start.3) | copy-done | bytes 32792
  9.8 0.8 %copy-done.4 = f32[32,256]{1,0:T(8,128)S(1)} copy-done((f32[32,256]{1,0:T(8,128)S(1)}, f32[32,256]{1,0:T(8,128)}, u32[]{:S(2)}) %copy-start.4) | copy-done | bytes 32792
  10.6 0.6 ground.1
  11.2 0.0 copy-start.2
  11.2 0.0 copy-start.7
  11.2 0.2 collective-permute-done.2.left
  11.4 2.1 %inner.1 = (f32[1152,128]{1,0:T(8,128)S(1)}, f32[8,256]{1,0:T(8,128)S(1)}, f32[8,256]{1,0:T(8,128)S(1)}) custom-call(f32[4,32,16,256]{3,2,1,0:T(8,128)S(1)} %copy-done.1, f32[64,256]{1,0:T(8,128)S(1)} %collective-permute-done.2.left, f32[136,256]{1,0:T(8,128)S(1)} %collective-permute-done.ht_then, f32[136,256]{1,0:T(8,128)S(1)} %collective-permute-done.1.ht_first, ...), custom_call_target="tpu_custom_call" | custom-call | flops 10000000 | bytes 6000000 | tf_op jit(solution)/shard_map/inner/pallas_call | solution.py:477
  13.6 30.1 %all_to_all.10 = f32[64,18,1,128]{3,2,1,0:T(1,128)S(1)} all-to-all(f32[64,18,1,128]{3,2,1,0:T(1,128)S(1)} %bitcast.7), channel_id=1, replica_groups=mesh['y'=4,'x'=2,'z'=8,'hx'=2,'core'=2] {'y','z','x'}, dimensions={0} | all-to-all | bytes 1179648 | tf_op jit(solution)/shard_map/all_to_all | solution.py:487
  43.6 2.2 %filter.1 = f32[1024,128]{1,0:T(8,128)} custom-call(bf16[2,2,128,640]{3,2,1,0:T(8,128)(2,1)S(1)} %copy-done.2, s32[1,64]{1,0:T(1,128)S(1)} %bitcast.8, f32[1152,128]{1,0:T(8,128)S(1)} %bitcast.5), custom_call_target="tpu_custom_call" | custom-call | tf_op jit(solution)/shard_map/filter/pallas_call | solution.py:499
  45.8 6.9 %all-to-all-start.1 = ((f32[64,16,128]{2,1,0:T(8,128)}), f32[64,16,128]{2,1,0:T(8,128)S(1)}, u32[]{:S(2)}, u32[]{:S(2)}) async-start(f32[64,16,128]{2,1,0:T(8,128)} %bitcast.3), calls=%async_computation.1 | async-start | bytes 1048576 | tf_op jit(solution)/shard_map/all_to_all | solution.py:507
  52.7 0.5 collective-permute-start.3
  53.3 1.6 %collective-permute-start.4 = (f32[8,256]{1,0:T(8,128)S(1)}, f32[8,256]{1,0:T(8,128)S(1)}, u32[]{:S(2)}, u32[]{:S(2)}) collective-permute-start(f32[8,256]{1,0:T(8,128)S(1)} %get-tuple-element.17), channel_id=1, source_target_pairs={{0,4},{4,8},{8,12},{12,16},{16,20},{20,24},{24,28},{28,32},{32,36}... | collective-permute-start | bytes 24584 | tf_op jit(solution)/shard_map/ppermute | solution.py:488
  54.8 4.5 %collective-permute-start.5 = (f32[8,256]{1,0:T(8,128)S(1)}, f32[8,256]{1,0:T(8,128)S(1)}, u32[]{:S(2)}, u32[]{:S(2)}) collective-permute-start(f32[8,256]{1,0:T(8,128)S(1)} %get-tuple-element.18), channel_id=1, source_target_pairs={{4,0},{8,4},{12,8},{16,12},{20,16},{24,20},{28,24},{32,28},{36,32}... | collective-permute-start | bytes 24584 | tf_op jit(solution)/shard_map/ppermute | solution.py:488
  59.4 4.3 %outer.1.stepped = f32[4,32,16,256]{3,2,1,0:T(8,128)} custom-call(f32[4,32,16,256]{3,2,1,0:T(8,128)S(1)} %copy-done.1, f32[136,256]{1,0:T(8,128)S(1)} %collective-permute-done.ht_then, f32[136,256]{1,0:T(8,128)S(1)} %collective-permute-done.1.ht_first, f32[64,256]{1,0:T(8,128)S(1)} %collective-permute-done.2.left, f32[3,32,256]{2,1,0:T(8,128)S(1)} %ground.1), custom_call_target="tpu_custom_call" | custom-call | flops 20000000 | bytes 20000000 | tf_op jit(solution)/shard_map/outer/pallas_call | solution.py:489
  63.7 1.6 %collective-permute-done.3.right = f32[64,256]{1,0:T(8,128)S(1)} collective-permute-done((f32[64,256]{1,0:T(8,128)S(1)}, f32[64,256]{1,0:T(8,128)S(1)}, u32[]{:S(2)}, u32[]{:S(2)}) %collective-permute-start.3) | collective-permute-done | bytes 65568 | tf_op jit(solution)/shard_map/ppermute | solution.py:470
  65.3 0.0 collective-permute-done.4.left_corner
  65.3 0.1 collective-permute-done.5.right_corner
  65.4 3.5 %all-to-all-done.1 = f32[64,16,128]{2,1,0:T(8,128)S(1)} async-done(((f32[64,16,128]{2,1,0:T(8,128)}), f32[64,16,128]{2,1,0:T(8,128)S(1)}, u32[]{:S(2)}, u32[]{:S(2)}) %all-to-all-start.1) | async-done | bytes 524320 | tf_op jit(solution)/shard_map/all_to_all | solution.py:507
  68.9 2.4 %merge.1 = f32[4,32,16,256]{3,2,1,0:T(8,128)} custom-call(f32[4,32,16,256]{3,2,1,0:T(8,128)} %outer.1.stepped, f32[1024,128]{1,0:T(8,128)S(1)} %bitcast.6, f32[64,256]{1,0:T(8,128)S(1)} %collective-permute-done.3.right, f32[8,256]{1,0:T(8,128)S(1)} %collective-permute-done.4.left_corner, ...), custom_call_target="tpu_custom_call", output_to_operand_aliasing={{}: (0, {})} | custom-call | tf_op jit(solution)/shard_map/merge/pallas_call | solution.py:508
  (13 shorter events, 0.0 us)
Async XLA Ops:
  0.0 1.6 %copy-start = (f32[4,32,16,256]{3,2,1,0:T(8,128)S(1)}, f32[4,32,16,256]{3,2,1,0:T(8,128)}, u32[]{:S(2)}) copy-start(f32[4,32,16,256]{3,2,1,0:T(8,128)} %state.7) | copy-start | bytes 6291460
  1.6 7.5 %copy-start.5 = (f32[8]{0:T(128)S(1)}, f32[8]{0:T(128)}, u32[]{:S(2)}) copy-start(f32[8]{0:T(128)} %resistance.1) | copy-start | bytes 100
  1.6 7.5 %copy-start.6 = (f32[8]{0:T(128)S(1)}, f32[8]{0:T(128)}, u32[]{:S(2)}) copy-start(f32[8]{0:T(128)} %relax.1) | copy-start | bytes 100
  1.6 9.8 %copy-start.1 = (f32[4,32,16,256]{3,2,1,0:T(8,128)S(1)}, f32[4,32,16,256]{3,2,1,0:T(8,128)}, u32[]{:S(2)}) copy-start(f32[4,32,16,256]{3,2,1,0:T(8,128)} %state.7) | copy-start | bytes 6291460
  1.9 9.5 %collective-permute-start = (f32[136,256]{1,0:T(8,128)S(1)}, f32[136,256]{1,0:T(8,128)S(1)}, u32[]{:S(2)}, u32[]{:S(2)}) collective-permute-start(f32[136,256]{1,0:T(8,128)S(1)} %get-tuple-element.12), channel_id=1, source_target_pairs={{1,2},{2,1},{5,6},{6,5},{9,10},{10,9},{13,14},{14,13},{17,18},{18,... | collective-permute-start | bytes 417800 | tf_op jit(solution)/shard_map/ppermute | solution.py:466
  2.7 8.7 %collective-permute-start.1 = (f32[136,256]{1,0:T(8,128)S(1)}, f32[136,256]{1,0:T(8,128)S(1)}, u32[]{:S(2)}, u32[]{:S(2)}) collective-permute-start(f32[136,256]{1,0:T(8,128)S(1)} %get-tuple-element.13), channel_id=1, source_target_pairs={{0,1},{2,3},{1,0},{3,2},{4,5},{6,7},{5,4},{7,6},{8,9},{10,11},{9,8... | collective-permute-start | bytes 417800 | tf_op jit(solution)/shard_map/ppermute | solution.py:466
  7.1 4.3 %collective-permute-start.2 = (f32[64,256]{1,0:T(8,128)S(1)}, f32[64,256]{1,0:T(8,128)S(1)}, u32[]{:S(2)}, u32[]{:S(2)}) collective-permute-start(f32[64,256]{1,0:T(8,128)S(1)} %get-tuple-element.14), channel_id=1, source_target_pairs={{0,4},{4,8},{8,12},{12,16},{16,20},{20,24},{24,28},{28,32},{32,36}... | collective-permute-start | bytes 196616 | tf_op jit(solution)/shard_map/ppermute | solution.py:470
  9.1 0.8 %copy-start.3 = (s32[32,256]{1,0:T(8,128)S(1)}, s32[32,256]{1,0:T(8,128)}, u32[]{:S(2)}) copy-start(s32[32,256]{1,0:T(8,128)} %zone.1) | copy-start | bytes 98308
  9.8 0.8 %copy-start.4 = (f32[32,256]{1,0:T(8,128)S(1)}, f32[32,256]{1,0:T(8,128)}, u32[]{:S(2)}) copy-start(f32[32,256]{1,0:T(8,128)} %aux.1) | copy-start | bytes 98308
  11.2 32.4 %copy-start.2 = (bf16[2,2,128,640]{3,2,1,0:T(8,128)(2,1)S(1)}, bf16[2,2,128,640]{3,2,1,0:T(8,128)(2,1)}, u32[]{:S(2)}) copy-start(bf16[2,2,128,640]{3,2,1,0:T(8,128)(2,1)} %constant.2.clone.table) | copy-start | bytes 1966084
  11.2 32.4 %copy-start.7 = (s32[64]{0:T(128)S(1)}, s32[64]{0:T(128)}, u32[]{:S(2)}) copy-start(s32[64]{0:T(128)} %param.12) | copy-start | bytes 772
  45.8 23.1 %all-to-all-start.1 = ((f32[64,16,128]{2,1,0:T(8,128)}), f32[64,16,128]{2,1,0:T(8,128)S(1)}, u32[]{:S(2)}, u32[]{:S(2)}) async-start(f32[64,16,128]{2,1,0:T(8,128)} %bitcast.3), calls=%async_computation.1 | async-start | bytes 1048576 | tf_op jit(solution)/shard_map/all_to_all | solution.py:507
  52.7 12.5 %collective-permute-start.3 = (f32[64,256]{1,0:T(8,128)S(1)}, f32[64,256]{1,0:T(8,128)S(1)}, u32[]{:S(2)}, u32[]{:S(2)}) collective-permute-start(f32[64,256]{1,0:T(8,128)S(1)} %get-tuple-element.16), channel_id=1, source_target_pairs={{4,0},{8,4},{12,8},{16,12},{20,16},{24,20},{28,24},{32,28},{36,32}... | collective-permute-start | bytes 196616 | tf_op jit(solution)/shard_map/ppermute | solution.py:470
  53.3 12.0 %collective-permute-start.4 = (f32[8,256]{1,0:T(8,128)S(1)}, f32[8,256]{1,0:T(8,128)S(1)}, u32[]{:S(2)}, u32[]{:S(2)}) collective-permute-start(f32[8,256]{1,0:T(8,128)S(1)} %get-tuple-element.17), channel_id=1, source_target_pairs={{0,4},{4,8},{8,12},{12,16},{16,20},{20,24},{24,28},{28,32},{32,36}... | collective-permute-start | bytes 24584 | tf_op jit(solution)/shard_map/ppermute | solution.py:488
  54.8 10.5 %collective-permute-start.5 = (f32[8,256]{1,0:T(8,128)S(1)}, f32[8,256]{1,0:T(8,128)S(1)}, u32[]{:S(2)}, u32[]{:S(2)}) collective-permute-start(f32[8,256]{1,0:T(8,128)S(1)} %get-tuple-element.18), channel_id=1, source_target_pairs={{4,0},{8,4},{12,8},{16,12},{20,16},{24,20},{28,24},{32,28},{36,32}... | collective-permute-start | bytes 24584 | tf_op jit(solution)/shard_map/ppermute | solution.py:488

commit v8 on v7

--- a/solution.py
+++ b/solution.py
@@ -17,39 +17,39 @@
 ROWS = NA // SECTORS
 HALF = ROWS // 2
 LONG = HALF + 2
-TURN_AT = SECTORS // 2 * LONG
 HTS = 16
 NR = 256
 COMPS = 4
 DT = 0.4
 
 AZ = ("y", "x", "z")
-SPREAD = ("y", "z", "x")
+SPREAD = ("z", "y")
+PEERS = 32
+SETS = COMPS * HTS // PEERS
 HT = ("hx", "core")
 
 
-def sector_of_chunk():
-    y, z, x = np.meshgrid(np.arange(4), np.arange(8), np.arange(2), indexing="ij")
-    return ((y * 2 + x) * 8 + z).reshape(-1)
-
-
 def mode_tables():
-    first = sector_of_chunk()[: SECTORS // 2, None] * ROWS
-    azimuth = (first - 2 + np.arange(LONG)[None, :]).reshape(-1)
-    out = np.zeros((2, 2, MODES, TURN_AT + 64), jnp.bfloat16)
+    z, y = np.meshgrid(np.arange(8), np.arange(2), indexing="ij")
+    first = (y * 16 + z).reshape(-1, 1) * ROWS
+    there = (first - 2 + np.arange(LONG)[None, :]).reshape(-1)
+    back = (first + np.arange(HALF)[None, :]).reshape(-1)
+    tables, turns = [], np.zeros((2, 2, MODES // 2, 128), np.float32)
     for parity in range(2):
         modes = np.arange(parity, MODES, 2)
-        phase = (modes[:, None] * azimuth[None, :] % NA) * (2.0 * math.pi / NA)
-        out[0, parity, :, :TURN_AT], out[1, parity, :, :TURN_AT] = split(np.concatenate([np.cos(phase), np.sin(phase)], 0))
-        turn = (modes * LONG % NA) * (2.0 * math.pi / NA)
-        for k, value in enumerate((np.cos(turn), np.sin(turn))):
-            rest = value.astype(np.float32)
-            for part in range(3):
-                large = rest.astype(jnp.bfloat16)
-                out[0, parity, : MODES // 2, TURN_AT + 3 * k + part] = large
-                rest = rest - large.astype(np.float32)
-        out[0, parity, : MODES // 2, TURN_AT + 6] = np.where(modes == 0, 1.0, 2.0) / NA
-    return out
+        waves = []
+        for azimuth in (there, back):
+            phase = (modes[:, None] * azimuth[None, :] % NA) * (2.0 * math.pi / NA)
+            waves.append(np.concatenate([np.cos(phase), np.sin(phase)], 0))
+        for x in range(2):
+            for k, by in enumerate((0, LONG, 0, HALF)):
+                turn = (modes * (by + x * 8 * ROWS) % NA) * (2.0 * math.pi / NA)
+                turns[x, parity, :, 2 * k] = np.cos(turn)
+                turns[x, parity, :, 2 * k + 1] = np.sin(turn)
+            turns[x, parity, :, 8] = np.where(modes == 0, 1.0, 2.0) / NA
+        tables.append(waves)
+    there, back = [np.stack(t).astype(np.float32) for t in zip(*tables)]
+    return split(there), split(back), turns
 
 
 def split(x):
@@ -111,10 +111,10 @@
 
 
 HT_ROWS = 136
-AZ_ROWS = 64
-
-
-def pack_kernel(state, to_right, to_left, ht_then, ht_first, up, down):
+AZ_ROWS = 72
+
+
+def pack_kernel(state, ht_then, ht_first, up, down):
     inv_r, half_arc = radial_rates(NR)
     zero = jnp.zeros((1, NR), jnp.float32)
     for out, edge, inside, sign in ((up, HTS - 1, HTS - 2, 1.0), (down, 0, 1, -1.0)):
@@ -132,8 +132,17 @@
     ht_first[...] = jnp.where(odd, down[...], up[...])
     ht_then[...] = jnp.where(odd, up[...], down[...])
 
+
+def pack_az_kernel(state, zone, resistance, after, to_right, to_left):
+    zero = jnp.zeros((1, NR), jnp.float32)
     edge_message(to_right, state, ROWS - 1, ROWS - 2, 1.0, zero, zero)
     edge_message(to_left, state, 0, 1, -1.0, zero, zero)
+    ids, found = zone[ROWS - 1 : ROWS], zero
+    for k in range(ZONES):
+        found = jnp.where(ids == k, 2.0 * (1.0 / resistance[0:1, k : k + 1]), found)
+    to_right[64:65] = found
+    to_right[65:AZ_ROWS] = jnp.zeros((AZ_ROWS - 65, NR), jnp.float32)
+    to_left[64:AZ_ROWS] = jnp.zeros((AZ_ROWS - 64, NR), jnp.float32)
 
 
 def edge_message(out, state, j, inside, sign, w_low, w_high):
@@ -259,10 +268,11 @@
     p0, v0 = state[0, 0, :, 0:128], state[2, 0, :, 0:128]
     own_p, own_v = mid[0, 1] - turn * left[16:32, 0:128], mid[2, 1] - turn * left[0:16, 0:128]
     far_p = -turn * v0
+    wall = jnp.where(jnp.logical_and(on_ground, height == 0), (0.25 * DT) * left[64:65, 0:128] * far_p, 0.0)
     far_low = jnp.where(on_ground, far_p[0:1], -turn * low[128:129, 0:128])
     far_high = -turn * high[128:129, 0:128]
     last = [
-        0.5 * (far_p - turn * own_v),
+        0.5 * (far_p - turn * own_v) + wall,
         (-0.5 * DT) * radial_diff(far_p),
         (-0.5 * turn) * (p0 + own_p),
         (-0.5 * DT) * row_diff(far_p, far_low, far_high),
@@ -272,9 +282,7 @@
     weight = corner_weight(128)
 
     end = ROWS - 1
-    at_ground = jnp.logical_and(on_ground, height == 0)
-    owed = [jnp.where(at_ground, ground[1, end : end + 1, 0:128], 0.0), none]
-    factor = jnp.where(at_ground, (-0.25 * DT) * turn * v0, 0.0)
+    owed = [none, none]
     for below, above in ((w_below(low, ground, end), high[32 + end : 33 + end]), (low[129:130], high[129:130])):
         below, above = weight * below[:, 0:128], -weight * above[:, 0:128]
         owed.append(jnp.where(height == HTS - 1, above, jnp.where(height == 0, below, 0.0)))
@@ -282,7 +290,7 @@
     emit(0, before, second(HALF))
     emit(1, last, second(HALF + 1))
     emit(HALF, second(HALF - 2), owed)
-    emit(HALF + 1, second(HALF - 1), [factor] + [none] * 3)
+    emit(HALF + 1, second(HALF - 1), [none] * COMPS)
 
     for out, j, corner in ((left_corner, 0, 128), (right_corner, end, 129)):
         rows = [w_below(low, ground, j), high[32 + j : 33 + j], low[corner : corner + 1], high[corner : corner + 1]]
@@ -303,61 +311,63 @@
             stepped[i, j] = value
 
 
-def ground_terms(circle):
-    near = lax.broadcasted_iota(jnp.int32, (1, 128), 1) < NI
-    sectors = sector_of_chunk().tolist()
-
-    def row(chunk, r):
-        return pl.ds(chunk * LONG + r, 1)
-
-    for k, sector in enumerate(sectors):
-        last = sectors.index((sector - 1) % SECTORS)
-        term = circle[row(last, HALF), :] * circle[row(k, HALF + 1), :]
-        circle[row(k, 1), :] = circle[row(k, 1), :] + jnp.where(near, pltpu.roll(term, NI, 1), 0.0)
-    for k in range(SECTORS):
-        for r in (HALF, HALF + 1):
-            circle[row(k, r), :] = jnp.where(near, circle[row(k, r), :], 0.0)
-
-
-def filter_kernel(table, cutoff, x_ref, o_ref, circle):
-    m = SECTORS // 2 * LONG
-    circle[...] = x_ref[...]
-
-    @pl.when(lax.axis_index("y") * 16 + lax.axis_index("z") * 2 + lax.axis_index("x") == 0)
-    def _():
-        ground_terms(circle)
-
-    first, second = circle[:m], circle[m:]
+def turns_of(turn, x, parity, way):
+    near = lax.broadcasted_iota(jnp.int32, (MODES // 2, 128), 1) < NI
+    return [
+        jnp.where(near, turn[x, parity, :, k : k + 1], turn[x, parity, :, k + 2 : k + 3])
+        for k in (4 * way, 4 * way + 1)
+    ]
+
+
+def analysis_kernel(wave, wave_small, turn, circle, sums, folded):
+    for z in range(8):
+        for y in range(2):
+            for q in range(SETS):
+                one, two = [circle[pl.ds(((4 * z + k) * SETS + q) * LONG, LONG), :] for k in (y, y + 2)]
+                at = pl.ds((2 * z + y) * LONG, LONG)
+                folded[0, q, at, :] = one + two
+                folded[1, q, at, :] = one - two
+    x = lax.axis_index("x")
+    h = MODES // 2
+    near = lax.broadcasted_iota(jnp.int32, (h, 128), 1) < NI
+    for parity in range(2):
+        cs, sn = turns_of(turn, x, parity, 0)
+        found = []
+        for q in range(SETS):
+            coef = product((wave[parity], wave_small[parity]), split(folded[parity, q]), ((1,), (0,)))
+            a, b = coef[:h], coef[h:]
+            found.append([t + pltpu.roll(t, NI, 1) for t in (a * cs - b * sn, a * sn + b * cs)])
+        for k in range(2):
+            at = (2 * parity + k) * h
+            sums[at : at + h] = jnp.where(near, found[0][k], found[1][k])
+
+
+def synthesis_kernel(wave, wave_small, turn, cutoff, mine, other, out):
+    x = lax.axis_index("x")
     h = MODES // 2
     mode = lax.broadcasted_iota(jnp.int32, (h, 128), 0) * 2
     near = lax.broadcasted_iota(jnp.int32, (h, 128), 1) < NI
     limit = jnp.concatenate([cutoff[...], cutoff[...]], 1)
-    outs = []
+    parts = []
     for parity in range(2):
-        folded = first + second if parity == 0 else first - second
-        waves = table[0, parity, :, :TURN_AT], table[1, parity, :, :TURN_AT]
-        parts = table[0, parity, :h, TURN_AT : TURN_AT + 64].astype(jnp.float32)
-        cs, sn = [parts[:, k : k + 1] + parts[:, k + 1 : k + 2] + parts[:, k + 2 : k + 3] for k in (0, 3)]
-        weight = parts[:, 6:7]
-        coef = product(waves, split(folded), ((1,), (0,)))
-        a, b = coef[:h], coef[h:]
-        a_all = jnp.where(near, a, a * cs - b * sn)
-        b_all = jnp.where(near, b, a * sn + b * cs)
-        keep = jnp.where(mode + parity < limit, weight, 0.0)
-        a_all = (a_all + pltpu.roll(a_all, NI, 1)) * keep
-        b_all = (b_all + pltpu.roll(b_all, NI, 1)) * keep
-        a_back = jnp.where(near, a_all, a_all * cs + b_all * sn)
-        b_back = jnp.where(near, b_all, b_all * cs - a_all * sn)
-        both = jnp.concatenate([a_back, b_back], 0)
-        outs.append(product(waves, split(both), ((0,), (0,))))
-    for half in range(2):
-        circle[half * m : (half + 1) * m] = outs[0] + outs[1] if half == 0 else outs[0] - outs[1]
-    row_near = lax.broadcasted_iota(jnp.int32, (HALF, 128), 1) < NI
-    for k in range(SECTORS):
-        at = k * LONG
-        o_ref[k * HALF : (k + 1) * HALF] = jnp.where(
-            row_near, circle[at + 2 : at + 2 + HALF], circle[at : at + HALF]
-        )
+        cs, sn = turns_of(turn, x, parity, 1)
+        keep = jnp.where(mode + parity < limit, turn[x, parity, :, 8:9], 0.0)
+        a, b = [
+            (mine[at : at + h] + other[at : at + h]) * keep for at in (2 * parity * h, (2 * parity + 1) * h)
+        ]
+        a_far, b_far = pltpu.roll(a, NI, 1), pltpu.roll(b, NI, 1)
+        for q in range(SETS):
+            a_all, b_all = [jnp.where(near == (q == 0), t, far) for t, far in ((a, a_far), (b, b_far))]
+            both = jnp.concatenate([a_all * cs + b_all * sn, b_all * cs - a_all * sn], 0)
+            parts.append(product((wave[parity], wave_small[parity]), split(both), ((0,), (0,))))
+    for q in range(SETS):
+        even, odd = parts[q], parts[SETS + q]
+        for z in range(8):
+            for y in range(2):
+                at = slice((2 * z + y) * HALF, (2 * z + y + 1) * HALF)
+                for k, value in ((y, even[at] + odd[at]), (y + 2, even[at] - odd[at])):
+                    to = ((4 * z + k) * SETS + q) * HALF
+                    out[to : to + HALF] = value
 
 
 def edge_terms(right, left_corner, right_corner, ground):
@@ -446,14 +456,21 @@
         return tuple(jax.ShapeDtypeStruct(d, f32) for d in dims)
 
     ht_message, az_message = (HT_ROWS, NR), (AZ_ROWS, NR)
-    to_right, to_left, ht_then, ht_first = call(
+    ht_then, ht_first = call(
         pack_kernel,
-        out_shape=shapes(az_message, az_message, ht_message, ht_message),
+        out_shape=shapes(ht_message, ht_message),
         in_specs=[vmem],
-        out_specs=(vmem,) * 4,
+        out_specs=(vmem,) * 2,
         scratch_shapes=[pltpu.VMEM(ht_message, f32)] * 2,
         name="pack",
     )(state)
+    to_right, to_left = call(
+        pack_az_kernel,
+        out_shape=shapes(az_message, az_message),
+        in_specs=[vmem] * 3 + [anywhere],
+        out_specs=(vmem,) * 2,
+        name="pack_az",
+    )(state, zone_id, resistance.reshape(1, ZONES), ht_first)
     ground = call(
         ground_kernel,
         out_shape=shapes((3, ROWS, NR))[0],
@@ -484,7 +501,7 @@
         cost_estimate=pl.CostEstimate(flops=10**7, bytes_accessed=6 * 10**6, transcendentals=0),
         name="inner",
     )(state, left, ht_then, ht_first, ground)
-    circle = lax.all_to_all(packed.reshape(SECTORS, LONG, 1, 128), SPREAD, 0, 0, tiled=True)
+    circle = lax.all_to_all(packed.reshape(PEERS, SETS * LONG, 1, 128), SPREAD, 0, 0, tiled=True)
     left_corner, right_corner = lax.ppermute(to_right, AZ, rightward), lax.ppermute(to_left, AZ, leftward)
     stepped = call(
         outer_kernel,
@@ -496,15 +513,24 @@
         cost_estimate=pl.CostEstimate(flops=2 * 10**7, bytes_accessed=2 * 10**7, transcendentals=0),
         name="outer",
     )(state, ht_then, ht_first, left, ground)
+    there, back, turns = jax.tree.map(jnp.asarray, mode_tables())
+    sums = call(
+        analysis_kernel,
+        out_shape=shapes((2 * MODES, 128))[0],
+        in_specs=[vmem] * 4,
+        out_specs=vmem,
+        scratch_shapes=[pltpu.VMEM((2, SETS, PEERS // 2 * LONG, 128), f32)],
+        name="analysis",
+    )(*there, turns, circle.reshape(PEERS * SETS * LONG, 128))
+    other = lax.ppermute(sums, "x", [(0, 1), (1, 0)])
     kept = call(
-        filter_kernel,
-        out_shape=shapes((NA // 2, 128))[0],
-        in_specs=[vmem] * 3,
+        synthesis_kernel,
+        out_shape=shapes((PEERS * SETS * HALF, 128))[0],
+        in_specs=[vmem] * 6,
         out_specs=vmem,
-        scratch_shapes=[pltpu.VMEM((SECTORS * LONG, 128), f32)],
-        name="filter",
-    )(jnp.asarray(mode_tables()), cutoff.reshape(1, NI), circle.reshape(SECTORS * LONG, 128))
-    back = lax.all_to_all(kept.reshape(SECTORS, HALF, 128), SPREAD, 0, 0, tiled=True)
+        name="synthesis",
+    )(*back, turns, cutoff.reshape(1, NI), sums, other)
+    back = lax.all_to_all(kept.reshape(PEERS, SETS * HALF, 128), SPREAD, 0, 0, tiled=True)
     return call(
         merge_kernel,
         out_shape=jax.ShapeDtypeStruct(stepped.shape, f32),

time: 72.4 us -> 74.6 us (1.030); the launches traced: 71.3 us -> 74.2 us
  waiting for transfers between devices: 5.44 us -> 12.2 us
  starting transfers between devices: 20.7 us -> 18.6 us
  local copies, waits for them, and re-layouts: 3.13 us -> 1.65 us
    ppermute x0 -> x1, waiting for transfers between devices: none -> 4.38 us  [per_device(): other = lax.ppermute(sums, 'x', [(0, 1), (1, 0)])]
    all_to_all x1, starting transfers between devices: 6.89 us -> 5.25 us  [per_device(): lax.all_to_all(kept.reshape(PEERS, SETS * HALF, 128), SPREAD, 0, 0, tiled...]
    ppermute x2, waiting for transfers between devices: 0.19 us -> 1.74 us  [per_device(): lax.ppermute(to_right, AZ, rightward)]
    unnamed x16 -> x24, local copies, waits for them, and re-layouts: 3.13 us -> 1.65 us
    ppermute x2, starting transfers between devices: 5.07 us -> 3.76 us  [per_device(): lax.ppermute(to_left, AZ, leftward)]
    pallas_call x2 -> x4, Pallas kernels: 2.45 us -> 2.31 us  [the longest x1 1.42 us: per_device(): call(synthesis_kernel, out_shape=shapes((PEERS * SETS * HALF, 128))[0], i...]
  transfers between devices with their start and end apart: 7 -> 8, of which waited for: 4 -> 5; matrix products, arithmetic and copies ran while one was open for 0% -> 0% of each run, Pallas kernels for 7% -> 7%
where the time goes in v8:
time: 74.6 us; the launch traced here: 74.2 us
  blocking collectives  30 us (40%)
  starting transfers between devices  18.6 us (25%)
  waiting for transfers between devices  12.2 us (16%)
  Pallas kernels  11.7 us (16%)
  local copies, waits for them, and re-layouts  1.65 us (2%)
    all_to_all x1, blocking collectives, per_device(): lax.all_to_all(packed.reshape(PEERS, SETS * LONG, 1, 128), SPREAD, 0, 0,...  30 us
    all_to_all x1, starting transfers between devices, per_device(): lax.all_to_all(kept.reshape(PEERS, SETS * HALF, 128), SPREAD, 0, 0, tiled...  5.25 us
    ppermute x2, starting transfers between devices, swap(): return lax.ppermute(x, HT, pairs + [(b, a) for a, b in pairs])  5.13 us
    ppermute x1, waiting for transfers between devices, per_device(): other = lax.ppermute(sums, 'x', [(0, 1), (1, 0)])  4.38 us
    pallas_call x1, Pallas kernels, per_device(): call(outer_kernel, mib=16, out_shape=shapes((COMPS, ROWS, HTS, NR))[0], i...  4.3 us
    all_to_all x1, waiting for transfers between devices, per_device(): lax.all_to_all(kept.reshape(PEERS, SETS * HALF, 128), SPREAD, 0, 0, tiled...  4.13 us
    ppermute x2, starting transfers between devices, per_device(): lax.ppermute(to_right, AZ, rightward)  3.78 us
    ppermute x2, starting transfers between devices, per_device(): lax.ppermute(to_left, AZ, leftward)  3.76 us
  transfers between devices with their start and end apart: 8, of which 5 were waited for; matrix products, arithmetic and copies ran while one was open for 0% of the time, Pallas kernels for 7%

profile of v8, /device:TPU:32, one launch (start us, length us, event | category | flops | bytes accessed | tf_op | source)
XLA Modules:
  0.0 74.2 jit_solution(440738971541891068)
XLA Ops:
  0.0 1.6 %copy-done = f32[4,32,16,256]{3,2,1,0:T(8,128)S(1)} copy-done((f32[4,32,16,256]{3,2,1,0:T(8,128)S(1)}, f32[4,32,16,256]{3,2,1,0:T(8,128)}, u32[]{:S(2)}) %copy-start) | copy-done | bytes 2097176
  1.6 0.2 pack.1
  1.9 0.7 collective-permute-start
  2.5 4.5 %collective-permute-start.1 = (f32[136,256]{1,0:T(8,128)S(1)}, f32[136,256]{1,0:T(8,128)S(1)}, u32[]{:S(2)}, u32[]{:S(2)}) collective-permute-start(f32[136,256]{1,0:T(8,128)S(1)} %get-tuple-element.13.after), channel_id=1, source_target_pairs={{0,1},{2,3},{1,0},{3,2},{4,5},{6,7},{5,4},{7,6},{8,9},{10,11},{9,8... | collective-permute-start | bytes 417800 | tf_op jit(solution)/shard_map/ppermute | solution.py:483
  7.0 0.1 pack_az.1
  7.1 2.0 %collective-permute-start.2 = (f32[72,256]{1,0:T(8,128)S(1)}, f32[72,256]{1,0:T(8,128)S(1)}, u32[]{:S(2)}, u32[]{:S(2)}) collective-permute-start(f32[72,256]{1,0:T(8,128)S(1)} %get-tuple-element.14), channel_id=1, source_target_pairs={{0,4},{4,8},{8,12},{12,16},{16,20},{20,24},{24,28},{28,32},{32,36}... | collective-permute-start | bytes 221192 | tf_op jit(solution)/shard_map/ppermute | solution.py:487
  9.1 0.6 ground.1
  9.7 0.0 copy-start.2
  9.8 1.7 %collective-permute-done.2.left = f32[72,256]{1,0:T(8,128)S(1)} collective-permute-done((f32[72,256]{1,0:T(8,128)S(1)}, f32[72,256]{1,0:T(8,128)S(1)}, u32[]{:S(2)}, u32[]{:S(2)}) %collective-permute-start.2) | collective-permute-done | bytes 73760 | tf_op jit(solution)/shard_map/ppermute | solution.py:487
  11.6 2.1 %inner.1 = (f32[1152,128]{1,0:T(8,128)S(1)}, f32[8,256]{1,0:T(8,128)S(1)}, f32[8,256]{1,0:T(8,128)S(1)}) custom-call(f32[4,32,16,256]{3,2,1,0:T(8,128)S(1)} %copy-done.1, f32[72,256]{1,0:T(8,128)S(1)} %collective-permute-done.2.left, f32[136,256]{1,0:T(8,128)S(1)} %collective-permute-done.ht_then, f32[136,256]{1,0:T(8,128)S(1)} %collective-permute-done.1.ht_first, ...), custom_call_target="tpu_custom_call" | custom-call | flops 10000000 | bytes 6000000 | tf_op jit(solution)/shard_map/inner/pallas_call | solution.py:494
  13.7 30.0 %all_to_all.10 = f32[32,36,1,128]{3,2,1,0:T(1,128)S(1)} all-to-all(f32[32,36,1,128]{3,2,1,0:T(1,128)S(1)} %bitcast.8), channel_id=1, replica_groups=mesh['y'=4,'x'=2,'z'=8,'hx'=2,'core'=2] {'z','y'}, dimensions={0} | all-to-all | bytes 1179648 | tf_op jit(solution)/shard_map/all_to_all | solution.py:504
  43.7 0.6 analysis.1.mine
  44.2 0.7 collective-permute-start.3
  44.9 4.4 %collective-permute-done.3.other = f32[256,128]{1,0:T(8,128)S(1)} collective-permute-done((f32[256,128]{1,0:T(8,128)S(1)}, f32[256,128]{1,0:T(8,128)S(1)}, u32[]{:S(2)}, u32[]{:S(2)}) %collective-permute-start.3) | collective-permute-done | bytes 131104 | tf_op jit(solution)/shard_map/ppermute | solution.py:525
  49.3 1.4 %synthesis.1 = f32[1024,128]{1,0:T(8,128)} custom-call(bf16[2,128,256]{2,1,0:T(8,128)(2,1)S(1)} %copy-done.7, bf16[2,128,256]{2,1,0:T(8,128)(2,1)S(1)} %copy-done.6, f32[2,2,64,128]{3,2,1,0:T(8,128)S(1)} %copy-done.2, s32[1,64]{1,0:T(1,128)S(1)} %bitcast.10, f32[256,128]{1,0:T(8,128)S(1)} %analysis.1.mine, f32[256,128]{1,0:T(8,128)S(1)} %collective-permute-done.3.other), custom_call_target="tpu_custom_call" | custom-call | tf_op jit(solution)/shard_map/synthesis/pallas_call | solution.py:526
  50.7 5.2 %all-to-all-start.1 = ((f32[32,32,128]{2,1,0:T(8,128)}), f32[32,32,128]{2,1,0:T(8,128)S(1)}, u32[]{:S(2)}, u32[]{:S(2)}) async-start(f32[32,32,128]{2,1,0:T(8,128)} %bitcast.4), calls=%async_computation.1 | async-start | bytes 1048576 | tf_op jit(solution)/shard_map/all_to_all | solution.py:533
  56.0 0.3 collective-permute-start.4
  56.3 1.8 %collective-permute-start.5 = (f32[8,256]{1,0:T(8,128)S(1)}, f32[8,256]{1,0:T(8,128)S(1)}, u32[]{:S(2)}, u32[]{:S(2)}) collective-permute-start(f32[8,256]{1,0:T(8,128)S(1)} %get-tuple-element.17), channel_id=1, source_target_pairs={{0,4},{4,8},{8,12},{12,16},{16,20},{20,24},{24,28},{28,32},{32,36}... | collective-permute-start | bytes 24584 | tf_op jit(solution)/shard_map/ppermute | solution.py:505
  58.1 3.4 %collective-permute-start.6 = (f32[8,256]{1,0:T(8,128)S(1)}, f32[8,256]{1,0:T(8,128)S(1)}, u32[]{:S(2)}, u32[]{:S(2)}) collective-permute-start(f32[8,256]{1,0:T(8,128)S(1)} %get-tuple-element.18), channel_id=1, source_target_pairs={{4,0},{8,4},{12,8},{16,12},{20,16},{24,20},{28,24},{32,28},{36,32}... | collective-permute-start | bytes 24584 | tf_op jit(solution)/shard_map/ppermute | solution.py:505
  61.5 4.3 %outer.1.stepped = f32[4,32,16,256]{3,2,1,0:T(8,128)} custom-call(f32[4,32,16,256]{3,2,1,0:T(8,128)S(1)} %copy-done.1, f32[136,256]{1,0:T(8,128)S(1)} %collective-permute-done.ht_then, f32[136,256]{1,0:T(8,128)S(1)} %collective-permute-done.1.ht_first, f32[72,256]{1,0:T(8,128)S(1)} %collective-permute-done.2.left, f32[3,32,256]{2,1,0:T(8,128)S(1)} %ground.1), custom_call_target="tpu_custom_call" | custom-call | flops 20000000 | bytes 20000000 | tf_op jit(solution)/shard_map/outer/pallas_call | solution.py:506
  65.8 1.8 %collective-permute-done.4.right = f32[72,256]{1,0:T(8,128)S(1)} collective-permute-done((f32[72,256]{1,0:T(8,128)S(1)}, f32[72,256]{1,0:T(8,128)S(1)}, u32[]{:S(2)}, u32[]{:S(2)}) %collective-permute-start.4) | collective-permute-done | bytes 73760 | tf_op jit(solution)/shard_map/ppermute | solution.py:487
  67.7 0.1 collective-permute-done.6.right_corner
  67.7 4.1 %all-to-all-done.1 = f32[32,32,128]{2,1,0:T(8,128)S(1)} async-done(((f32[32,32,128]{2,1,0:T(8,128)}), f32[32,32,128]{2,1,0:T(8,128)S(1)}, u32[]{:S(2)}, u32[]{:S(2)}) %all-to-all-start.1) | async-done | bytes 524320 | tf_op jit(solution)/shard_map/all_to_all | solution.py:533
  71.9 2.4 %merge.1 = f32[4,32,16,256]{3,2,1,0:T(8,128)} custom-call(f32[4,32,16,256]{3,2,1,0:T(8,128)} %outer.1.stepped, f32[1024,128]{1,0:T(8,128)S(1)} %bitcast.7, f32[72,256]{1,0:T(8,128)S(1)} %collective-permute-done.4.right, f32[8,256]{1,0:T(8,128)S(1)} %collective-permute-done.5.left_corner, ...), custom_call_target="tpu_custom_call", output_to_operand_aliasing={{}: (0, {})} | custom-call | tf_op jit(solution)/shard_map/merge/pallas_call | solution.py:534
  (25 shorter events, 0.1 us)
Async XLA Ops:
  0.0 1.6 %copy-start = (f32[4,32,16,256]{3,2,1,0:T(8,128)S(1)}, f32[4,32,16,256]{3,2,1,0:T(8,128)}, u32[]{:S(2)}) copy-start(f32[4,32,16,256]{3,2,1,0:T(8,128)} %state.9) | copy-start | bytes 6291460
  1.6 5.4 %copy-start.5 = (s32[32,256]{1,0:T(8,128)S(1)}, s32[32,256]{1,0:T(8,128)}, u32[]{:S(2)}) copy-start(s32[32,256]{1,0:T(8,128)} %zone.3) | copy-start | bytes 98308
  1.6 5.4 %copy-start.9 = (f32[8]{0:T(128)S(1)}, f32[8]{0:T(128)}, u32[]{:S(2)}) copy-start(f32[8]{0:T(128)} %resistance.1) | copy-start | bytes 100
  1.6 7.5 %copy-start.8 = (f32[32,256]{1,0:T(8,128)S(1)}, f32[32,256]{1,0:T(8,128)}, u32[]{:S(2)}) copy-start(f32[32,256]{1,0:T(8,128)} %aux.1) | copy-start | bytes 98308
  1.6 7.5 %copy-start.11 = (f32[8]{0:T(128)S(1)}, f32[8]{0:T(128)}, u32[]{:S(2)}) copy-start(f32[8]{0:T(128)} %relax.1) | copy-start | bytes 100
  1.9 9.7 %collective-permute-start = (f32[136,256]{1,0:T(8,128)S(1)}, f32[136,256]{1,0:T(8,128)S(1)}, u32[]{:S(2)}, u32[]{:S(2)}) collective-permute-start(f32[136,256]{1,0:T(8,128)S(1)} %get-tuple-element.12), channel_id=1, source_target_pairs={{1,2},{2,1},{5,6},{6,5},{9,10},{10,9},{13,14},{14,13},{17,18},{18,... | collective-permute-start | bytes 417800 | tf_op jit(solution)/shard_map/ppermute | solution.py:483
  2.5 9.0 %collective-permute-start.1 = (f32[136,256]{1,0:T(8,128)S(1)}, f32[136,256]{1,0:T(8,128)S(1)}, u32[]{:S(2)}, u32[]{:S(2)}) collective-permute-start(f32[136,256]{1,0:T(8,128)S(1)} %get-tuple-element.13.after), channel_id=1, source_target_pairs={{0,1},{2,3},{1,0},{3,2},{4,5},{6,7},{5,4},{7,6},{8,9},{10,11},{9,8... | collective-permute-start | bytes 417800 | tf_op jit(solution)/shard_map/ppermute | solution.py:483
  7.0 4.5 %copy-start.1 = (f32[4,32,16,256]{3,2,1,0:T(8,128)S(1)}, f32[4,32,16,256]{3,2,1,0:T(8,128)}, u32[]{:S(2)}) copy-start(f32[4,32,16,256]{3,2,1,0:T(8,128)} %state.9) | copy-start | bytes 6291460
  7.1 4.4 %collective-permute-start.2 = (f32[72,256]{1,0:T(8,128)S(1)}, f32[72,256]{1,0:T(8,128)S(1)}, u32[]{:S(2)}, u32[]{:S(2)}) collective-permute-start(f32[72,256]{1,0:T(8,128)S(1)} %get-tuple-element.14), channel_id=1, source_target_pairs={{0,4},{4,8},{8,12},{12,16},{16,20},{20,24},{24,28},{28,32},{32,36}... | collective-permute-start | bytes 221192 | tf_op jit(solution)/shard_map/ppermute | solution.py:487
  9.7 33.9 %copy-start.2 = (f32[2,2,64,128]{3,2,1,0:T(8,128)S(1)}, f32[2,2,64,128]{3,2,1,0:T(8,128)}, u32[]{:S(2)}) copy-start(f32[2,2,64,128]{3,2,1,0:T(8,128)} %constant.14.clone.turn) | copy-start | bytes 393220
  9.7 33.9 %copy-start.3 = (bf16[2,128,288]{2,1,0:T(8,128)(2,1)S(1)}, bf16[2,128,288]{2,1,0:T(8,128)(2,1)}, u32[]{:S(2)}) copy-start(bf16[2,128,288]{2,1,0:T(8,128)(2,1)} %constant.11.clone.wave_small) | copy-start | bytes 442372
  9.8 33.9 %copy-start.4 = (bf16[2,128,288]{2,1,0:T(8,128)(2,1)S(1)}, bf16[2,128,288]{2,1,0:T(8,128)(2,1)}, u32[]{:S(2)}) copy-start(bf16[2,128,288]{2,1,0:T(8,128)(2,1)} %constant.10.clone.wave) | copy-start | bytes 442372
  9.8 39.5 %copy-start.6 = (bf16[2,128,256]{2,1,0:T(8,128)(2,1)S(1)}, bf16[2,128,256]{2,1,0:T(8,128)(2,1)}, u32[]{:S(2)}) copy-start(bf16[2,128,256]{2,1,0:T(8,128)(2,1)} %constant.13.clone.wave_small) | copy-start | bytes 393220
  9.8 39.5 %copy-start.7 = (bf16[2,128,256]{2,1,0:T(8,128)(2,1)S(1)}, bf16[2,128,256]{2,1,0:T(8,128)(2,1)}, u32[]{:S(2)}) copy-start(bf16[2,128,256]{2,1,0:T(8,128)(2,1)} %constant.12.clone.wave) | copy-start | bytes 393220
  9.8 39.5 %copy-start.10 = (s32[64]{0:T(128)S(1)}, s32[64]{0:T(128)}, u32[]{:S(2)}) copy-start(s32[64]{0:T(128)} %param.16) | copy-start | bytes 772
  44.2 5.1 %collective-permute-start.3 = (f32[256,128]{1,0:T(8,128)S(1)}, f32[256,128]{1,0:T(8,128)S(1)}, u32[]{:S(2)}, u32[]{:S(2)}) collective-permute-start(f32[256,128]{1,0:T(8,128)S(1)} %analysis.1.mine), channel_id=1, source_target_pairs={{0,32},{32,0},{1,33},{33,1},{2,34},{34,2},{3,35},{35,3},{4,36},{36... | collective-permute-start | bytes 393224 | tf_op jit(solution)/shard_map/ppermute | solution.py:525
  50.7 21.1 %all-to-all-start.1 = ((f32[32,32,128]{2,1,0:T(8,128)}), f32[32,32,128]{2,1,0:T(8,128)S(1)}, u32[]{:S(2)}, u32[]{:S(2)}) async-start(f32[32,32,128]{2,1,0:T(8,128)} %bitcast.4), calls=%async_computation.1 | async-start | bytes 1048576 | tf_op jit(solution)/shard_map/all_to_all | solution.py:533
  56.0 11.7 %collective-permute-start.4 = (f32[72,256]{1,0:T(8,128)S(1)}, f32[72,256]{1,0:T(8,128)S(1)}, u32[]{:S(2)}, u32[]{:S(2)}) collective-permute-start(f32[72,256]{1,0:T(8,128)S(1)} %get-tuple-element.16), channel_id=1, source_target_pairs={{4,0},{8,4},{12,8},{16,12},{20,16},{24,20},{28,24},{32,28},{36,32}... | collective-permute-start | bytes 221192 | tf_op jit(solution)/shard_map/ppermute | solution.py:487
  56.3 11.4 %collective-permute-start.5 = (f32[8,256]{1,0:T(8,128)S(1)}, f32[8,256]{1,0:T(8,128)S(1)}, u32[]{:S(2)}, u32[]{:S(2)}) collective-permute-start(f32[8,256]{1,0:T(8,128)S(1)} %get-tuple-element.17), channel_id=1, source_target_pairs={{0,4},{4,8},{8,12},{12,16},{16,20},{20,24},{24,28},{28,32},{32,36}... | collective-permute-start | bytes 24584 | tf_op jit(solution)/shard_map/ppermute | solution.py:505
  58.1 9.7 %collective-permute-start.6 = (f32[8,256]{1,0:T(8,128)S(1)}, f32[8,256]{1,0:T(8,128)S(1)}, u32[]{:S(2)}, u32[]{:S(2)}) collective-permute-start(f32[8,256]{1,0:T(8,128)S(1)} %get-tuple-element.18), channel_id=1, source_target_pairs={{4,0},{8,4},{12,8},{16,12},{20,16},{24,20},{28,24},{32,28},{36,32}... | collective-permute-start | bytes 24584 | tf_op jit(solution)/shard_map/ppermute | solution.py:505

commit v9 on v4

--- a/solution.py
+++ b/solution.py
@@ -23,17 +23,12 @@
 DT = 0.4
 
 AZ = ("y", "x", "z")
-SPREAD = ("y", "z", "x")
+SPREAD = AZ
 HT = ("hx", "core")
 
 
-def sector_of_chunk():
-    y, z, x = np.meshgrid(np.arange(4), np.arange(8), np.arange(2), indexing="ij")
-    return ((y * 2 + x) * 8 + z).reshape(-1)
-
-
 def mode_tables():
-    first = sector_of_chunk()[: SECTORS // 2, None] * ROWS
+    first = np.arange(SECTORS // 2)[:, None] * ROWS
     there = (first - 1 + np.arange(LONG)[None, :]).reshape(-1)
     back = (first + np.arange(HALF)[None, :]).reshape(-1)
     tables = []
@@ -114,6 +109,7 @@
 
 HT_ROWS = 136
 AZ_ROWS = 64
+AZ_LONG = 144
 
 
 def pack_kernel(state, az_then, ht_then, az_first, ht_first, up, down, to_left, to_right):
@@ -141,10 +137,11 @@
 
     for odd, one, two, ahead, behind in (
         (odd_slab(), ht_first, ht_then, up, down),
-        (odd_sector(), az_first, az_then, to_right, to_left),
+        (odd_sector(), az_first, az_then.at[0:AZ_ROWS], to_right, to_left),
     ):
         one[...] = jnp.where(odd, behind[...], ahead[...])
         two[...] = jnp.where(odd, ahead[...], behind[...])
+    az_then[AZ_ROWS:AZ_LONG] = jnp.zeros((AZ_LONG - AZ_ROWS, NR), jnp.float32)
 
 
 def ground_kernel(resistance, relax, state, zone, aux, ground):
@@ -232,7 +229,7 @@
     state, az_then, ht_then, az_first, ht_first, ground, packed, low, high, left, right, to_left, to_right, mid, ghost
 ):
     unswap(odd_slab(), ht_first, ht_then, low, high)
-    unswap(odd_sector(), az_first, az_then, left, right)
+    unswap(odd_sector(), az_first, az_then.at[0:AZ_ROWS], left, right)
     near = lax.broadcasted_iota(jnp.int32, (HTS, 128), 1) < NI
     height = lax.broadcasted_iota(jnp.int32, (HTS, 128), 0)
     second = two_stages(128, state, low, high, left, right, ground, mid, ghost)
@@ -363,7 +360,7 @@
     ht_message, az_message = (HT_ROWS, NR), (AZ_ROWS, NR)
     az_then, ht_then, az_first, ht_first = call(
         pack_kernel,
-        out_shape=shapes(az_message, ht_message, az_message, ht_message),
+        out_shape=shapes((AZ_LONG, NR), ht_message, az_message, ht_message),
         in_specs=[vmem],
         out_specs=(vmem,) * 4,
         scratch_shapes=[pltpu.VMEM(m, f32) for m in (ht_message, ht_message, az_message, az_message)],

time: 72.7 us -> 71.8 us (0.988); the launches traced: 71.2 us -> 71.4 us
  waiting for transfers between devices: 9.48 us -> 11.1 us
  starting transfers between devices: 22.7 us -> 21.8 us
    all_to_all x1, waiting for transfers between devices: 5.07 us -> 6.59 us  [per_device(): lax.all_to_all(kept.reshape(SECTORS, HALF, 128), SPREAD, 0, 0, tiled=True)]
    all_to_all x1, starting transfers between devices: 6.87 us -> 5.39 us  [per_device(): lax.all_to_all(kept.reshape(SECTORS, HALF, 128), SPREAD, 0, 0, tiled=True)]
  transfers between devices with their start and end apart: 7 -> 7, of which waited for: 3 -> 4; matrix products, arithmetic and copies ran while one was open for 0% -> 0% of each run, Pallas kernels for 7% -> 7%
where the time goes in v9:
time: 71.8 us; the launch traced here: 71.4 us
  blocking collectives  24 us (33%)
  starting transfers between devices  21.8 us (30%)
  Pallas kernels  11.3 us (16%)
  waiting for transfers between devices  11.1 us (15%)
  local copies, waits for them, and re-layouts  3.16 us (4%)
    all_to_all x1, blocking collectives, per_device(): lax.all_to_all(packed.reshape(SECTORS, LONG, 1, 128), SPREAD, 0, 0, tiled...  24 us
    ppermute x4, starting transfers between devices, swap(): return lax.ppermute(x, axes, pairs + [(b, a) for a, b in pairs])  14.3 us
    all_to_all x1, waiting for transfers between devices, per_device(): lax.all_to_all(kept.reshape(SECTORS, HALF, 128), SPREAD, 0, 0, tiled=True)  6.59 us
    all_to_all x1, starting transfers between devices, per_device(): lax.all_to_all(kept.reshape(SECTORS, HALF, 128), SPREAD, 0, 0, tiled=True)  5.39 us
    pallas_call x1, Pallas kernels, per_device(): call(outer_kernel, mib=16, out_shape=shapes((COMPS, ROWS, HTS, NR))[0], i...  4.28 us
    unnamed x24, local copies, waits for them, and re-layouts  3.16 us
    ppermute x1, waiting for transfers between devices, per_device(): lax.ppermute(to_right, AZ, [(i, (i + 1) % SECTORS) for i in range(SECTORS)])  3.03 us
    pallas_call x1, Pallas kernels, per_device(): call(merge_kernel, out_shape=jax.ShapeDtypeStruct(stepped.shape, f32), in...  2.21 us
  transfers between devices with their start and end apart: 7, of which 4 were waited for; matrix products, arithmetic and copies ran while one was open for 0% of the time, Pallas kernels for 7%

profile of v9, /device:TPU:32, one launch (start us, length us, event | category | flops | bytes accessed | tf_op | source)
XLA Modules:
  0.0 71.4 jit_solution(8101286159575355538)
XLA Ops:
  0.0 1.6 %copy-done = f32[4,32,16,256]{3,2,1,0:T(8,128)S(1)} copy-done((f32[4,32,16,256]{3,2,1,0:T(8,128)S(1)}, f32[4,32,16,256]{3,2,1,0:T(8,128)}, u32[]{:S(2)}) %copy-start) | copy-done | bytes 2097176
  1.6 0.3 pack.1
  1.9 2.0 %collective-permute-start = (f32[144,256]{1,0:T(8,128)S(1)}, f32[144,256]{1,0:T(8,128)S(1)}, u32[]{:S(2)}, u32[]{:S(2)}) collective-permute-start(f32[144,256]{1,0:T(8,128)S(1)} %get-tuple-element.16), channel_id=1, source_target_pairs={{4,8},{12,16},{20,24},{28,32},{36,40},{44,48},{52,56},{60,64},{68,... | collective-permute-start | bytes 442376 | tf_op jit(solution)/shard_map/ppermute | solution.py:378
  3.9 0.7 collective-permute-start.1
  4.5 4.5 %collective-permute-start.3 = (f32[136,256]{1,0:T(8,128)S(1)}, f32[136,256]{1,0:T(8,128)S(1)}, u32[]{:S(2)}, u32[]{:S(2)}) collective-permute-start(f32[136,256]{1,0:T(8,128)S(1)} %get-tuple-element.19), channel_id=1, source_target_pairs={{0,1},{2,3},{1,0},{3,2},{4,5},{6,7},{5,4},{7,6},{8,9},{10,11},{9,8... | collective-permute-start | bytes 417800 | tf_op jit(solution)/shard_map/ppermute | solution.py:378
  9.0 7.1 %collective-permute-start.2 = (f32[64,256]{1,0:T(8,128)S(1)}, f32[64,256]{1,0:T(8,128)S(1)}, u32[]{:S(2)}, u32[]{:S(2)}) collective-permute-start(f32[64,256]{1,0:T(8,128)S(1)} %get-tuple-element.18), channel_id=1, source_target_pairs={{0,4},{8,12},{16,20},{24,28},{32,36},{40,44},{48,52},{56,60},{64,6... | collective-permute-start | bytes 196616 | tf_op jit(solution)/shard_map/ppermute | solution.py:378
  16.2 0.8 %copy-done.7 = s32[32,256]{1,0:T(8,128)S(1)} copy-done((s32[32,256]{1,0:T(8,128)S(1)}, s32[32,256]{1,0:T(8,128)}, u32[]{:S(2)}) %copy-start.7) | copy-done | bytes 32792
  16.9 0.8 %copy-done.8 = f32[32,256]{1,0:T(8,128)S(1)} copy-done((f32[32,256]{1,0:T(8,128)S(1)}, f32[32,256]{1,0:T(8,128)}, u32[]{:S(2)}) %copy-start.8) | copy-done | bytes 32792
  17.7 0.6 ground.1
  18.3 0.0 copy-start.2
  18.3 0.0 copy-start.3
  18.3 0.0 copy-start.4
  18.4 0.1 collective-permute-done.2.az_first
  18.5 1.9 %inner.1 = (f32[1088,128]{1,0:T(8,128)S(1)}, f32[136,256]{1,0:T(8,128)S(1)}, f32[136,256]{1,0:T(8,128)S(1)}, f32[64,256]{1,0:T(8,128)S(1)}, f32[64,256]{1,0:T(8,...) custom-call(f32[4,32,16,256]{3,2,1,0:T(8,128)S(1)} %copy-done.1, f32[144,256]{1,0:T(8,128)S(1)} %collective-permute-done.az_then, ...), custom_call_target="tpu_custom_call" | custom-call | flops 10000000 | bytes 6000000 | tf_op jit(solution)/shard_map/inner/pallas_call | solution.py:388
  20.4 24.0 %all_to_all.10 = f32[64,17,1,128]{3,2,1,0:T(1,128)S(1)} all-to-all(f32[64,17,1,128]{3,2,1,0:T(1,128)S(1)} %bitcast.7), channel_id=1, replica_groups=mesh['y'=4,'x'=2,'z'=8,'hx'=2,'core'=2] {'y','x','z'}, dimensions={0} | all-to-all | bytes 1114112 | tf_op jit(solution)/shard_map/all_to_all | solution.py:400
  44.4 2.1 %filter.1 = f32[1024,128]{1,0:T(8,128)} custom-call(bf16[2,128,544]{2,1,0:T(8,128)(2,1)S(1)} %copy-done.3, bf16[2,128,544]{2,1,0:T(8,128)(2,1)S(1)} %copy-done.2, bf16[2,128,512]{2,1,0:T(8,128)(2,1)S(1)} %copy-done.5, bf16[2,128,512]{2,1,0:T(8,128)(2,1)S(1)} %copy-done.4, f32[2,64,128]{2,1,0:T(8,128)S(1)} %copy-done.6, s32[1,64]{1,0:T(1,128)S(1)} %bitcast.8, ...), custom_call_target="tpu_custom_call" | custom-call | tf_op jit(solution)/shard_map/filter/pallas_call | solution.py:413
  46.5 5.4 %all-to-all-start.1 = ((f32[64,16,128]{2,1,0:T(8,128)}), f32[64,16,128]{2,1,0:T(8,128)S(1)}, u32[]{:S(2)}, u32[]{:S(2)}) async-start(f32[64,16,128]{2,1,0:T(8,128)} %bitcast.3), calls=%async_computation.1 | async-start | bytes 1048576 | tf_op jit(solution)/shard_map/all_to_all | solution.py:416
  51.9 1.5 %collective-permute-start.4 = (f32[8,256]{1,0:T(8,128)S(1)}, f32[8,256]{1,0:T(8,128)S(1)}, u32[]{:S(2)}, u32[]{:S(2)}) collective-permute-start(f32[8,256]{1,0:T(8,128)S(1)} %get-tuple-element.25), channel_id=1, source_target_pairs={{0,4},{4,8},{8,12},{12,16},{16,20},{20,24},{24,28},{28,32},{32,36}... | collective-permute-start | bytes 24584 | tf_op jit(solution)/shard_map/ppermute | solution.py:401
  53.4 0.6 collective-permute-start.5
  54.0 4.3 %outer.1.stepped = f32[4,32,16,256]{3,2,1,0:T(8,128)} custom-call(f32[4,32,16,256]{3,2,1,0:T(8,128)S(1)} %copy-done.1, f32[136,256]{1,0:T(8,128)S(1)} %get-tuple-element.20.low, f32[136,256]{1,0:T(8,128)S(1)} %get-tuple-element.21.high, f32[64,256]{1,0:T(8,128)S(1)} %get-tuple-element.22.left, f32[64,256]{1,0:T(8,128)S(1)} %get-tuple-element.23.right, ...), custom_call_target="tpu_custom_call" | custom-call | flops 20000000 | bytes 20000000 | tf_op jit(solution)/shard_map/outer/pallas_call | solution.py:403
  58.3 3.0 %collective-permute-done.4.left_corner = f32[8,256]{1,0:T(8,128)S(1)} collective-permute-done((f32[8,256]{1,0:T(8,128)S(1)}, f32[8,256]{1,0:T(8,128)S(1)}, u32[]{:S(2)}, u32[]{:S(2)}) %collective-permute-start.4) | collective-permute-done | bytes 8224 | tf_op jit(solution)/shard_map/ppermute | solution.py:401
  61.3 1.3 %collective-permute-done.5.right_corner = f32[8,256]{1,0:T(8,128)S(1)} collective-permute-done((f32[8,256]{1,0:T(8,128)S(1)}, f32[8,256]{1,0:T(8,128)S(1)}, u32[]{:S(2)}, u32[]{:S(2)}) %collective-permute-start.5) | collective-permute-done | bytes 8224 | tf_op jit(solution)/shard_map/ppermute | solution.py:402
  62.6 6.6 %all-to-all-done.1 = f32[64,16,128]{2,1,0:T(8,128)S(1)} async-done(((f32[64,16,128]{2,1,0:T(8,128)}), f32[64,16,128]{2,1,0:T(8,128)S(1)}, u32[]{:S(2)}, u32[]{:S(2)}) %all-to-all-start.1) | async-done | bytes 524320 | tf_op jit(solution)/shard_map/all_to_all | solution.py:416
  69.2 2.2 %merge.1 = f32[4,32,16,256]{3,2,1,0:T(8,128)} custom-call(f32[4,32,16,256]{3,2,1,0:T(8,128)} %outer.1.stepped, f32[1024,128]{1,0:T(8,128)S(1)} %bitcast.6, f32[8,256]{1,0:T(8,128)S(1)} %collective-permute-done.4.left_corner, f32[8,256]{1,0:T(8,128)S(1)} %collective-permute-done.5.right_corner), custom_call_target="tpu_custom_call", output_to_operand_aliasing={{}: (0, {})} | custom-call | tf_op jit(solution)/shard_map/merge/pallas_call | solution.py:417
  (21 shorter events, 0.1 us)
Async XLA Ops:
  0.0 1.6 %copy-start = (f32[4,32,16,256]{3,2,1,0:T(8,128)S(1)}, f32[4,32,16,256]{3,2,1,0:T(8,128)}, u32[]{:S(2)}) copy-start(f32[4,32,16,256]{3,2,1,0:T(8,128)} %state.7) | copy-start | bytes 6291460
  1.6 14.6 %copy-start.10 = (f32[8]{0:T(128)S(1)}, f32[8]{0:T(128)}, u32[]{:S(2)}) copy-start(f32[8]{0:T(128)} %resistance.1) | copy-start | bytes 100
  1.6 14.6 %copy-start.11 = (f32[8]{0:T(128)S(1)}, f32[8]{0:T(128)}, u32[]{:S(2)}) copy-start(f32[8]{0:T(128)} %relax.1) | copy-start | bytes 100
  1.6 16.9 %copy-start.1 = (f32[4,32,16,256]{3,2,1,0:T(8,128)S(1)}, f32[4,32,16,256]{3,2,1,0:T(8,128)}, u32[]{:S(2)}) copy-start(f32[4,32,16,256]{3,2,1,0:T(8,128)} %state.7) | copy-start | bytes 6291460
  1.9 16.6 %collective-permute-start = (f32[144,256]{1,0:T(8,128)S(1)}, f32[144,256]{1,0:T(8,128)S(1)}, u32[]{:S(2)}, u32[]{:S(2)}) collective-permute-start(f32[144,256]{1,0:T(8,128)S(1)} %get-tuple-element.16), channel_id=1, source_target_pairs={{4,8},{12,16},{20,24},{28,32},{36,40},{44,48},{52,56},{60,64},{68,... | collective-permute-start | bytes 442376 | tf_op jit(solution)/shard_map/ppermute | solution.py:378
  3.9 14.6 %collective-permute-start.1 = (f32[136,256]{1,0:T(8,128)S(1)}, f32[136,256]{1,0:T(8,128)S(1)}, u32[]{:S(2)}, u32[]{:S(2)}) collective-permute-start(f32[136,256]{1,0:T(8,128)S(1)} %get-tuple-element.17), channel_id=1, source_target_pairs={{1,2},{2,1},{5,6},{6,5},{9,10},{10,9},{13,14},{14,13},{17,18},{18,... | collective-permute-start | bytes 417800 | tf_op jit(solution)/shard_map/ppermute | solution.py:378
  4.5 14.0 %collective-permute-start.3 = (f32[136,256]{1,0:T(8,128)S(1)}, f32[136,256]{1,0:T(8,128)S(1)}, u32[]{:S(2)}, u32[]{:S(2)}) collective-permute-start(f32[136,256]{1,0:T(8,128)S(1)} %get-tuple-element.19), channel_id=1, source_target_pairs={{0,1},{2,3},{1,0},{3,2},{4,5},{6,7},{5,4},{7,6},{8,9},{10,11},{9,8... | collective-permute-start | bytes 417800 | tf_op jit(solution)/shard_map/ppermute | solution.py:378
  9.0 9.5 %collective-permute-start.2 = (f32[64,256]{1,0:T(8,128)S(1)}, f32[64,256]{1,0:T(8,128)S(1)}, u32[]{:S(2)}, u32[]{:S(2)}) collective-permute-start(f32[64,256]{1,0:T(8,128)S(1)} %get-tuple-element.18), channel_id=1, source_target_pairs={{0,4},{8,12},{16,20},{24,28},{32,36},{40,44},{48,52},{56,60},{64,6... | collective-permute-start | bytes 196616 | tf_op jit(solution)/shard_map/ppermute | solution.py:378
  16.1 0.8 %copy-start.7 = (s32[32,256]{1,0:T(8,128)S(1)}, s32[32,256]{1,0:T(8,128)}, u32[]{:S(2)}) copy-start(s32[32,256]{1,0:T(8,128)} %zone.1) | copy-start | bytes 98308
  16.9 0.8 %copy-start.8 = (f32[32,256]{1,0:T(8,128)S(1)}, f32[32,256]{1,0:T(8,128)}, u32[]{:S(2)}) copy-start(f32[32,256]{1,0:T(8,128)} %aux.1) | copy-start | bytes 98308
  18.3 26.1 %copy-start.2 = (bf16[2,128,544]{2,1,0:T(8,128)(2,1)S(1)}, bf16[2,128,544]{2,1,0:T(8,128)(2,1)}, u32[]{:S(2)}) copy-start(bf16[2,128,544]{2,1,0:T(8,128)(2,1)} %constant.11.clone.there_small) | copy-start | bytes 835588
  18.3 26.1 %copy-start.3 = (bf16[2,128,544]{2,1,0:T(8,128)(2,1)S(1)}, bf16[2,128,544]{2,1,0:T(8,128)(2,1)}, u32[]{:S(2)}) copy-start(bf16[2,128,544]{2,1,0:T(8,128)(2,1)} %constant.10.clone.there) | copy-start | bytes 835588
  18.3 26.1 %copy-start.4 = (bf16[2,128,512]{2,1,0:T(8,128)(2,1)S(1)}, bf16[2,128,512]{2,1,0:T(8,128)(2,1)}, u32[]{:S(2)}) copy-start(bf16[2,128,512]{2,1,0:T(8,128)(2,1)} %constant.13.clone.back_small) | copy-start | bytes 786436
  18.3 26.1 %copy-start.5 = (bf16[2,128,512]{2,1,0:T(8,128)(2,1)S(1)}, bf16[2,128,512]{2,1,0:T(8,128)(2,1)}, u32[]{:S(2)}) copy-start(bf16[2,128,512]{2,1,0:T(8,128)(2,1)} %constant.12.clone.back) | copy-start | bytes 786436
  18.3 26.1 %copy-start.6 = (f32[2,64,128]{2,1,0:T(8,128)S(1)}, f32[2,64,128]{2,1,0:T(8,128)}, u32[]{:S(2)}) copy-start(f32[2,64,128]{2,1,0:T(8,128)} %constant.14.clone.turn) | copy-start | bytes 196612
  18.3 26.0 %copy-start.9 = (s32[64]{0:T(128)S(1)}, s32[64]{0:T(128)}, u32[]{:S(2)}) copy-start(s32[64]{0:T(128)} %param.16) | copy-start | bytes 772
  46.5 22.7 %all-to-all-start.1 = ((f32[64,16,128]{2,1,0:T(8,128)}), f32[64,16,128]{2,1,0:T(8,128)S(1)}, u32[]{:S(2)}, u32[]{:S(2)}) async-start(f32[64,16,128]{2,1,0:T(8,128)} %bitcast.3), calls=%async_computation.1 | async-start | bytes 1048576 | tf_op jit(solution)/shard_map/all_to_all | solution.py:416
  51.9 9.4 %collective-permute-start.4 = (f32[8,256]{1,0:T(8,128)S(1)}, f32[8,256]{1,0:T(8,128)S(1)}, u32[]{:S(2)}, u32[]{:S(2)}) collective-permute-start(f32[8,256]{1,0:T(8,128)S(1)} %get-tuple-element.25), channel_id=1, source_target_pairs={{0,4},{4,8},{8,12},{12,16},{16,20},{20,24},{24,28},{28,32},{32,36}... | collective-permute-start | bytes 24584 | tf_op jit(solution)/shard_map/ppermute | solution.py:401
  53.4 9.2 %collective-permute-start.5 = (f32[8,256]{1,0:T(8,128)S(1)}, f32[8,256]{1,0:T(8,128)S(1)}, u32[]{:S(2)}, u32[]{:S(2)}) collective-permute-start(f32[8,256]{1,0:T(8,128)S(1)} %get-tuple-element.26), channel_id=1, source_target_pairs={{4,0},{8,4},{12,8},{16,12},{20,16},{24,20},{28,24},{32,28},{36,32}... | collective-permute-start | bytes 24584 | tf_op jit(solution)/shard_map/ppermute | solution.py:402

commit v10 on v9

--- a/solution.py
+++ b/solution.py
@@ -112,7 +112,7 @@
 AZ_LONG = 144
 
 
-def pack_kernel(state, az_then, ht_then, az_first, ht_first, up, down, to_left, to_right):
+def pack_kernel(state, az_then, ht_first, az_first, ht_then, up, down, to_left, to_right):
     inv_r, half_arc = radial_rates(NR)
     zero = jnp.zeros((1, NR), jnp.float32)
     for out, edge, inside, sign in ((up, HTS - 1, HTS - 2, 1.0), (down, 0, 1, -1.0)):
@@ -226,7 +226,7 @@
 
 
 def inner_kernel(
-    state, az_then, ht_then, az_first, ht_first, ground, packed, low, high, left, right, to_left, to_right, mid, ghost
+    state, az_then, ht_first, az_first, ht_then, ground, packed, low, high, left, right, to_left, to_right, mid, ghost
 ):
     unswap(odd_slab(), ht_first, ht_then, low, high)
     unswap(odd_sector(), az_first, az_then.at[0:AZ_ROWS], left, right)
@@ -358,7 +358,7 @@
         return tuple(jax.ShapeDtypeStruct(d, f32) for d in dims)
 
     ht_message, az_message = (HT_ROWS, NR), (AZ_ROWS, NR)
-    az_then, ht_then, az_first, ht_first = call(
+    az_then, ht_first, az_first, ht_then = call(
         pack_kernel,
         out_shape=shapes((AZ_LONG, NR), ht_message, az_message, ht_message),
         in_specs=[vmem],
@@ -396,7 +396,7 @@
         scratch_shapes=scratch(128),
         cost_estimate=pl.CostEstimate(flops=10**7, bytes_accessed=6 * 10**6, transcendentals=0),
         name="inner",
-    )(state, az_then, ht_then, az_first, ht_first, ground)
+    )(state, az_then, ht_first, az_first, ht_then, ground)
     circle = lax.all_to_all(packed.reshape(SECTORS, LONG, 1, 128), SPREAD, 0, 0, tiled=True)
     left_corner = lax.ppermute(to_right, AZ, [(i, (i + 1) % SECTORS) for i in range(SECTORS)])
     right_corner = lax.ppermute(to_left, AZ, [((i + 1) % SECTORS, i) for i in range(SECTORS)])

time: 71.8 us -> 72.6 us (1.011)
  blocking collectives: 24 us -> 28.2 us
  starting transfers between devices: 21.8 us -> 17.8 us
    all_to_all x1, blocking collectives: 24 us -> 28.2 us  [per_device(): lax.all_to_all(packed.reshape(SECTORS, LONG, 1, 128), SPREAD, 0, 0, tiled...]
    ppermute x4, starting transfers between devices: 14.3 us -> 10.2 us  [swap(): return lax.ppermute(x, axes, pairs + [(b, a) for a, b in pairs])]
  transfers between devices with their start and end apart: 7 -> 7, of which waited for: 4 -> 3; matrix products, arithmetic and copies ran while one was open for 0% -> 0% of each run, Pallas kernels for 7% -> 7%
where the time goes in v10:
time: 72.6 us; the launch traced here: 72.2 us
  blocking collectives  28.2 us (39%)
  starting transfers between devices  17.8 us (25%)
  waiting for transfers between devices  11.6 us (16%)
  Pallas kernels  11.3 us (16%)
  local copies, waits for them, and re-layouts  3.16 us (4%)
    all_to_all x1, blocking collectives, per_device(): lax.all_to_all(packed.reshape(SECTORS, LONG, 1, 128), SPREAD, 0, 0, tiled...  28.2 us
    ppermute x4, starting transfers between devices, swap(): return lax.ppermute(x, axes, pairs + [(b, a) for a, b in pairs])  10.2 us
    all_to_all x1, waiting for transfers between devices, per_device(): lax.all_to_all(kept.reshape(SECTORS, HALF, 128), SPREAD, 0, 0, tiled=True)  6.5 us
    all_to_all x1, starting transfers between devices, per_device(): lax.all_to_all(kept.reshape(SECTORS, HALF, 128), SPREAD, 0, 0, tiled=True)  5.53 us
    pallas_call x1, Pallas kernels, per_device(): call(outer_kernel, mib=16, out_shape=shapes((COMPS, ROWS, HTS, NR))[0], i...  4.28 us
    ppermute x1, waiting for transfers between devices, per_device(): lax.ppermute(to_right, AZ, [(i, (i + 1) % SECTORS) for i in range(SECTORS)])  3.49 us
    unnamed x24, local copies, waits for them, and re-layouts  3.16 us
    pallas_call x1, Pallas kernels, per_device(): call(merge_kernel, out_shape=jax.ShapeDtypeStruct(stepped.shape, f32), in...  2.21 us
  transfers between devices with their start and end apart: 7, of which 3 were waited for; matrix products, arithmetic and copies ran while one was open for 0% of the time, Pallas kernels for 7%

profile of v10, /device:TPU:32, one launch (start us, length us, event | category | flops | bytes accessed | tf_op | source)
XLA Modules:
  0.0 72.2 jit_solution(12908388755018639289)
XLA Ops:
  0.0 1.6 %copy-done = f32[4,32,16,256]{3,2,1,0:T(8,128)S(1)} copy-done((f32[4,32,16,256]{3,2,1,0:T(8,128)S(1)}, f32[4,32,16,256]{3,2,1,0:T(8,128)}, u32[]{:S(2)}) %copy-start) | copy-done | bytes 2097176
  1.6 0.3 pack.1
  1.9 2.0 %collective-permute-start = (f32[144,256]{1,0:T(8,128)S(1)}, f32[144,256]{1,0:T(8,128)S(1)}, u32[]{:S(2)}, u32[]{:S(2)}) collective-permute-start(f32[144,256]{1,0:T(8,128)S(1)} %get-tuple-element.16), channel_id=1, source_target_pairs={{4,8},{12,16},{20,24},{28,32},{36,40},{44,48},{52,56},{60,64},{68,... | collective-permute-start | bytes 442376 | tf_op jit(solution)/shard_map/ppermute | solution.py:378
  3.9 0.7 collective-permute-start.3
  4.6 7.5 %collective-permute-start.2 = (f32[64,256]{1,0:T(8,128)S(1)}, f32[64,256]{1,0:T(8,128)S(1)}, u32[]{:S(2)}, u32[]{:S(2)}) collective-permute-start(f32[64,256]{1,0:T(8,128)S(1)} %get-tuple-element.18), channel_id=1, source_target_pairs={{0,4},{8,12},{16,20},{24,28},{32,36},{40,44},{48,52},{56,60},{64,6... | collective-permute-start | bytes 196616 | tf_op jit(solution)/shard_map/ppermute | solution.py:378
  12.1 0.8 %copy-done.7 = s32[32,256]{1,0:T(8,128)S(1)} copy-done((s32[32,256]{1,0:T(8,128)S(1)}, s32[32,256]{1,0:T(8,128)}, u32[]{:S(2)}) %copy-start.7) | copy-done | bytes 32792
  12.8 0.8 %copy-done.8 = f32[32,256]{1,0:T(8,128)S(1)} copy-done((f32[32,256]{1,0:T(8,128)S(1)}, f32[32,256]{1,0:T(8,128)}, u32[]{:S(2)}) %copy-start.8) | copy-done | bytes 32792
  13.6 0.6 ground.1
  14.2 0.0 copy-start.2
  14.2 0.0 copy-start.3
  14.2 0.0 copy-start.4
  14.3 0.0 copy-start.6
  14.3 0.0 collective-permute-done.2.az_first
  14.3 1.9 %inner.1 = (f32[1088,128]{1,0:T(8,128)S(1)}, f32[136,256]{1,0:T(8,128)S(1)}, f32[136,256]{1,0:T(8,128)S(1)}, f32[64,256]{1,0:T(8,128)S(1)}, f32[64,256]{1,0:T(8,...) custom-call(f32[4,32,16,256]{3,2,1,0:T(8,128)S(1)} %copy-done.1, f32[144,256]{1,0:T(8,128)S(1)} %collective-permute-done.az_then, ...), custom_call_target="tpu_custom_call" | custom-call | flops 10000000 | bytes 6000000 | tf_op jit(solution)/shard_map/inner/pallas_call | solution.py:388
  16.2 28.2 %all_to_all.10 = f32[64,17,1,128]{3,2,1,0:T(1,128)S(1)} all-to-all(f32[64,17,1,128]{3,2,1,0:T(1,128)S(1)} %bitcast.7), channel_id=1, replica_groups=mesh['y'=4,'x'=2,'z'=8,'hx'=2,'core'=2] {'y','x','z'}, dimensions={0} | all-to-all | bytes 1114112 | tf_op jit(solution)/shard_map/all_to_all | solution.py:400
  44.4 2.1 %filter.1 = f32[1024,128]{1,0:T(8,128)} custom-call(bf16[2,128,544]{2,1,0:T(8,128)(2,1)S(1)} %copy-done.3, bf16[2,128,544]{2,1,0:T(8,128)(2,1)S(1)} %copy-done.2, bf16[2,128,512]{2,1,0:T(8,128)(2,1)S(1)} %copy-done.5, bf16[2,128,512]{2,1,0:T(8,128)(2,1)S(1)} %copy-done.4, f32[2,64,128]{2,1,0:T(8,128)S(1)} %copy-done.6, s32[1,64]{1,0:T(1,128)S(1)} %bitcast.8, ...), custom_call_target="tpu_custom_call" | custom-call | tf_op jit(solution)/shard_map/filter/pallas_call | solution.py:413
  46.5 5.5 %all-to-all-start.1 = ((f32[64,16,128]{2,1,0:T(8,128)}), f32[64,16,128]{2,1,0:T(8,128)S(1)}, u32[]{:S(2)}, u32[]{:S(2)}) async-start(f32[64,16,128]{2,1,0:T(8,128)} %bitcast.3), calls=%async_computation.1 | async-start | bytes 1048576 | tf_op jit(solution)/shard_map/all_to_all | solution.py:416
  52.0 1.5 %collective-permute-start.4 = (f32[8,256]{1,0:T(8,128)S(1)}, f32[8,256]{1,0:T(8,128)S(1)}, u32[]{:S(2)}, u32[]{:S(2)}) collective-permute-start(f32[8,256]{1,0:T(8,128)S(1)} %get-tuple-element.25), channel_id=1, source_target_pairs={{0,4},{4,8},{8,12},{12,16},{16,20},{20,24},{24,28},{28,32},{32,36}... | collective-permute-start | bytes 24584 | tf_op jit(solution)/shard_map/ppermute | solution.py:401
  53.6 0.6 collective-permute-start.5
  54.1 4.3 %outer.1.stepped = f32[4,32,16,256]{3,2,1,0:T(8,128)} custom-call(f32[4,32,16,256]{3,2,1,0:T(8,128)S(1)} %copy-done.1, f32[136,256]{1,0:T(8,128)S(1)} %get-tuple-element.20.low, f32[136,256]{1,0:T(8,128)S(1)} %get-tuple-element.21.high, f32[64,256]{1,0:T(8,128)S(1)} %get-tuple-element.22.left, f32[64,256]{1,0:T(8,128)S(1)} %get-tuple-element.23.right, ...), custom_call_target="tpu_custom_call" | custom-call | flops 20000000 | bytes 20000000 | tf_op jit(solution)/shard_map/outer/pallas_call | solution.py:403
  58.4 3.5 %collective-permute-done.4.left_corner = f32[8,256]{1,0:T(8,128)S(1)} collective-permute-done((f32[8,256]{1,0:T(8,128)S(1)}, f32[8,256]{1,0:T(8,128)S(1)}, u32[]{:S(2)}, u32[]{:S(2)}) %collective-permute-start.4) | collective-permute-done | bytes 8224 | tf_op jit(solution)/shard_map/ppermute | solution.py:401
  61.9 1.5 %collective-permute-done.5.right_corner = f32[8,256]{1,0:T(8,128)S(1)} collective-permute-done((f32[8,256]{1,0:T(8,128)S(1)}, f32[8,256]{1,0:T(8,128)S(1)}, u32[]{:S(2)}, u32[]{:S(2)}) %collective-permute-start.5) | collective-permute-done | bytes 8224 | tf_op jit(solution)/shard_map/ppermute | solution.py:402
  63.4 6.5 %all-to-all-done.1 = f32[64,16,128]{2,1,0:T(8,128)S(1)} async-done(((f32[64,16,128]{2,1,0:T(8,128)}), f32[64,16,128]{2,1,0:T(8,128)S(1)}, u32[]{:S(2)}, u32[]{:S(2)}) %all-to-all-start.1) | async-done | bytes 524320 | tf_op jit(solution)/shard_map/all_to_all | solution.py:416
  69.9 2.2 %merge.1 = f32[4,32,16,256]{3,2,1,0:T(8,128)} custom-call(f32[4,32,16,256]{3,2,1,0:T(8,128)} %outer.1.stepped, f32[1024,128]{1,0:T(8,128)S(1)} %bitcast.6, f32[8,256]{1,0:T(8,128)S(1)} %collective-permute-done.4.left_corner, f32[8,256]{1,0:T(8,128)S(1)} %collective-permute-done.5.right_corner), custom_call_target="tpu_custom_call", output_to_operand_aliasing={{}: (0, {})} | custom-call | tf_op jit(solution)/shard_map/merge/pallas_call | solution.py:417
  (21 shorter events, 0.0 us)
Async XLA Ops:
  0.0 1.6 %copy-start = (f32[4,32,16,256]{3,2,1,0:T(8,128)S(1)}, f32[4,32,16,256]{3,2,1,0:T(8,128)}, u32[]{:S(2)}) copy-start(f32[4,32,16,256]{3,2,1,0:T(8,128)} %state.7) | copy-start | bytes 6291460
  1.6 10.5 %copy-start.10 = (f32[8]{0:T(128)S(1)}, f32[8]{0:T(128)}, u32[]{:S(2)}) copy-start(f32[8]{0:T(128)} %resistance.1) | copy-start | bytes 100
  1.6 10.5 %copy-start.11 = (f32[8]{0:T(128)S(1)}, f32[8]{0:T(128)}, u32[]{:S(2)}) copy-start(f32[8]{0:T(128)} %relax.1) | copy-start | bytes 100
  1.6 12.7 %copy-start.1 = (f32[4,32,16,256]{3,2,1,0:T(8,128)S(1)}, f32[4,32,16,256]{3,2,1,0:T(8,128)}, u32[]{:S(2)}) copy-start(f32[4,32,16,256]{3,2,1,0:T(8,128)} %state.7) | copy-start | bytes 6291460
  1.9 12.4 %collective-permute-start = (f32[144,256]{1,0:T(8,128)S(1)}, f32[144,256]{1,0:T(8,128)S(1)}, u32[]{:S(2)}, u32[]{:S(2)}) collective-permute-start(f32[144,256]{1,0:T(8,128)S(1)} %get-tuple-element.16), channel_id=1, source_target_pairs={{4,8},{12,16},{20,24},{28,32},{36,40},{44,48},{52,56},{60,64},{68,... | collective-permute-start | bytes 442376 | tf_op jit(solution)/shard_map/ppermute | solution.py:378
  3.9 10.4 %collective-permute-start.1 = (f32[136,256]{1,0:T(8,128)S(1)}, f32[136,256]{1,0:T(8,128)S(1)}, u32[]{:S(2)}, u32[]{:S(2)}) collective-permute-start(f32[136,256]{1,0:T(8,128)S(1)} %get-tuple-element.17), channel_id=1, source_target_pairs={{0,1},{2,3},{1,0},{3,2},{4,5},{6,7},{5,4},{7,6},{8,9},{10,11},{9,8... | collective-permute-start | bytes 417800 | tf_op jit(solution)/shard_map/ppermute | solution.py:378
  3.9 10.4 %collective-permute-start.3 = (f32[136,256]{1,0:T(8,128)S(1)}, f32[136,256]{1,0:T(8,128)S(1)}, u32[]{:S(2)}, u32[]{:S(2)}) collective-permute-start(f32[136,256]{1,0:T(8,128)S(1)} %get-tuple-element.19), channel_id=1, source_target_pairs={{1,2},{2,1},{5,6},{6,5},{9,10},{10,9},{13,14},{14,13},{17,18},{18,... | collective-permute-start | bytes 417800 | tf_op jit(solution)/shard_map/ppermute | solution.py:378
  4.6 9.8 %collective-permute-start.2 = (f32[64,256]{1,0:T(8,128)S(1)}, f32[64,256]{1,0:T(8,128)S(1)}, u32[]{:S(2)}, u32[]{:S(2)}) collective-permute-start(f32[64,256]{1,0:T(8,128)S(1)} %get-tuple-element.18), channel_id=1, source_target_pairs={{0,4},{8,12},{16,20},{24,28},{32,36},{40,44},{48,52},{56,60},{64,6... | collective-permute-start | bytes 196616 | tf_op jit(solution)/shard_map/ppermute | solution.py:378
  12.1 0.8 %copy-start.7 = (s32[32,256]{1,0:T(8,128)S(1)}, s32[32,256]{1,0:T(8,128)}, u32[]{:S(2)}) copy-start(s32[32,256]{1,0:T(8,128)} %zone.1) | copy-start | bytes 98308
  12.8 0.8 %copy-start.8 = (f32[32,256]{1,0:T(8,128)S(1)}, f32[32,256]{1,0:T(8,128)}, u32[]{:S(2)}) copy-start(f32[32,256]{1,0:T(8,128)} %aux.1) | copy-start | bytes 98308
  14.2 30.2 %copy-start.2 = (bf16[2,128,544]{2,1,0:T(8,128)(2,1)S(1)}, bf16[2,128,544]{2,1,0:T(8,128)(2,1)}, u32[]{:S(2)}) copy-start(bf16[2,128,544]{2,1,0:T(8,128)(2,1)} %constant.11.clone.there_small) | copy-start | bytes 835588
  14.2 30.2 %copy-start.3 = (bf16[2,128,544]{2,1,0:T(8,128)(2,1)S(1)}, bf16[2,128,544]{2,1,0:T(8,128)(2,1)}, u32[]{:S(2)}) copy-start(bf16[2,128,544]{2,1,0:T(8,128)(2,1)} %constant.10.clone.there) | copy-start | bytes 835588
  14.2 30.1 %copy-start.4 = (bf16[2,128,512]{2,1,0:T(8,128)(2,1)S(1)}, bf16[2,128,512]{2,1,0:T(8,128)(2,1)}, u32[]{:S(2)}) copy-start(bf16[2,128,512]{2,1,0:T(8,128)(2,1)} %constant.13.clone.back_small) | copy-start | bytes 786436
  14.2 30.1 %copy-start.5 = (bf16[2,128,512]{2,1,0:T(8,128)(2,1)S(1)}, bf16[2,128,512]{2,1,0:T(8,128)(2,1)}, u32[]{:S(2)}) copy-start(bf16[2,128,512]{2,1,0:T(8,128)(2,1)} %constant.12.clone.back) | copy-start | bytes 786436
  14.3 30.1 %copy-start.6 = (f32[2,64,128]{2,1,0:T(8,128)S(1)}, f32[2,64,128]{2,1,0:T(8,128)}, u32[]{:S(2)}) copy-start(f32[2,64,128]{2,1,0:T(8,128)} %constant.14.clone.turn) | copy-start | bytes 196612
  14.3 30.1 %copy-start.9 = (s32[64]{0:T(128)S(1)}, s32[64]{0:T(128)}, u32[]{:S(2)}) copy-start(s32[64]{0:T(128)} %param.16) | copy-start | bytes 772
  46.5 23.5 %all-to-all-start.1 = ((f32[64,16,128]{2,1,0:T(8,128)}), f32[64,16,128]{2,1,0:T(8,128)S(1)}, u32[]{:S(2)}, u32[]{:S(2)}) async-start(f32[64,16,128]{2,1,0:T(8,128)} %bitcast.3), calls=%async_computation.1 | async-start | bytes 1048576 | tf_op jit(solution)/shard_map/all_to_all | solution.py:416
  52.0 9.9 %collective-permute-start.4 = (f32[8,256]{1,0:T(8,128)S(1)}, f32[8,256]{1,0:T(8,128)S(1)}, u32[]{:S(2)}, u32[]{:S(2)}) collective-permute-start(f32[8,256]{1,0:T(8,128)S(1)} %get-tuple-element.25), channel_id=1, source_target_pairs={{0,4},{4,8},{8,12},{12,16},{16,20},{20,24},{24,28},{28,32},{32,36}... | collective-permute-start | bytes 24584 | tf_op jit(solution)/shard_map/ppermute | solution.py:401
  53.6 9.9 %collective-permute-start.5 = (f32[8,256]{1,0:T(8,128)S(1)}, f32[8,256]{1,0:T(8,128)S(1)}, u32[]{:S(2)}, u32[]{:S(2)}) collective-permute-start(f32[8,256]{1,0:T(8,128)S(1)} %get-tuple-element.26), channel_id=1, source_target_pairs={{4,0},{8,4},{12,8},{16,12},{20,16},{24,20},{28,24},{32,28},{36,32}... | collective-permute-start | bytes 24584 | tf_op jit(solution)/shard_map/ppermute | solution.py:402

commit v11 on v10

--- a/solution.py
+++ b/solution.py
@@ -112,7 +112,7 @@
 AZ_LONG = 144
 
 
-def pack_kernel(state, az_then, ht_first, az_first, ht_then, up, down, to_left, to_right):
+def pack_kernel(state, az_first, az_then, ht_then, ht_first, up, down, to_left, to_right):
     inv_r, half_arc = radial_rates(NR)
     zero = jnp.zeros((1, NR), jnp.float32)
     for out, edge, inside, sign in ((up, HTS - 1, HTS - 2, 1.0), (down, 0, 1, -1.0)):
@@ -137,11 +137,12 @@
 
     for odd, one, two, ahead, behind in (
         (odd_slab(), ht_first, ht_then, up, down),
-        (odd_sector(), az_first, az_then.at[0:AZ_ROWS], to_right, to_left),
+        (odd_sector(), az_first.at[0:AZ_ROWS], az_then.at[0:AZ_ROWS], to_right, to_left),
     ):
         one[...] = jnp.where(odd, behind[...], ahead[...])
         two[...] = jnp.where(odd, ahead[...], behind[...])
-    az_then[AZ_ROWS:AZ_LONG] = jnp.zeros((AZ_LONG - AZ_ROWS, NR), jnp.float32)
+    for out in (az_first, az_then):
+        out[AZ_ROWS:AZ_LONG] = jnp.zeros((AZ_LONG - AZ_ROWS, NR), jnp.float32)
 
 
 def ground_kernel(resistance, relax, state, zone, aux, ground):
@@ -226,10 +227,10 @@
 
 
 def inner_kernel(
-    state, az_then, ht_first, az_first, ht_then, ground, packed, low, high, left, right, to_left, to_right, mid, ghost
+    state, az_first, az_then, ht_then, ht_first, ground, packed, low, high, left, right, to_left, to_right, mid, ghost
 ):
     unswap(odd_slab(), ht_first, ht_then, low, high)
-    unswap(odd_sector(), az_first, az_then.at[0:AZ_ROWS], left, right)
+    unswap(odd_sector(), az_first.at[0:AZ_ROWS], az_then.at[0:AZ_ROWS], left, right)
     near = lax.broadcasted_iota(jnp.int32, (HTS, 128), 1) < NI
     height = lax.broadcasted_iota(jnp.int32, (HTS, 128), 0)
     second = two_stages(128, state, low, high, left, right, ground, mid, ghost)
@@ -358,9 +359,9 @@
         return tuple(jax.ShapeDtypeStruct(d, f32) for d in dims)
 
     ht_message, az_message = (HT_ROWS, NR), (AZ_ROWS, NR)
-    az_then, ht_first, az_first, ht_then = call(
+    az_first, az_then, ht_then, ht_first = call(
         pack_kernel,
-        out_shape=shapes((AZ_LONG, NR), ht_message, az_message, ht_message),
+        out_shape=shapes((AZ_LONG, NR), (AZ_LONG, NR), ht_message, ht_message),
         in_specs=[vmem],
         out_specs=(vmem,) * 4,
         scratch_shapes=[pltpu.VMEM(m, f32) for m in (ht_message, ht_message, az_message, az_message)],
@@ -396,7 +397,7 @@
         scratch_shapes=scratch(128),
         cost_estimate=pl.CostEstimate(flops=10**7, bytes_accessed=6 * 10**6, transcendentals=0),
         name="inner",
-    )(state, az_then, ht_first, az_first, ht_then, ground)
+    )(state, az_first, az_then, ht_then, ht_first, ground)
     circle = lax.all_to_all(packed.reshape(SECTORS, LONG, 1, 128), SPREAD, 0, 0, tiled=True)
     left_corner = lax.ppermute(to_right, AZ, [(i, (i + 1) % SECTORS) for i in range(SECTORS)])
     right_corner = lax.ppermute(to_left, AZ, [((i + 1) % SECTORS, i) for i in range(SECTORS)])

time: 72.6 us -> 73.2 us (level)
  blocking collectives: 28.2 us -> 30 us
  starting transfers between devices: 17.8 us -> 16.6 us
    all_to_all x1, blocking collectives: 28.2 us -> 30 us  [per_device(): lax.all_to_all(packed.reshape(SECTORS, LONG, 1, 128), SPREAD, 0, 0, tiled...]
    ppermute x4, starting transfers between devices: 10.2 us -> 9.04 us  [swap(): return lax.ppermute(x, axes, pairs + [(b, a) for a, b in pairs])]
where the time goes in v11:
time: 73.2 us; the launch traced here: 72.8 us
  blocking collectives  30 us (41%)
  starting transfers between devices  16.6 us (23%)
  waiting for transfers between devices  11.5 us (16%)
  Pallas kernels  11.3 us (15%)
  local copies, waits for them, and re-layouts  3.16 us (4%)
    all_to_all x1, blocking collectives, per_device(): lax.all_to_all(packed.reshape(SECTORS, LONG, 1, 128), SPREAD, 0, 0, tiled...  30 us
    ppermute x4, starting transfers between devices, swap(): return lax.ppermute(x, axes, pairs + [(b, a) for a, b in pairs])  9.04 us
    all_to_all x1, waiting for transfers between devices, per_device(): lax.all_to_all(kept.reshape(SECTORS, HALF, 128), SPREAD, 0, 0, tiled=True)  6.5 us
    all_to_all x1, starting transfers between devices, per_device(): lax.all_to_all(kept.reshape(SECTORS, HALF, 128), SPREAD, 0, 0, tiled=True)  5.49 us
    pallas_call x1, Pallas kernels, per_device(): call(outer_kernel, mib=16, out_shape=shapes((COMPS, ROWS, HTS, NR))[0], i...  4.28 us
    ppermute x1, waiting for transfers between devices, per_device(): lax.ppermute(to_right, AZ, [(i, (i + 1) % SECTORS) for i in range(SECTORS)])  3.47 us
    unnamed x24, local copies, waits for them, and re-layouts  3.16 us
    pallas_call x1, Pallas kernels, per_device(): call(merge_kernel, out_shape=jax.ShapeDtypeStruct(stepped.shape, f32), in...  2.21 us
  transfers between devices with their start and end apart: 7, of which 3 were waited for; matrix products, arithmetic and copies ran while one was open for 0% of the time, Pallas kernels for 7%

profile of v11, /device:TPU:32, one launch (start us, length us, event | category | flops | bytes accessed | tf_op | source)
XLA Modules:
  0.0 72.8 jit_solution(4924784007959164222)
XLA Ops:
  0.0 1.6 %copy-done = f32[4,32,16,256]{3,2,1,0:T(8,128)S(1)} copy-done((f32[4,32,16,256]{3,2,1,0:T(8,128)S(1)}, f32[4,32,16,256]{3,2,1,0:T(8,128)}, u32[]{:S(2)}) %copy-start) | copy-done | bytes 2097176
  1.6 0.3 pack.1
  1.9 1.9 %collective-permute-start = (f32[144,256]{1,0:T(8,128)S(1)}, f32[144,256]{1,0:T(8,128)S(1)}, u32[]{:S(2)}, u32[]{:S(2)}) collective-permute-start(f32[144,256]{1,0:T(8,128)S(1)} %get-tuple-element.16), channel_id=1, source_target_pairs={{0,4},{8,12},{16,20},{24,28},{32,36},{40,44},{48,52},{56,60},{64,6... | collective-permute-start | bytes 442376 | tf_op jit(solution)/shard_map/ppermute | solution.py:379
  3.8 2.0 %collective-permute-start.1 = (f32[144,256]{1,0:T(8,128)S(1)}, f32[144,256]{1,0:T(8,128)S(1)}, u32[]{:S(2)}, u32[]{:S(2)}) collective-permute-start(f32[144,256]{1,0:T(8,128)S(1)} %get-tuple-element.17), channel_id=1, source_target_pairs={{4,8},{12,16},{20,24},{28,32},{36,40},{44,48},{52,56},{60,64},{68,... | collective-permute-start | bytes 442376 | tf_op jit(solution)/shard_map/ppermute | solution.py:379
  5.8 0.7 collective-permute-start.2
  6.5 4.5 %collective-permute-start.3 = (f32[136,256]{1,0:T(8,128)S(1)}, f32[136,256]{1,0:T(8,128)S(1)}, u32[]{:S(2)}, u32[]{:S(2)}) collective-permute-start(f32[136,256]{1,0:T(8,128)S(1)} %get-tuple-element.19), channel_id=1, source_target_pairs={{0,1},{2,3},{1,0},{3,2},{4,5},{6,7},{5,4},{7,6},{8,9},{10,11},{9,8... | collective-permute-start | bytes 417800 | tf_op jit(solution)/shard_map/ppermute | solution.py:379
  10.9 0.8 %copy-done.7 = s32[32,256]{1,0:T(8,128)S(1)} copy-done((s32[32,256]{1,0:T(8,128)S(1)}, s32[32,256]{1,0:T(8,128)}, u32[]{:S(2)}) %copy-start.7) | copy-done | bytes 32792
  11.7 0.8 %copy-done.8 = f32[32,256]{1,0:T(8,128)S(1)} copy-done((f32[32,256]{1,0:T(8,128)S(1)}, f32[32,256]{1,0:T(8,128)}, u32[]{:S(2)}) %copy-start.8) | copy-done | bytes 32792
  12.5 0.6 ground.1
  13.1 0.0 copy-start.3
  13.1 0.0 copy-start.4
  13.1 0.0 copy-start.5
  13.1 0.0 copy-start.6
  13.2 1.9 %inner.1 = (f32[1088,128]{1,0:T(8,128)S(1)}, f32[136,256]{1,0:T(8,128)S(1)}, f32[136,256]{1,0:T(8,128)S(1)}, f32[64,256]{1,0:T(8,128)S(1)}, f32[64,256]{1,0:T(8,...) custom-call(f32[4,32,16,256]{3,2,1,0:T(8,128)S(1)} %copy-done.1, f32[144,256]{1,0:T(8,128)S(1)} %collective-permute-done.az_first, ...), custom_call_target="tpu_custom_call" | custom-call | flops 10000000 | bytes 6000000 | tf_op jit(solution)/shard_map/inner/pallas_call | solution.py:389
  15.1 30.0 %all_to_all.10 = f32[64,17,1,128]{3,2,1,0:T(1,128)S(1)} all-to-all(f32[64,17,1,128]{3,2,1,0:T(1,128)S(1)} %bitcast.7), channel_id=1, replica_groups=mesh['y'=4,'x'=2,'z'=8,'hx'=2,'core'=2] {'y','x','z'}, dimensions={0} | all-to-all | bytes 1114112 | tf_op jit(solution)/shard_map/all_to_all | solution.py:401
  45.1 2.1 %filter.1 = f32[1024,128]{1,0:T(8,128)} custom-call(bf16[2,128,544]{2,1,0:T(8,128)(2,1)S(1)} %copy-done.3, bf16[2,128,544]{2,1,0:T(8,128)(2,1)S(1)} %copy-done.2, bf16[2,128,512]{2,1,0:T(8,128)(2,1)S(1)} %copy-done.5, bf16[2,128,512]{2,1,0:T(8,128)(2,1)S(1)} %copy-done.4, f32[2,64,128]{2,1,0:T(8,128)S(1)} %copy-done.6, s32[1,64]{1,0:T(1,128)S(1)} %bitcast.8, ...), custom_call_target="tpu_custom_call" | custom-call | tf_op jit(solution)/shard_map/filter/pallas_call | solution.py:414
  47.2 5.5 %all-to-all-start.1 = ((f32[64,16,128]{2,1,0:T(8,128)}), f32[64,16,128]{2,1,0:T(8,128)S(1)}, u32[]{:S(2)}, u32[]{:S(2)}) async-start(f32[64,16,128]{2,1,0:T(8,128)} %bitcast.3), calls=%async_computation.1 | async-start | bytes 1048576 | tf_op jit(solution)/shard_map/all_to_all | solution.py:417
  52.7 1.5 %collective-permute-start.4 = (f32[8,256]{1,0:T(8,128)S(1)}, f32[8,256]{1,0:T(8,128)S(1)}, u32[]{:S(2)}, u32[]{:S(2)}) collective-permute-start(f32[8,256]{1,0:T(8,128)S(1)} %get-tuple-element.25), channel_id=1, source_target_pairs={{0,4},{4,8},{8,12},{12,16},{16,20},{20,24},{24,28},{28,32},{32,36}... | collective-permute-start | bytes 24584 | tf_op jit(solution)/shard_map/ppermute | solution.py:402
  54.2 0.6 collective-permute-start.5
  54.8 4.3 %outer.1.stepped = f32[4,32,16,256]{3,2,1,0:T(8,128)} custom-call(f32[4,32,16,256]{3,2,1,0:T(8,128)S(1)} %copy-done.1, f32[136,256]{1,0:T(8,128)S(1)} %get-tuple-element.20.low, f32[136,256]{1,0:T(8,128)S(1)} %get-tuple-element.21.high, f32[64,256]{1,0:T(8,128)S(1)} %get-tuple-element.22.left, f32[64,256]{1,0:T(8,128)S(1)} %get-tuple-element.23.right, ...), custom_call_target="tpu_custom_call" | custom-call | flops 20000000 | bytes 20000000 | tf_op jit(solution)/shard_map/outer/pallas_call | solution.py:404
  59.0 3.5 %collective-permute-done.4.left_corner = f32[8,256]{1,0:T(8,128)S(1)} collective-permute-done((f32[8,256]{1,0:T(8,128)S(1)}, f32[8,256]{1,0:T(8,128)S(1)}, u32[]{:S(2)}, u32[]{:S(2)}) %collective-permute-start.4) | collective-permute-done | bytes 8224 | tf_op jit(solution)/shard_map/ppermute | solution.py:402
  62.5 1.5 %collective-permute-done.5.right_corner = f32[8,256]{1,0:T(8,128)S(1)} collective-permute-done((f32[8,256]{1,0:T(8,128)S(1)}, f32[8,256]{1,0:T(8,128)S(1)}, u32[]{:S(2)}, u32[]{:S(2)}) %collective-permute-start.5) | collective-permute-done | bytes 8224 | tf_op jit(solution)/shard_map/ppermute | solution.py:403
  64.0 6.5 %all-to-all-done.1 = f32[64,16,128]{2,1,0:T(8,128)S(1)} async-done(((f32[64,16,128]{2,1,0:T(8,128)}), f32[64,16,128]{2,1,0:T(8,128)S(1)}, u32[]{:S(2)}, u32[]{:S(2)}) %all-to-all-start.1) | async-done | bytes 524320 | tf_op jit(solution)/shard_map/all_to_all | solution.py:417
  70.6 2.2 %merge.1 = f32[4,32,16,256]{3,2,1,0:T(8,128)} custom-call(f32[4,32,16,256]{3,2,1,0:T(8,128)} %outer.1.stepped, f32[1024,128]{1,0:T(8,128)S(1)} %bitcast.6, f32[8,256]{1,0:T(8,128)S(1)} %collective-permute-done.4.left_corner, f32[8,256]{1,0:T(8,128)S(1)} %collective-permute-done.5.right_corner), custom_call_target="tpu_custom_call", output_to_operand_aliasing={{}: (0, {})} | custom-call | tf_op jit(solution)/shard_map/merge/pallas_call | solution.py:418
  (21 shorter events, 0.0 us)
Async XLA Ops:
  0.0 1.6 %copy-start = (f32[4,32,16,256]{3,2,1,0:T(8,128)S(1)}, f32[4,32,16,256]{3,2,1,0:T(8,128)}, u32[]{:S(2)}) copy-start(f32[4,32,16,256]{3,2,1,0:T(8,128)} %state.7) | copy-start | bytes 6291460
  1.6 9.3 %copy-start.10 = (f32[8]{0:T(128)S(1)}, f32[8]{0:T(128)}, u32[]{:S(2)}) copy-start(f32[8]{0:T(128)} %resistance.1) | copy-start | bytes 100
  1.6 9.3 %copy-start.11 = (f32[8]{0:T(128)S(1)}, f32[8]{0:T(128)}, u32[]{:S(2)}) copy-start(f32[8]{0:T(128)} %relax.1) | copy-start | bytes 100
  1.6 11.6 %copy-start.1 = (f32[4,32,16,256]{3,2,1,0:T(8,128)S(1)}, f32[4,32,16,256]{3,2,1,0:T(8,128)}, u32[]{:S(2)}) copy-start(f32[4,32,16,256]{3,2,1,0:T(8,128)} %state.7) | copy-start | bytes 6291460
  1.9 11.3 %collective-permute-start = (f32[144,256]{1,0:T(8,128)S(1)}, f32[144,256]{1,0:T(8,128)S(1)}, u32[]{:S(2)}, u32[]{:S(2)}) collective-permute-start(f32[144,256]{1,0:T(8,128)S(1)} %get-tuple-element.16), channel_id=1, source_target_pairs={{0,4},{8,12},{16,20},{24,28},{32,36},{40,44},{48,52},{56,60},{64,6... | collective-permute-start | bytes 442376 | tf_op jit(solution)/shard_map/ppermute | solution.py:379
  3.8 9.4 %collective-permute-start.1 = (f32[144,256]{1,0:T(8,128)S(1)}, f32[144,256]{1,0:T(8,128)S(1)}, u32[]{:S(2)}, u32[]{:S(2)}) collective-permute-start(f32[144,256]{1,0:T(8,128)S(1)} %get-tuple-element.17), channel_id=1, source_target_pairs={{4,8},{12,16},{20,24},{28,32},{36,40},{44,48},{52,56},{60,64},{68,... | collective-permute-start | bytes 442376 | tf_op jit(solution)/shard_map/ppermute | solution.py:379
  5.8 7.3 %collective-permute-start.2 = (f32[136,256]{1,0:T(8,128)S(1)}, f32[136,256]{1,0:T(8,128)S(1)}, u32[]{:S(2)}, u32[]{:S(2)}) collective-permute-start(f32[136,256]{1,0:T(8,128)S(1)} %get-tuple-element.18), channel_id=1, source_target_pairs={{1,2},{2,1},{5,6},{6,5},{9,10},{10,9},{13,14},{14,13},{17,18},{18,... | collective-permute-start | bytes 417800 | tf_op jit(solution)/shard_map/ppermute | solution.py:379
  6.5 6.7 %collective-permute-start.3 = (f32[136,256]{1,0:T(8,128)S(1)}, f32[136,256]{1,0:T(8,128)S(1)}, u32[]{:S(2)}, u32[]{:S(2)}) collective-permute-start(f32[136,256]{1,0:T(8,128)S(1)} %get-tuple-element.19), channel_id=1, source_target_pairs={{0,1},{2,3},{1,0},{3,2},{4,5},{6,7},{5,4},{7,6},{8,9},{10,11},{9,8... | collective-permute-start | bytes 417800 | tf_op jit(solution)/shard_map/ppermute | solution.py:379
  10.9 0.8 %copy-start.7 = (s32[32,256]{1,0:T(8,128)S(1)}, s32[32,256]{1,0:T(8,128)}, u32[]{:S(2)}) copy-start(s32[32,256]{1,0:T(8,128)} %zone.1) | copy-start | bytes 98308
  11.7 0.8 %copy-start.8 = (f32[32,256]{1,0:T(8,128)S(1)}, f32[32,256]{1,0:T(8,128)}, u32[]{:S(2)}) copy-start(f32[32,256]{1,0:T(8,128)} %aux.1) | copy-start | bytes 98308
  13.1 32.0 %copy-start.2 = (bf16[2,128,544]{2,1,0:T(8,128)(2,1)S(1)}, bf16[2,128,544]{2,1,0:T(8,128)(2,1)}, u32[]{:S(2)}) copy-start(bf16[2,128,544]{2,1,0:T(8,128)(2,1)} %constant.11.clone.there_small) | copy-start | bytes 835588
  13.1 32.0 %copy-start.3 = (bf16[2,128,544]{2,1,0:T(8,128)(2,1)S(1)}, bf16[2,128,544]{2,1,0:T(8,128)(2,1)}, u32[]{:S(2)}) copy-start(bf16[2,128,544]{2,1,0:T(8,128)(2,1)} %constant.10.clone.there) | copy-start | bytes 835588
  13.1 31.9 %copy-start.4 = (bf16[2,128,512]{2,1,0:T(8,128)(2,1)S(1)}, bf16[2,128,512]{2,1,0:T(8,128)(2,1)}, u32[]{:S(2)}) copy-start(bf16[2,128,512]{2,1,0:T(8,128)(2,1)} %constant.13.clone.back_small) | copy-start | bytes 786436
  13.1 31.9 %copy-start.5 = (bf16[2,128,512]{2,1,0:T(8,128)(2,1)S(1)}, bf16[2,128,512]{2,1,0:T(8,128)(2,1)}, u32[]{:S(2)}) copy-start(bf16[2,128,512]{2,1,0:T(8,128)(2,1)} %constant.12.clone.back) | copy-start | bytes 786436
  13.1 31.9 %copy-start.6 = (f32[2,64,128]{2,1,0:T(8,128)S(1)}, f32[2,64,128]{2,1,0:T(8,128)}, u32[]{:S(2)}) copy-start(f32[2,64,128]{2,1,0:T(8,128)} %constant.14.clone.turn) | copy-start | bytes 196612
  13.1 31.9 %copy-start.9 = (s32[64]{0:T(128)S(1)}, s32[64]{0:T(128)}, u32[]{:S(2)}) copy-start(s32[64]{0:T(128)} %param.16) | copy-start | bytes 772
  47.2 23.4 %all-to-all-start.1 = ((f32[64,16,128]{2,1,0:T(8,128)}), f32[64,16,128]{2,1,0:T(8,128)S(1)}, u32[]{:S(2)}, u32[]{:S(2)}) async-start(f32[64,16,128]{2,1,0:T(8,128)} %bitcast.3), calls=%async_computation.1 | async-start | bytes 1048576 | tf_op jit(solution)/shard_map/all_to_all | solution.py:417
  52.7 9.8 %collective-permute-start.4 = (f32[8,256]{1,0:T(8,128)S(1)}, f32[8,256]{1,0:T(8,128)S(1)}, u32[]{:S(2)}, u32[]{:S(2)}) collective-permute-start(f32[8,256]{1,0:T(8,128)S(1)} %get-tuple-element.25), channel_id=1, source_target_pairs={{0,4},{4,8},{8,12},{12,16},{16,20},{20,24},{24,28},{28,32},{32,36}... | collective-permute-start | bytes 24584 | tf_op jit(solution)/shard_map/ppermute | solution.py:402
  54.2 9.9 %collective-permute-start.5 = (f32[8,256]{1,0:T(8,128)S(1)}, f32[8,256]{1,0:T(8,128)S(1)}, u32[]{:S(2)}, u32[]{:S(2)}) collective-permute-start(f32[8,256]{1,0:T(8,128)S(1)} %get-tuple-element.26), channel_id=1, source_target_pairs={{4,0},{8,4},{12,8},{16,12},{20,16},{24,20},{28,24},{32,28},{36,32}... | collective-permute-start | bytes 24584 | tf_op jit(solution)/shard_map/ppermute | solution.py:403
